TPU v7x, 32 devices: a whole 2x2x4 slice. The times are simulated.
32 devices in a mesh: batch: 4 (over y, x), centre: 8 (over z, core).
Axes of the slice: x: 2, y: 2, z: 4, core: 2. Of those that a mesh axis runs over, the one named last changes fastest.
Arguments:
- batch_pool: bfloat16 [1312, 1024], P(('batch', 'centre')), may hold values from -6 to 6
- batch_index: int32 [1024], P(('batch', 'centre')), may hold values from 0 to 1311, as said below
- centre_pool: bfloat16 [18440, 1024], P('centre'), may hold values from -6 to 6
- centre_index: int32 [16384], P('centre'), may hold values from 0 to 18439, as said below
- targets: float32 [1024, 301], P(('batch', 'centre')), may hold values from -6 to 6
- coefficients: float32 [16384, 301], P('centre'), may hold values from -1.5 to 1.5
Outputs:
- updated: float32 [16384, 301], P('centre')
- residual: float32 [1024, 301], P(('batch', 'centre'))
Inputs may be any that keep to these rules, and one draw needn't show every extreme that they name: `batch_index`: the entries of each aligned block of 32 are distinct and lie in the same aligned block of 41 pool rows, block for block. `centre_index`: the entries of each aligned block of 2048 are distinct and lie in the same aligned block of 2305 pool rows, block for block.
All inputs are finite; a program needn't handle non-finite values.
Results may differ from a plain program's by a relative error of at most 0.0034.
Values may be sent and summed in bfloat16 or wider, within the bound.
No kernel may reach another device: no remote copies, remote signals or barrier semaphores. Data moves between devices by JAX's collectives and lax.ppermute only.
A program may use at most 64 MiB of HBM per device.

v0:
```python
import functools
import math

import jax
import jax.numpy as jnp
from jax import lax
from jax.experimental import pallas as pl
from jax.experimental.pallas import tpu as pltpu
from jax.sharding import PartitionSpec as P

LANES = 128


def flip(value, axis, distance):
    count = lax.axis_size(axis)
    return lax.ppermute(value, axis, [(i, i ^ distance) for i in range(count)])


def after(value, *others):
    return lax.optimization_barrier((value,) + others)[0]


def contract_last(left, right):
    return lax.dot_general(
        left, right, (((1,), (1,)), ((), ())), preferred_element_type=jnp.float32
    )


def spans(total, most):
    return [(at, min(most, total - at)) for at in range(0, total, most)]


def tiles(count):
    return -(-count // LANES) * LANES


WHOLE = pl.BlockSpec(memory_space=pltpu.VMEM)
SCALARS = pl.BlockSpec(memory_space=pltpu.SMEM)
FAR = pl.BlockSpec(memory_space=pltpu.HBM)


def call(body, operands, outputs, scratch=(), limit=28):
    arrays = [array for array, _ in operands]
    shapes = [jax.ShapeDtypeStruct(shape, dtype) for shape, dtype, _ in outputs]
    return pl.pallas_call(
        body,
        in_specs=[place for _, place in operands],
        out_specs=[place for _, _, place in outputs],
        out_shape=shapes,
        scratch_shapes=list(scratch),
        cost_estimate=pl.CostEstimate(flops=1024, bytes_accessed=1024, transcendentals=0),
        compiler_params=pltpu.CompilerParams(vmem_limit_bytes=limit << 20),
    )(*arrays)


def turned(column):
    return jnp.concatenate(
        [
            jnp.broadcast_to(column[at : at + LANES], (LANES, LANES)).T[:1]
            for at in range(0, column.shape[0], LANES)
        ],
        axis=1,
    )


def pool_rows(pool_ref, at, size):
    if at + size <= pool_ref.shape[0]:
        return pool_ref[at : at + size, :]
    place = lax.broadcasted_iota(jnp.int32, (size, pool_ref.shape[1]), 0)
    rows = jnp.zeros(place.shape, jnp.float32)
    for row in range(at, pool_ref.shape[0]):
        rows = jnp.where(place == row - at, pool_ref[row : row + 1, :].astype(jnp.float32), rows)
    return rows.astype(jnp.bfloat16)


def place_body(index_ref, base_ref, pool_far, placed_ref, square_ref, kept_ref, pool_ref, done_ref):
    fetch = pltpu.make_async_copy(pool_far, pool_ref, done_ref)
    fetch.start()
    index = index_ref[...]
    base = base_ref[...]
    kept_ref[...] = base
    half = base.astype(jnp.bfloat16)
    cuts = spans(placed_ref.shape[1], 2 * LANES)
    left, arrival = list(cuts), min(3, len(cuts) - 1)
    for turn, (at, size) in enumerate(cuts):
        place = lax.broadcasted_iota(jnp.int32, (size, index.shape[1]), 0) + at
        chosen = jnp.where(index == place, 1.0, 0.0).astype(jnp.bfloat16)
        placed_ref[:, at : at + size] = contract_last(half, chosen).astype(jnp.bfloat16)
        if turn == arrival:
            fetch.wait()
        share = -(-len(left) // (len(cuts) - turn)) if turn >= arrival else 0
        for from_row, count in left[:share]:
            rows = pool_rows(pool_ref, from_row, count).astype(jnp.float32)
            square_ref[:, from_row : from_row + count] = turned(
                jnp.sum(rows * rows, axis=1, keepdims=True)
            )
        left = left[share:]


def place_coefficients(index, base, pool):
    width = tiles(pool.shape[0])
    return call(
        place_body,
        [(index, WHOLE), (base, WHOLE), (pool, FAR)],
        [
            ((base.shape[0], width), jnp.bfloat16, WHOLE),
            ((1, width), jnp.float32, WHOLE),
            (base.shape, jnp.float32, WHOLE),
            (pool.shape, jnp.bfloat16, WHOLE),
        ],
        [pltpu.SemaphoreType.DMA(())],
        limit=41,
    )


def turn_over(source_ref, target_ref):
    for row in range(0, source_ref.shape[0], LANES):
        for column in range(0, source_ref.shape[1], LANES):
            target_ref[column : column + LANES, row : row + LANES] = source_ref[
                row : row + LANES, column : column + LANES
            ].T


def arrange_body(place_ref, targets_ref, *refs):
    pieces, (side_ref, placed_ref, wide_ref, tall_ref) = refs[:-4], refs[-4:]
    count = targets_ref.shape[0]
    for k, piece_ref in enumerate(pieces):
        at = pl.multiple_of((place_ref[0] ^ k) * count, count)
        side_ref[pl.ds(at, count), :] = piece_ref[...]
    wide_ref[...] = jnp.zeros_like(wide_ref)
    at = pl.multiple_of(place_ref[0] * count, count)
    wide_ref[pl.ds(at, count), : targets_ref.shape[1]] = targets_ref[...]
    turn_over(wide_ref, tall_ref)
    placed_ref[...] = tall_ref[: placed_ref.shape[0], : placed_ref.shape[1]]


def arrange(place, targets, pieces):
    count, outs = targets.shape
    rows = count * len(pieces)
    high, wide = tiles(rows), tiles(outs)
    return call(
        arrange_body,
        [(place, SCALARS), (targets, WHOLE)] + [(piece, WHOLE) for piece in pieces],
        [
            ((rows, pieces[0].shape[1]), jnp.bfloat16, WHOLE),
            ((outs, rows), jnp.float32, WHOLE),
        ],
        [pltpu.VMEM((high, wide), jnp.float32), pltpu.VMEM((wide, high), jnp.float32)],
    )


def kernel_of(squared):
    least = jnp.maximum(squared, 1e-30)
    return jnp.exp2(least * -math.log2(math.e) * lax.rsqrt(least)).astype(jnp.bfloat16)


def halves_and_squares(samples):
    wide = samples.astype(jnp.float32)
    return (wide * -2.0).astype(jnp.bfloat16), jnp.sum(wide * wide, axis=1, keepdims=True)


def column_of(row):
    return jnp.concatenate(
        [
            jnp.broadcast_to(row[:, at : at + LANES], (LANES, LANES)).T
            for at in range(0, row.shape[1], LANES)
        ],
        axis=0,
    )


def terms_body(side_ref, other_ref, pool_ref, square_ref, placed_ref, *refs):
    terms_ref, other_terms_ref, kernel_ref = refs
    samples = jnp.concatenate([side_ref[...], other_ref[...]], axis=0)
    samples, own_square = halves_and_squares(samples)
    own_square = turned(own_square)
    for at, size in spans(placed_ref.shape[1], 4 * LANES):
        cross = contract_last(pool_rows(pool_ref, at, size), samples)
        pool_square = column_of(square_ref[:, at : at + size])[:, :1]
        kernel_ref[at : at + size, :] = kernel_of(pool_square + own_square + cross)
    terms = jnp.dot(placed_ref[...], kernel_ref[...], preferred_element_type=jnp.float32)
    rows = side_ref.shape[0]
    terms_ref[...] = terms[:, :rows]
    other_terms_ref[...] = terms[:, rows:]


def pool_terms(side, other, pool, square, placed):
    outs, rows = placed.shape[0], side.shape[0]
    return call(
        terms_body,
        [(array, WHOLE) for array in (side, other, pool, square, placed)],
        [((outs, rows), jnp.float32, WHOLE)] * 2,
        [pltpu.VMEM((placed.shape[1], 2 * rows), jnp.bfloat16)],
    )


def pick_body(first, index_ref, pool_ref, side_ref, other_ref, rows_ref, square_ref, kernel_ref):
    whole = pool_ref.shape[0] // LANES * LANES
    samples = jnp.concatenate([side_ref[...], other_ref[...]], axis=0)
    samples, own_square = halves_and_squares(samples)
    for at, size in spans(rows_ref.shape[0], 8 * LANES):
        wanted = column_of(index_ref[:, first + at : first + at + size])
        lane = lax.broadcasted_iota(jnp.int32, (size, LANES), 1)
        chosen = jnp.concatenate(
            [
                jnp.where(wanted == lane + part, 1.0, 0.0).astype(jnp.bfloat16)
                for part in range(0, whole, LANES)
            ],
            axis=1,
        )
        rows = jnp.dot(chosen, pool_ref[:whole, :], preferred_element_type=jnp.float32)
        for row in range(whole, pool_ref.shape[0]):
            rows = rows + jnp.where(
                wanted[:, :1] == row, pool_ref[row : row + 1, :].astype(jnp.float32), 0.0
            )
        half = rows.astype(jnp.bfloat16)
        square = turned(jnp.sum(rows * rows, axis=1, keepdims=True))
        rows_ref[at : at + size, :] = half
        square_ref[:, at : at + size] = square
        kernel_ref[:, at : at + size] = kernel_of(
            own_square + square + contract_last(samples, half)
        )


def pick_rows(index, pool, side, other, first, count):
    rows = side.shape[0] + other.shape[0]
    return call(
        functools.partial(pick_body, first),
        [(index, WHOLE), (pool, WHOLE), (side, WHOLE), (other, WHOLE)],
        [
            ((count, pool.shape[1]), jnp.bfloat16, WHOLE),
            ((1, count), jnp.float32, WHOLE),
            ((rows, count), jnp.bfloat16, WHOLE),
        ],
    )


def block_body(parts, *refs):
    samples = jnp.concatenate([ref[...] for ref in refs[:parts]], axis=0)
    kernel_ref = refs[-1]
    samples, own_square = halves_and_squares(samples)
    start = 0
    for rows_ref, square_ref in zip(refs[parts:-1:2], refs[parts + 1 : -1 : 2]):
        for at, size in spans(rows_ref.shape[0], 2 * LANES):
            cross = contract_last(samples, rows_ref[at : at + size, :])
            kernel = kernel_of(own_square + square_ref[:, at : at + size] + cross)
            kernel_ref[:, start + at : start + at + size] = kernel
        start += rows_ref.shape[0]


def kernel_block(samples, picked):
    rows = sum(part.shape[0] for part in samples)
    count = sum(square.shape[1] for _, square, _ in picked)
    return call(
        functools.partial(block_body, len(samples)),
        [(part, WHOLE) for part in samples]
        + [(array, WHOLE) for each in picked for array in each[:2]],
        [((rows, count), jnp.bfloat16, WHOLE)],
    )[0]


def gradient_span(residual_ref, kernel_refs, owns, first, at, size):
    own_refs, rest_refs = kernel_refs[:owns], kernel_refs[owns:]
    span = own_refs[0].shape[1]
    own_ref, own_at = own_refs[at // span], at % span
    rows = residual_ref.shape[1] - sum(rest_ref.shape[0] for rest_ref in rest_refs)
    gradient = jnp.dot(
        residual_ref[:, :rows],
        own_ref[first : first + rows, own_at : own_at + size],
        preferred_element_type=jnp.float32,
    )
    for rest_ref in rest_refs:
        gradient = gradient + jnp.dot(
            residual_ref[:, rows:], rest_ref[:, at : at + size], preferred_element_type=jnp.float32
        )
    return gradient


def descend_body(step, owns, kernels, place_ref, total_ref, residual_ref, base_ref, *refs):
    kernel_refs, refs = refs[:kernels], refs[kernels:]
    out_ref, own_far, tall_ref, wide_ref, own_ref, done_ref = refs
    outs, rows = total_ref.shape
    count = own_ref.shape[0]
    tall_ref[...] = jnp.zeros_like(tall_ref)
    tall_ref[:outs, :rows] = total_ref[...]
    turn_over(tall_ref, wide_ref)
    at = pl.multiple_of(place_ref[0] * count, count)
    own_ref[...] = wide_ref[pl.ds(at, count), :outs]
    store = pltpu.make_async_copy(own_ref, own_far, done_ref)
    store.start()
    for at, size in spans(base_ref.shape[1], 4 * LANES):
        gradient = gradient_span(residual_ref, kernel_refs, owns, 0, at, size)
        out_ref[:, at : at + size] = base_ref[:, at : at + size] - step * gradient
    store.wait()


def descend(place, total, count, residual, base, owns, rests, step):
    outs, rows = total.shape
    high, wide = tiles(rows), tiles(outs)
    kernels = [*owns, *rests]
    return call(
        functools.partial(descend_body, step, len(owns), len(kernels)),
        [(place, SCALARS)] + [(array, WHOLE) for array in (total, residual, base, *kernels)],
        [(base.shape, jnp.float32, WHOLE), ((count, outs), jnp.float32, FAR)],
        [
            pltpu.VMEM((wide, high), jnp.float32),
            pltpu.VMEM((high, wide), jnp.float32),
            pltpu.VMEM((count, outs), jnp.float32),
            pltpu.SemaphoreType.DMA(()),
        ],
    )


def finish_body(step, owns, kernels, first, residual_ref, base_ref, *refs):
    kernel_refs, (out_far, held_ref, done_ref) = refs[:kernels], refs[kernels:]
    stores = []
    for turn, (at, size) in enumerate(spans(base_ref.shape[1], 4 * LANES)):
        gradient = gradient_span(residual_ref, kernel_refs, owns, first, at, size)
        held_ref[:, at : at + size] = base_ref[:, at : at + size] - step * gradient
        span = pl.ds(at, size)
        stores.append(
            pltpu.make_async_copy(held_ref.at[:, span], out_far.at[:, span], done_ref.at[turn])
        )
        stores[-1].start()
    for store in stores:
        store.wait()


def finish(residual, base, owns, rests, first, step):
    turns = len(spans(base.shape[1], 4 * LANES))
    kernels = [*owns, *rests]
    return call(
        functools.partial(finish_body, step, len(owns), len(kernels), first),
        [(array, WHOLE) for array in (residual, base, *kernels)],
        [(base.shape, jnp.float32, FAR)],
        [pltpu.VMEM(base.shape, jnp.float32), pltpu.SemaphoreType.DMA((turns,))],
    )[0]


def on_device(batch_pool, batch_index, centre_pool, centre_index, targets, coefficients):
    own_count = batch_index.shape[0]
    batch_size, centre_size = lax.axis_size("batch"), lax.axis_size("centre")
    batch_place, centre_place = lax.axis_index("batch"), lax.axis_index("centre")
    device_place = batch_place * centre_size + centre_place
    batch_total = own_count * batch_size * centre_size
    far_size, far_place = centre_size // 2, lax.shift_right_logical(centre_place, 1)
    rows = far_size * own_count
    hold_all = batch_total * (centre_index.shape[0] + batch_pool.shape[1]) * 2 <= 1 << 24

    count = centre_index.shape[0]
    indices = lax.optimization_barrier(
        jnp.concatenate(
            [
                centre_index - centre_place * centre_pool.shape[0],
                batch_index - device_place * batch_pool.shape[0],
            ]
        )
    )
    chosen = indices[count:, None] == jnp.arange(batch_pool.shape[0])
    local_rows = jnp.dot(
        chosen.astype(jnp.bfloat16), batch_pool, preferred_element_type=jnp.float32
    ).astype(jnp.bfloat16)
    pieces = [local_rows] + [flip(local_rows, "centre", 2 * k) for k in range(1, far_size)]

    place = jnp.reshape(far_place, (1,)).astype(jnp.int32)
    index, place = lax.optimization_barrier((indices[:count].reshape(1, -1), place))
    placed, pool_square, base, pool = place_coefficients(index, coefficients.T, centre_pool)
    placed, *pieces = lax.optimization_barrier((placed, *pieces))
    side, placed_targets = arrange(place, targets, pieces)
    other = flip(side, "centre", 1)
    terms, other_terms = pool_terms(side, other, pool, pool_square, placed)
    foreign = [flip(side, "batch", k) for k in range(1, batch_size)] if hold_all else []

    total = terms - placed_targets + flip(other_terms, "centre", 1)
    cuts = far_size.bit_length() - 1 if count % (LANES * far_size) == 0 else 1
    picked = []
    distance = 2
    while distance < centre_size:
        if len(picked) < cuts:
            at, size = len(picked) * (count // cuts), count // cuts
            picked.append(pick_rows(after(index, total), pool, side, other, at, size))
        total = after(total + flip(total, "centre", distance), *picked[-1])
        distance *= 2
    if hold_all:
        foreign = lax.optimization_barrier((total, *foreign))[1:]
        side_rows = jnp.concatenate(foreign, axis=0)
        other_rows = flip(side_rows, "centre", 1)
    kernels = [kernel for _, _, kernel in picked]
    residual_side = total.astype(jnp.bfloat16)
    rests, other_rests = [], []
    if hold_all:
        rests, other_rests = [kernel_block([side_rows], picked)], [kernel_block([other_rows], picked)]
        parts = [residual_side] + [flip(residual_side, "batch", k) for k in range(1, batch_size)]
        rests, other_rests, parts = lax.optimization_barrier((rests, other_rests, parts))
        residual_side = jnp.concatenate(parts, axis=1)
    residual_other = flip(residual_side, "centre", 1)

    step = 8.0 / math.sqrt(batch_total)
    start = base if hold_all else jnp.zeros_like(base)
    updated, residual = descend(
        place, total, own_count, residual_side, start, kernels, rests, step
    )
    updated = finish(residual_other, updated, kernels, other_rests, rows, step)
    if not hold_all:
        updated = base + lax.psum(updated, "batch")
    return (updated.T, residual)


def solution(mesh):
    return jax.shard_map(
        on_device,
        mesh=mesh,
        in_specs=(
            P(("batch", "centre"), None),
            P(("batch", "centre")),
            P("centre", None),
            P("centre"),
            P(("batch", "centre"), None),
            P("centre", None),
        ),
        out_specs=(P("centre", None), P(("batch", "centre"), None)),
        check_vma=False,
    )
```

profile of v0, /device:TPU:1, one launch (start us, length us, event | category | flops | bytes accessed | tf_op | source)
XLA Modules:
  0.0 55.1 jit_solution(5767789972551697042)
XLA Ops:
  0.6 0.0 copy-start
  0.7 0.7 %broadcast_subtract_fusion.1 = s32[32]{0:T(128)S(1)} fusion(s32[32]{0:T(128)} %param.7, s32[]{:T(128)S(6)} %mul.11), kind=kLoop, calls=%fused_computation.13 | loop fusion | flops 32 | bytes 260 | tf_op jit(solution)/shard_map/sub | solution.py:355
  1.3 0.7 %broadcast_subtract_fusion = s32[2048]{0:T(1024)S(1)} fusion(s32[2048]{0:T(1024)} %param.9, s32[]{:T(128)S(6)} %mul.9), kind=kLoop, calls=%fused_computation.12 | loop fusion | flops 2048 | bytes 16388 | tf_op jit(solution)/shard_map/sub | solution.py:354
  2.1 0.0 copy-done
  2.1 0.2 convolution_convert_fusion.refs_0_
  2.3 2.2 %collective-permute-start = (bf16[32,1024]{1,0:T(8,128)(2,1)S(1)}, bf16[32,1024]{1,0:T(8,128)(2,1)S(1)}, u32[]{:S(2)}, u32[]{:S(2)}) collective-permute-start(bf16[32,1024]{1,0:T(8,128)(2,1)S(1)} %convolution_convert_fusion.refs_0_), channel_id=1, source_target_pairs={{0,2},{1,3},{2,0},{3,1},{4,6},{5,7},{6,4},{7,5},{8,10},{9,11},{10,... | collective-permute-start | bytes 196616 | tf_op jit(solution)/shard_map/ppermute | solution.py:16
  4.5 2.3 %collective-permute-start.1 = (bf16[32,1024]{1,0:T(8,128)(2,1)S(1)}, bf16[32,1024]{1,0:T(8,128)(2,1)S(1)}, u32[]{:S(2)}, u32[]{:S(2)}) collective-permute-start(bf16[32,1024]{1,0:T(8,128)(2,1)S(1)} %convolution_convert_fusion.refs_0_), channel_id=1, source_target_pairs={{0,4},{1,5},{2,6},{3,7},{4,0},{5,1},{6,2},{7,3},{8,12},{9,13},{10,... | collective-permute-start | bytes 196616 | tf_op jit(solution)/shard_map/ppermute | solution.py:16
  6.8 0.0 collective-permute-start.2
  6.8 0.0 copy-start.1
  6.8 1.7 %copy-done.1 = f32[2048,301]{0,1:T(8,128)S(1)} copy-done((f32[2048,301]{0,1:T(8,128)S(1)}, f32[2048,301]{0,1:T(8,128)}, u32[]{:S(2)}) %copy-start.1) | copy-done | bytes 2465816
  8.5 0.0 copy-start.2
  8.5 5.9 %shard_map.77 = (bf16[301,2432]{1,0:T(8,128)(2,1)S(1)}, f32[1,2432]{1,0:T(1,128)S(1)}, f32[301,2048]{1,0:T(8,128)S(1)}, bf16[2305,1024]{1,0:T(8,128)(2,1)S(1)}) custom-call(s32[1,2048]{1,0:T(1,128)S(1)} %bitcast.6, f32[301,2048]{1,0:T(8,128)S(1)} %bitcast.5, bf16[2305,1024]{1,0:T(8,128)(2,1)} %pool_far.1), custom_call_target="tpu_custom_call" | custom-call | flops 1024 | bytes 1024 | tf_op jit(solution)/shard_map/pallas_call | solution.py:45
  14.3 0.0 collective-permute-done.refs_1_
  14.3 0.0 collective-permute-done.1.refs_2_
  14.4 0.0 collective-permute-done.2.refs_3_
  14.4 0.0 copy-done.2
  14.4 0.2 shard_map.78
  14.5 1.3 %collective-permute-start.3 = (bf16[128,1024]{1,0:T(8,128)(2,1)S(1)}, bf16[128,1024]{1,0:T(8,128)(2,1)S(1)}, u32[]{:S(2)}, u32[]{:S(2)}) collective-permute-start(bf16[128,1024]{1,0:T(8,128)(2,1)S(1)} %get-tuple-element.45.side_ref), channel_id=1, source_target_pairs={{0,1},{1,0},{2,3},{3,2},{4,5},{5,4},{6,7},{7,6},{8,9},{9,8},{10,11... | collective-permute-start | bytes 786440 | tf_op jit(solution)/shard_map/ppermute | solution.py:16
  15.8 1.2 %collective-permute-done.3.other_ref = bf16[128,1024]{1,0:T(8,128)(2,1)S(1)} collective-permute-done((bf16[128,1024]{1,0:T(8,128)(2,1)S(1)}, bf16[128,1024]{1,0:T(8,128)(2,1)S(1)}, u32[]{:S(2)}, u32[]{:S(2)}) %collective-permute-start.3) | collective-permute-done | bytes 262176 | tf_op jit(solution)/shard_map/ppermute | solution.py:16
  17.0 2.9 %shard_map.79 = (f32[301,128]{1,0:T(8,128)S(1)}, f32[301,128]{1,0:T(8,128)S(1)}) custom-call(bf16[128,1024]{1,0:T(8,128)(2,1)S(1)} %get-tuple-element.45.side_ref, bf16[128,1024]{1,0:T(8,128)(2,1)S(1)} %collective-permute-done.3.other_ref, bf16[2305,1024]{1,0:T(8,128)(2,1)S(1)} %get-tuple-element.46.pool_ref, f32[1,2432]{1,0:T(1,128)S(1)} %get-tuple-element.47.square_ref, ...), custom_call_target="tpu_custom_call" | custom-call | flops 1024 | bytes 1024 | tf_op jit(solution)/shard_map/pallas_call | solution.py:45
  19.9 0.4 collective-permute-start.4
  20.4 1.0 %collective-permute-done.4 = f32[301,128]{1,0:T(8,128)S(1)} collective-permute-done((f32[301,128]{1,0:T(8,128)S(1)}, f32[301,128]{1,0:T(8,128)S(1)}, u32[]{:S(2)}, u32[]{:S(2)}) %collective-permute-start.4) | collective-permute-done | bytes 154144 | tf_op jit(solution)/shard_map/ppermute | solution.py:16
  21.4 0.7 %collective-permute-start.5 = (f32[301,128]{1,0:T(8,128)S(1)}, f32[301,128]{1,0:T(8,128)S(1)}, u32[]{:S(2)}, u32[]{:S(2)}) collective-permute-start(f32[301,128]{1,0:T(8,128)S(1)} %subtract_add_fusion), channel_id=1, source_target_pairs={{0,2},{1,3},{2,0},{3,1},{4,6},{5,7},{6,4},{7,5},{8,10},{9,11},{10,... | collective-permute-start | bytes 462344 | tf_op jit(solution)/shard_map/ppermute | solution.py:16
  22.1 1.2 %collective-permute-start.7 = (bf16[128,1024]{1,0:T(8,128)(2,1)S(1)}, bf16[128,1024]{1,0:T(8,128)(2,1)S(1)}, u32[]{:S(2)}, u32[]{:S(2)}) collective-permute-start(bf16[128,1024]{1,0:T(8,128)(2,1)S(1)} %get-tuple-element.45.side_ref), channel_id=1, source_target_pairs={{0,8},{8,0},{16,24},{24,16},{1,9},{9,1},{17,25},{25,17},{2,10},{10... | collective-permute-start | bytes 786440 | tf_op jit(solution)/shard_map/ppermute | solution.py:16
  23.3 1.2 %collective-permute-start.8 = (bf16[128,1024]{1,0:T(8,128)(2,1)S(1)}, bf16[128,1024]{1,0:T(8,128)(2,1)S(1)}, u32[]{:S(2)}, u32[]{:S(2)}) collective-permute-start(bf16[128,1024]{1,0:T(8,128)(2,1)S(1)} %get-tuple-element.45.side_ref), channel_id=1, source_target_pairs={{0,16},{8,24},{16,0},{24,8},{1,17},{9,25},{17,1},{25,9},{2,18},{10... | collective-permute-start | bytes 786440 | tf_op jit(solution)/shard_map/ppermute | solution.py:16
  24.6 0.2 collective-permute-start.9
  24.8 6.1 %shard_map.80 = (bf16[1024,1024]{1,0:T(8,128)(2,1)S(1)}, f32[1,1024]{1,0:T(1,128)S(1)}, bf16[256,1024]{1,0:T(8,128)(2,1)S(1)}) custom-call(s32[1,2048]{1,0:T(1,128)S(1)} %bitcast.7, bf16[2305,1024]{1,0:T(8,128)(2,1)S(1)} %get-tuple-element.46.pool_ref, bf16[128,1024]{1,0:T(8,128)(2,1)S(1)} %get-tuple-element.45.side_ref, ...), custom_call_target="tpu_custom_call" | custom-call | flops 1024 | bytes 1024 | tf_op jit(solution)/shard_map/pallas_call | solution.py:45
  30.9 0.0 collective-permute-done.5
  30.9 3.3 %collective-permute-start.6 = (f32[301,128]{1,0:T(8,128)S(1)}, f32[301,128]{1,0:T(8,128)S(1)}, u32[]{:S(2)}, u32[]{:S(2)}) collective-permute-start(f32[301,128]{1,0:T(8,128)S(1)} %add.14), channel_id=1, source_target_pairs={{0,4},{1,5},{2,6},{3,7},{4,0},{5,1},{6,2},{7,3},{8,12},{9,13},{10,... | collective-permute-start | bytes 462344 | tf_op jit(solution)/shard_map/ppermute | solution.py:16
  34.2 6.2 %shard_map.81 = (bf16[1024,1024]{1,0:T(8,128)(2,1)S(1)}, f32[1,1024]{1,0:T(1,128)S(1)}, bf16[256,1024]{1,0:T(8,128)(2,1)S(1)}) custom-call(s32[1,2048]{1,0:T(1,128)S(1)} %bitcast.8, bf16[2305,1024]{1,0:T(8,128)(2,1)S(1)} %get-tuple-element.46.pool_ref, bf16[128,1024]{1,0:T(8,128)(2,1)S(1)} %get-tuple-element.45.side_ref, ...), custom_call_target="tpu_custom_call" | custom-call | flops 1024 | bytes 1024 | tf_op jit(solution)/shard_map/pallas_call | solution.py:45
  40.4 1.3 %collective-permute-done.6 = f32[301,128]{1,0:T(8,128)S(1)} collective-permute-done((f32[301,128]{1,0:T(8,128)S(1)}, f32[301,128]{1,0:T(8,128)S(1)}, u32[]{:S(2)}, u32[]{:S(2)}) %collective-permute-start.6) | collective-permute-done | bytes 154144 | tf_op jit(solution)/shard_map/ppermute | solution.py:16
  41.7 0.0 collective-permute-done.7
  41.7 0.0 collective-permute-done.8
  41.7 0.0 collective-permute-done.9
  41.8 0.7 %collective-permute-start.10 = (bf16[384,1024]{1,0:T(8,128)(2,1)S(1)}, bf16[384,1024]{1,0:T(8,128)(2,1)S(1)}, u32[]{:S(2)}, u32[]{:S(2)}) collective-permute-start(bf16[384,1024]{1,0:T(8,128)(2,1)S(1)} %constant_dynamic-update-slice_fusion.refs_0_), channel_id=1, source_target_pairs={{0,1},{1,0},{2,3},{3,2},{4,5},{5,4},{6,7},{7,6},{8,9},{9,8},{10,11... | collective-permute-start | bytes 2359304 | tf_op jit(solution)/shard_map/ppermute | solution.py:16
  42.5 1.4 %collective-permute-start.11 = (bf16[301,128]{1,0:T(8,128)(2,1)S(1)}, bf16[301,128]{1,0:T(8,128)(2,1)S(1)}, u32[]{:S(2)}, u32[]{:S(2)}) collective-permute-start(bf16[301,128]{1,0:T(8,128)(2,1)S(1)} %convert_element_type.8), channel_id=1, source_target_pairs={{0,8},{8,0},{16,24},{24,16},{1,9},{9,1},{17,25},{25,17},{2,10},{10... | collective-permute-start | bytes 231176 | tf_op jit(solution)/shard_map/ppermute | solution.py:16
  43.9 1.2 %collective-permute-start.12 = (bf16[301,128]{1,0:T(8,128)(2,1)S(1)}, bf16[301,128]{1,0:T(8,128)(2,1)S(1)}, u32[]{:S(2)}, u32[]{:S(2)}) collective-permute-start(bf16[301,128]{1,0:T(8,128)(2,1)S(1)} %convert_element_type.8), channel_id=1, source_target_pairs={{0,16},{8,24},{16,0},{24,8},{1,17},{9,25},{17,1},{25,9},{2,18},{10... | collective-permute-start | bytes 231176 | tf_op jit(solution)/shard_map/ppermute | solution.py:16
  45.2 0.1 collective-permute-start.13
  45.2 2.3 %shard_map.82.refs_2_ = bf16[384,2048]{1,0:T(8,128)(2,1)S(1)} custom-call(bf16[384,1024]{1,0:T(8,128)(2,1)S(1)} %constant_dynamic-update-slice_fusion.refs_0_, bf16[1024,1024]{1,0:T(8,128)(2,1)S(1)} %get-tuple-element.53.refs_1_, f32[1,1024]{1,0:T(1,128)S(1)} %get-tuple-element.54.refs_2_, bf16[1024,1024]{1,0:T(8,128)(2,1)S(1)} %get-tuple-element.58.refs_3_, ...), custom_call_target="tpu_custom_call" | custom-call | flops 1024 | bytes 1024 | tf_op jit(solution)/shard_map/pallas_call | solution.py:45
  47.5 0.0 collective-permute-done.10.refs_0_
  47.5 2.3 %shard_map.83.refs_2_ = bf16[384,2048]{1,0:T(8,128)(2,1)S(1)} custom-call(bf16[384,1024]{1,0:T(8,128)(2,1)S(1)} %collective-permute-done.10.refs_0_, bf16[1024,1024]{1,0:T(8,128)(2,1)S(1)} %get-tuple-element.53.refs_1_, f32[1,1024]{1,0:T(1,128)S(1)} %get-tuple-element.54.refs_2_, bf16[1024,1024]{1,0:T(8,128)(2,1)S(1)} %get-tuple-element.58.refs_3_, ...), custom_call_target="tpu_custom_call" | custom-call | flops 1024 | bytes 1024 | tf_op jit(solution)/shard_map/pallas_call | solution.py:45
  49.8 0.0 collective-permute-done.11
  49.8 0.0 collective-permute-done.12
  49.8 0.0 collective-permute-done.13
  49.9 1.3 %collective-permute-start.14 = (bf16[301,512]{1,0:T(8,128)(2,1)S(1)}, bf16[301,512]{1,0:T(8,128)(2,1)S(1)}, u32[]{:S(2)}, u32[]{:S(2)}) collective-permute-start(bf16[301,512]{1,0:T(8,128)(2,1)S(1)} %constant_dynamic-update-slice_fusion.3.residual_ref), channel_id=1, source_target_pairs={{0,1},{1,0},{2,3},{3,2},{4,5},{5,4},{6,7},{7,6},{8,9},{9,8},{10,11... | collective-permute-start | bytes 924680 | tf_op jit(solution)/shard_map/ppermute | solution.py:16
  51.2 1.7 %shard_map.84 = (f32[301,2048]{1,0:T(8,128)S(1)}, f32[32,301]{1,0:T(8,128)}) custom-call(s32[1]{0:T(128)} %bitcast.1.place_ref, f32[301,128]{1,0:T(8,128)S(1)} %add.15.total_ref, bf16[301,512]{1,0:T(8,128)(2,1)S(1)} %constant_dynamic-update-slice_fusion.3.residual_ref, f32[301,2048]{1,0:T(8,128)S(1)} %get-tuple-element.69.base_ref, ...), custom_call_target="tpu_custom_call" | custom-call | flops 1024 | bytes 1024 | tf_op jit(solution)/shard_map/pallas_call | solution.py:45
  52.9 0.0 collective-permute-done.14.residual_ref
  52.9 2.0 %shard_map.85 = f32[301,2048]{1,0:T(8,128)} custom-call(bf16[301,512]{1,0:T(8,128)(2,1)S(1)} %collective-permute-done.14.residual_ref, f32[301,2048]{1,0:T(8,128)S(1)} %get-tuple-element.71.base_ref, bf16[256,1024]{1,0:T(8,128)(2,1)S(1)} %get-tuple-element.55.refs_0_, bf16[256,1024]{1,0:T(8,128)(2,1)S(1)} %get-tuple-element.60.refs_1_, ...), custom_call_target="tpu_custom_call" | custom-call | flops 1024 | bytes 1024 | tf_op jit(solution)/shard_map/pallas_call | solution.py:45
  (14 shorter events, 0.2 us)
Async XLA Ops:
  0.6 1.4 %copy-start = (bf16[41,1024]{1,0:T(8,128)(2,1)S(1)}, bf16[41,1024]{1,0:T(8,128)(2,1)}, u32[]{:S(2)}) copy-start(bf16[41,1024]{1,0:T(8,128)(2,1)} %param.6) | copy-start | bytes 251908
  2.3 12.1 %collective-permute-start = (bf16[32,1024]{1,0:T(8,128)(2,1)S(1)}, bf16[32,1024]{1,0:T(8,128)(2,1)S(1)}, u32[]{:S(2)}, u32[]{:S(2)}) collective-permute-start(bf16[32,1024]{1,0:T(8,128)(2,1)S(1)} %convolution_convert_fusion.refs_0_), channel_id=1, source_target_pairs={{0,2},{1,3},{2,0},{3,1},{4,6},{5,7},{6,4},{7,5},{8,10},{9,11},{10,... | collective-permute-start | bytes 196616 | tf_op jit(solution)/shard_map/ppermute | solution.py:16
  4.5 9.9 %collective-permute-start.1 = (bf16[32,1024]{1,0:T(8,128)(2,1)S(1)}, bf16[32,1024]{1,0:T(8,128)(2,1)S(1)}, u32[]{:S(2)}, u32[]{:S(2)}) collective-permute-start(bf16[32,1024]{1,0:T(8,128)(2,1)S(1)} %convolution_convert_fusion.refs_0_), channel_id=1, source_target_pairs={{0,4},{1,5},{2,6},{3,7},{4,0},{5,1},{6,2},{7,3},{8,12},{9,13},{10,... | collective-permute-start | bytes 196616 | tf_op jit(solution)/shard_map/ppermute | solution.py:16
  6.8 7.6 %collective-permute-start.2 = (bf16[32,1024]{1,0:T(8,128)(2,1)S(1)}, bf16[32,1024]{1,0:T(8,128)(2,1)S(1)}, u32[]{:S(2)}, u32[]{:S(2)}) collective-permute-start(bf16[32,1024]{1,0:T(8,128)(2,1)S(1)} %convolution_convert_fusion.refs_0_), channel_id=1, source_target_pairs={{0,6},{1,7},{2,4},{3,5},{4,2},{5,3},{6,0},{7,1},{8,14},{9,15},{10,... | collective-permute-start | bytes 196616 | tf_op jit(solution)/shard_map/ppermute | solution.py:16
  6.8 1.7 %copy-start.1 = (f32[2048,301]{0,1:T(8,128)S(1)}, f32[2048,301]{0,1:T(8,128)}, u32[]{:S(2)}) copy-start(f32[2048,301]{0,1:T(8,128)} %param.11) | copy-start | bytes 7397380
  8.5 5.9 %copy-start.2 = (f32[32,301]{1,0:T(8,128)S(1)}, f32[32,301]{1,0:T(8,128)}, u32[]{:S(2)}) copy-start(f32[32,301]{1,0:T(8,128)} %targets_ref.1) | copy-start | bytes 115588
  14.5 2.5 %collective-permute-start.3 = (bf16[128,1024]{1,0:T(8,128)(2,1)S(1)}, bf16[128,1024]{1,0:T(8,128)(2,1)S(1)}, u32[]{:S(2)}, u32[]{:S(2)}) collective-permute-start(bf16[128,1024]{1,0:T(8,128)(2,1)S(1)} %get-tuple-element.45.side_ref), channel_id=1, source_target_pairs={{0,1},{1,0},{2,3},{3,2},{4,5},{5,4},{6,7},{7,6},{8,9},{9,8},{10,11... | collective-permute-start | bytes 786440 | tf_op jit(solution)/shard_map/ppermute | solution.py:16
  19.9 1.5 %collective-permute-start.4 = (f32[301,128]{1,0:T(8,128)S(1)}, f32[301,128]{1,0:T(8,128)S(1)}, u32[]{:S(2)}, u32[]{:S(2)}) collective-permute-start(f32[301,128]{1,0:T(8,128)S(1)} %get-tuple-element.51), channel_id=1, source_target_pairs={{0,1},{1,0},{2,3},{3,2},{4,5},{5,4},{6,7},{7,6},{8,9},{9,8},{10,11... | collective-permute-start | bytes 462344 | tf_op jit(solution)/shard_map/ppermute | solution.py:16
  21.4 9.4 %collective-permute-start.5 = (f32[301,128]{1,0:T(8,128)S(1)}, f32[301,128]{1,0:T(8,128)S(1)}, u32[]{:S(2)}, u32[]{:S(2)}) collective-permute-start(f32[301,128]{1,0:T(8,128)S(1)} %subtract_add_fusion), channel_id=1, source_target_pairs={{0,2},{1,3},{2,0},{3,1},{4,6},{5,7},{6,4},{7,5},{8,10},{9,11},{10,... | collective-permute-start | bytes 462344 | tf_op jit(solution)/shard_map/ppermute | solution.py:16
  22.1 19.6 %collective-permute-start.7 = (bf16[128,1024]{1,0:T(8,128)(2,1)S(1)}, bf16[128,1024]{1,0:T(8,128)(2,1)S(1)}, u32[]{:S(2)}, u32[]{:S(2)}) collective-permute-start(bf16[128,1024]{1,0:T(8,128)(2,1)S(1)} %get-tuple-element.45.side_ref), channel_id=1, source_target_pairs={{0,8},{8,0},{16,24},{24,16},{1,9},{9,1},{17,25},{25,17},{2,10},{10... | collective-permute-start | bytes 786440 | tf_op jit(solution)/shard_map/ppermute | solution.py:16
  23.3 18.4 %collective-permute-start.8 = (bf16[128,1024]{1,0:T(8,128)(2,1)S(1)}, bf16[128,1024]{1,0:T(8,128)(2,1)S(1)}, u32[]{:S(2)}, u32[]{:S(2)}) collective-permute-start(bf16[128,1024]{1,0:T(8,128)(2,1)S(1)} %get-tuple-element.45.side_ref), channel_id=1, source_target_pairs={{0,16},{8,24},{16,0},{24,8},{1,17},{9,25},{17,1},{25,9},{2,18},{10... | collective-permute-start | bytes 786440 | tf_op jit(solution)/shard_map/ppermute | solution.py:16
  24.6 17.2 %collective-permute-start.9 = (bf16[128,1024]{1,0:T(8,128)(2,1)S(1)}, bf16[128,1024]{1,0:T(8,128)(2,1)S(1)}, u32[]{:S(2)}, u32[]{:S(2)}) collective-permute-start(bf16[128,1024]{1,0:T(8,128)(2,1)S(1)} %get-tuple-element.45.side_ref), channel_id=1, source_target_pairs={{0,24},{8,16},{16,8},{24,0},{1,25},{9,17},{17,9},{25,1},{2,26},{10... | collective-permute-start | bytes 786440 | tf_op jit(solution)/shard_map/ppermute | solution.py:16
  30.9 10.8 %collective-permute-start.6 = (f32[301,128]{1,0:T(8,128)S(1)}, f32[301,128]{1,0:T(8,128)S(1)}, u32[]{:S(2)}, u32[]{:S(2)}) collective-permute-start(f32[301,128]{1,0:T(8,128)S(1)} %add.14), channel_id=1, source_target_pairs={{0,4},{1,5},{2,6},{3,7},{4,0},{5,1},{6,2},{7,3},{8,12},{9,13},{10,... | collective-permute-start | bytes 462344 | tf_op jit(solution)/shard_map/ppermute | solution.py:16
  41.8 5.7 %collective-permute-start.10 = (bf16[384,1024]{1,0:T(8,128)(2,1)S(1)}, bf16[384,1024]{1,0:T(8,128)(2,1)S(1)}, u32[]{:S(2)}, u32[]{:S(2)}) collective-permute-start(bf16[384,1024]{1,0:T(8,128)(2,1)S(1)} %constant_dynamic-update-slice_fusion.refs_0_), channel_id=1, source_target_pairs={{0,1},{1,0},{2,3},{3,2},{4,5},{5,4},{6,7},{7,6},{8,9},{9,8},{10,11... | collective-permute-start | bytes 2359304 | tf_op jit(solution)/shard_map/ppermute | solution.py:16
  42.5 7.3 %collective-permute-start.11 = (bf16[301,128]{1,0:T(8,128)(2,1)S(1)}, bf16[301,128]{1,0:T(8,128)(2,1)S(1)}, u32[]{:S(2)}, u32[]{:S(2)}) collective-permute-start(bf16[301,128]{1,0:T(8,128)(2,1)S(1)} %convert_element_type.8), channel_id=1, source_target_pairs={{0,8},{8,0},{16,24},{24,16},{1,9},{9,1},{17,25},{25,17},{2,10},{10... | collective-permute-start | bytes 231176 | tf_op jit(solution)/shard_map/ppermute | solution.py:16
  43.9 5.9 %collective-permute-start.12 = (bf16[301,128]{1,0:T(8,128)(2,1)S(1)}, bf16[301,128]{1,0:T(8,128)(2,1)S(1)}, u32[]{:S(2)}, u32[]{:S(2)}) collective-permute-start(bf16[301,128]{1,0:T(8,128)(2,1)S(1)} %convert_element_type.8), channel_id=1, source_target_pairs={{0,16},{8,24},{16,0},{24,8},{1,17},{9,25},{17,1},{25,9},{2,18},{10... | collective-permute-start | bytes 231176 | tf_op jit(solution)/shard_map/ppermute | solution.py:16
  45.2 4.6 %collective-permute-start.13 = (bf16[301,128]{1,0:T(8,128)(2,1)S(1)}, bf16[301,128]{1,0:T(8,128)(2,1)S(1)}, u32[]{:S(2)}, u32[]{:S(2)}) collective-permute-start(bf16[301,128]{1,0:T(8,128)(2,1)S(1)} %convert_element_type.8), channel_id=1, source_target_pairs={{0,24},{8,16},{16,8},{24,0},{1,25},{9,17},{17,9},{25,1},{2,26},{10... | collective-permute-start | bytes 231176 | tf_op jit(solution)/shard_map/ppermute | solution.py:16
  49.9 3.0 %collective-permute-start.14 = (bf16[301,512]{1,0:T(8,128)(2,1)S(1)}, bf16[301,512]{1,0:T(8,128)(2,1)S(1)}, u32[]{:S(2)}, u32[]{:S(2)}) collective-permute-start(bf16[301,512]{1,0:T(8,128)(2,1)S(1)} %constant_dynamic-update-slice_fusion.3.residual_ref), channel_id=1, source_target_pairs={{0,1},{1,0},{2,3},{3,2},{4,5},{5,4},{6,7},{7,6},{8,9},{9,8},{10,11... | collective-permute-start | bytes 924680 | tf_op jit(solution)/shard_map/ppermute | solution.py:16
where the time goes:
time: 55.3 us; the launch traced here: 55.1 us
  Pallas kernels  29.5 us (53%)
  starting transfers between devices  17.5 us (32%)
  waiting for transfers between devices  3.49 us (6%)
  local copies, waits for them, and re-layouts  1.86 us (3%)
  other arithmetic  1.48 us (3%)
  between operations  1.05 us (2%)
    pallas_call x9, Pallas kernels, call(): pl.pallas_call(body, in_specs=[place for _, place in operands], out_specs...  29.5 us
    ppermute x15, starting transfers between devices, flip(): return lax.ppermute(value, axis, [(i, i ^ distance) for i in range(count)])  17.5 us
    ppermute x15, waiting for transfers between devices, flip(): return lax.ppermute(value, axis, [(i, i ^ distance) for i in range(count)])  3.49 us
    unnamed x11, local copies, waits for them, and re-layouts  1.81 us
  transfers between devices with their start and end apart: 15, of which 3 were waited for; matrix products, arithmetic and copies ran while one was open for 0% of the time, Pallas kernels for 44%

commit v1 on v0

--- a/solution.py
+++ b/solution.py
@@ -194,43 +194,70 @@
     )
 
 
-def pick_body(first, index_ref, pool_ref, side_ref, other_ref, rows_ref, square_ref, kernel_ref):
+def pick_span(index_ref, pool_ref, rows_ref, square_ref, first, at, size):
     whole = pool_ref.shape[0] // LANES * LANES
+    wanted = column_of(index_ref[:, first + at : first + at + size])
+    lane = lax.broadcasted_iota(jnp.int32, (size, LANES), 1)
+    chosen = jnp.concatenate(
+        [
+            jnp.where(wanted == lane + part, 1.0, 0.0).astype(jnp.bfloat16)
+            for part in range(0, whole, LANES)
+        ],
+        axis=1,
+    )
+    rows = jnp.dot(chosen, pool_ref[:whole, :], preferred_element_type=jnp.float32)
+    for row in range(whole, pool_ref.shape[0]):
+        rows = rows + jnp.where(
+            wanted[:, :1] == row, pool_ref[row : row + 1, :].astype(jnp.float32), 0.0
+        )
+    rows_ref[at : at + size, :] = rows.astype(jnp.bfloat16)
+    square_ref[:, at : at + size] = turned(jnp.sum(rows * rows, axis=1, keepdims=True))
+
+
+def pick_body(first, index_ref, pool_ref, rows_ref, square_ref):
+    for at, size in spans(rows_ref.shape[0], 8 * LANES):
+        pick_span(index_ref, pool_ref, rows_ref, square_ref, first, at, size)
+
+
+def pick_rows(index, pool, first, count):
+    return call(
+        functools.partial(pick_body, first),
+        [(index, WHOLE), (pool, WHOLE)],
+        [((count, pool.shape[1]), jnp.bfloat16, WHOLE), ((1, count), jnp.float32, WHOLE)],
+    )
+
+
+def pick_own_body(first, index_ref, pool_ref, side_ref, other_ref, *refs):
+    *before, rows_ref, square_ref, kernel_ref = refs
     samples = jnp.concatenate([side_ref[...], other_ref[...]], axis=0)
     samples, own_square = halves_and_squares(samples)
+    start = 0
+    for early_ref, early_square_ref in zip(before[::2], before[1::2]):
+        span = early_ref.shape[0]
+        kernel_ref[:, start : start + span] = kernel_of(
+            own_square + early_square_ref[...] + contract_last(samples, early_ref[...])
+        )
+        start += span
     for at, size in spans(rows_ref.shape[0], 8 * LANES):
-        wanted = column_of(index_ref[:, first + at : first + at + size])
-        lane = lax.broadcasted_iota(jnp.int32, (size, LANES), 1)
-        chosen = jnp.concatenate(
-            [
-                jnp.where(wanted == lane + part, 1.0, 0.0).astype(jnp.bfloat16)
-                for part in range(0, whole, LANES)
-            ],
-            axis=1,
-        )
-        rows = jnp.dot(chosen, pool_ref[:whole, :], preferred_element_type=jnp.float32)
-        for row in range(whole, pool_ref.shape[0]):
-            rows = rows + jnp.where(
-                wanted[:, :1] == row, pool_ref[row : row + 1, :].astype(jnp.float32), 0.0
-            )
-        half = rows.astype(jnp.bfloat16)
-        square = turned(jnp.sum(rows * rows, axis=1, keepdims=True))
-        rows_ref[at : at + size, :] = half
-        square_ref[:, at : at + size] = square
-        kernel_ref[:, at : at + size] = kernel_of(
-            own_square + square + contract_last(samples, half)
-        )
-
-
-def pick_rows(index, pool, side, other, first, count):
+        pick_span(index_ref, pool_ref, rows_ref, square_ref, first, at, size)
+        kernel_ref[:, start + at : start + at + size] = kernel_of(
+            own_square
+            + square_ref[:, at : at + size]
+            + contract_last(samples, rows_ref[at : at + size, :])
+        )
+
+
+def pick_rows_and_own(index, pool, side, other, before, first, count):
     rows = side.shape[0] + other.shape[0]
-    return call(
-        functools.partial(pick_body, first),
-        [(index, WHOLE), (pool, WHOLE), (side, WHOLE), (other, WHOLE)],
+    early = sum(square.shape[1] for _, square in before)
+    return call(
+        functools.partial(pick_own_body, first),
+        [(array, WHOLE) for array in (index, pool, side, other)]
+        + [(array, WHOLE) for pair in before for array in pair],
         [
             ((count, pool.shape[1]), jnp.bfloat16, WHOLE),
             ((1, count), jnp.float32, WHOLE),
-            ((rows, count), jnp.bfloat16, WHOLE),
+            ((rows, early + count), jnp.bfloat16, WHOLE),
         ],
     )
 
@@ -250,11 +277,11 @@
 
 def kernel_block(samples, picked):
     rows = sum(part.shape[0] for part in samples)
-    count = sum(square.shape[1] for _, square, _ in picked)
+    count = sum(square.shape[1] for _, square in picked)
     return call(
         functools.partial(block_body, len(samples)),
         [(part, WHOLE) for part in samples]
-        + [(array, WHOLE) for each in picked for array in each[:2]],
+        + [(array, WHOLE) for pair in picked for array in pair],
         [((rows, count), jnp.bfloat16, WHOLE)],
     )[0]
 
@@ -368,24 +395,38 @@
     placed, *pieces = lax.optimization_barrier((placed, *pieces))
     side, placed_targets = arrange(place, targets, pieces)
     other = flip(side, "centre", 1)
+    steps = far_size.bit_length() - 1
+    span = count // (2 * steps) if steps and count % (2 * steps * LANES) == 0 else count
+    early = span // 2 if span < count and span % (2 * LANES) == 0 else 0
+    picked = []
+    if early:
+        picked.append(pick_rows(after(index, side), pool, 0, early))
+        other = after(other, *picked[-1])
     terms, other_terms = pool_terms(side, other, pool, pool_square, placed)
     foreign = [flip(side, "batch", k) for k in range(1, batch_size)] if hold_all else []
 
-    total = terms - placed_targets + flip(other_terms, "centre", 1)
-    cuts = far_size.bit_length() - 1 if count % (LANES * far_size) == 0 else 1
-    picked = []
+    flipped = flip(other_terms, "centre", 1)
+    if early:
+        picked.append(pick_rows(after(index, other_terms), pool, early, early))
+        flipped = after(flipped, *picked[-1])
+    total = terms - placed_targets + flipped
+    kernels, at = [], 2 * early
     distance = 2
     while distance < centre_size:
-        if len(picked) < cuts:
-            at, size = len(picked) * (count // cuts), count // cuts
-            picked.append(pick_rows(after(index, total), pool, side, other, at, size))
+        if at < count:
+            size = span if not kernels else 2 * span
+            size = min(size, count - at)
+            before = [] if kernels else picked
+            *pair, kernel = pick_rows_and_own(
+                after(index, total), pool, side, other, before, at, size
+            )
+            picked, kernels, at = [*picked, pair], [*kernels, kernel], at + size
         total = after(total + flip(total, "centre", distance), *picked[-1])
         distance *= 2
     if hold_all:
         foreign = lax.optimization_barrier((total, *foreign))[1:]
         side_rows = jnp.concatenate(foreign, axis=0)
         other_rows = flip(side_rows, "centre", 1)
-    kernels = [kernel for _, _, kernel in picked]
     residual_side = total.astype(jnp.bfloat16)
     rests, other_rests = [], []
     if hold_all:

time: 55.3 us -> 53.6 us (0.969)
  waiting for transfers between devices: 3.49 us -> 1.12 us
  Pallas kernels: 29.5 us -> 30.4 us
    ppermute x15, waiting for transfers between devices: 3.49 us -> 1.12 us  [flip(): return lax.ppermute(value, axis, [(i, i ^ distance) for i in range(count)])]
    pallas_call x9 -> x11, Pallas kernels: 29.5 us -> 30.4 us  [call(): pl.pallas_call(body, in_specs=[place for _, place in operands], out_specs...]
  transfers between devices with their start and end apart: 15 -> 15, of which waited for: 3 -> 1; matrix products, arithmetic and copies ran while one was open for 0% -> 0% of each run, Pallas kernels for 44% -> 47%
where the time goes in v1:
time: 53.6 us; the launch traced here: 53.4 us
  Pallas kernels  30.4 us (57%)
  starting transfers between devices  17.3 us (32%)
  local copies, waits for them, and re-layouts  1.86 us (3%)
  other arithmetic  1.49 us (3%)
  waiting for transfers between devices  1.12 us (2%)
  between operations  1.05 us (2%)
    pallas_call x11, Pallas kernels, call(): pl.pallas_call(body, in_specs=[place for _, place in operands], out_specs...  30.4 us
    ppermute x15, starting transfers between devices, flip(): return lax.ppermute(value, axis, [(i, i ^ distance) for i in range(count)])  17.3 us
    unnamed x11, local copies, waits for them, and re-layouts  1.81 us
    ppermute x15, waiting for transfers between devices, flip(): return lax.ppermute(value, axis, [(i, i ^ distance) for i in range(count)])  1.12 us
  transfers between devices with their start and end apart: 15, of which 1 were waited for; matrix products, arithmetic and copies ran while one was open for 0% of the time, Pallas kernels for 47%

profile of v1, /device:TPU:1, one launch (start us, length us, event | category | flops | bytes accessed | tf_op | source)
XLA Modules:
  0.0 53.4 jit_solution(3235838003646826381)
XLA Ops:
  0.6 0.0 copy-start
  0.7 0.7 %broadcast_subtract_fusion.1 = s32[32]{0:T(128)S(1)} fusion(s32[32]{0:T(128)} %param.7, s32[]{:T(128)S(6)} %mul.11), kind=kLoop, calls=%fused_computation.13 | loop fusion | flops 32 | bytes 260 | tf_op jit(solution)/shard_map/sub | solution.py:382
  1.3 0.7 %broadcast_subtract_fusion = s32[2048]{0:T(1024)S(1)} fusion(s32[2048]{0:T(1024)} %param.9, s32[]{:T(128)S(6)} %mul.9), kind=kLoop, calls=%fused_computation.12 | loop fusion | flops 2048 | bytes 16388 | tf_op jit(solution)/shard_map/sub | solution.py:381
  2.1 0.0 copy-done
  2.1 0.2 convolution_convert_fusion.refs_0_
  2.3 2.2 %collective-permute-start = (bf16[32,1024]{1,0:T(8,128)(2,1)S(1)}, bf16[32,1024]{1,0:T(8,128)(2,1)S(1)}, u32[]{:S(2)}, u32[]{:S(2)}) collective-permute-start(bf16[32,1024]{1,0:T(8,128)(2,1)S(1)} %convolution_convert_fusion.refs_0_), channel_id=1, source_target_pairs={{0,2},{1,3},{2,0},{3,1},{4,6},{5,7},{6,4},{7,5},{8,10},{9,11},{10,... | collective-permute-start | bytes 196616 | tf_op jit(solution)/shard_map/ppermute | solution.py:16
  4.5 2.3 %collective-permute-start.1 = (bf16[32,1024]{1,0:T(8,128)(2,1)S(1)}, bf16[32,1024]{1,0:T(8,128)(2,1)S(1)}, u32[]{:S(2)}, u32[]{:S(2)}) collective-permute-start(bf16[32,1024]{1,0:T(8,128)(2,1)S(1)} %convolution_convert_fusion.refs_0_), channel_id=1, source_target_pairs={{0,4},{1,5},{2,6},{3,7},{4,0},{5,1},{6,2},{7,3},{8,12},{9,13},{10,... | collective-permute-start | bytes 196616 | tf_op jit(solution)/shard_map/ppermute | solution.py:16
  6.8 0.0 collective-permute-start.2
  6.8 1.7 %copy-done.1 = f32[2048,301]{0,1:T(8,128)S(1)} copy-done((f32[2048,301]{0,1:T(8,128)S(1)}, f32[2048,301]{0,1:T(8,128)}, u32[]{:S(2)}) %copy-start.1) | copy-done | bytes 2465816
  8.5 5.9 %shard_map.77 = (bf16[301,2432]{1,0:T(8,128)(2,1)S(1)}, f32[1,2432]{1,0:T(1,128)S(1)}, f32[301,2048]{1,0:T(8,128)S(1)}, bf16[2305,1024]{1,0:T(8,128)(2,1)S(1)}) custom-call(s32[1,2048]{1,0:T(1,128)S(1)} %bitcast.6, f32[301,2048]{1,0:T(8,128)S(1)} %bitcast.5, bf16[2305,1024]{1,0:T(8,128)(2,1)} %pool_far.1), custom_call_target="tpu_custom_call" | custom-call | flops 1024 | bytes 1024 | tf_op jit(solution)/shard_map/pallas_call | solution.py:45
  14.3 0.0 collective-permute-done.refs_1_
  14.3 0.0 collective-permute-done.1.refs_2_
  14.4 0.0 collective-permute-done.2.refs_3_
  14.4 0.0 copy-done.2
  14.4 0.2 shard_map.78
  14.5 1.3 %collective-permute-start.3 = (bf16[128,1024]{1,0:T(8,128)(2,1)S(1)}, bf16[128,1024]{1,0:T(8,128)(2,1)S(1)}, u32[]{:S(2)}, u32[]{:S(2)}) collective-permute-start(bf16[128,1024]{1,0:T(8,128)(2,1)S(1)} %get-tuple-element.53.side_ref), channel_id=1, source_target_pairs={{0,1},{1,0},{2,3},{3,2},{4,5},{5,4},{6,7},{7,6},{8,9},{9,8},{10,11... | collective-permute-start | bytes 786440 | tf_op jit(solution)/shard_map/ppermute | solution.py:16
  15.8 1.6 %shard_map.79 = (bf16[256,1024]{1,0:T(8,128)(2,1)S(1)}, f32[1,256]{1,0:T(1,128)S(1)}) custom-call(s32[1,2048]{1,0:T(1,128)S(1)} %bitcast.7, bf16[2305,1024]{1,0:T(8,128)(2,1)S(1)} %get-tuple-element.55.pool_ref), custom_call_target="tpu_custom_call" | custom-call | flops 1024 | bytes 1024 | tf_op jit(solution)/shard_map/pallas_call | solution.py:45
  17.4 0.0 collective-permute-done.3.other_ref
  17.4 3.0 %shard_map.80 = (f32[301,128]{1,0:T(8,128)S(1)}, f32[301,128]{1,0:T(8,128)S(1)}) custom-call(bf16[128,1024]{1,0:T(8,128)(2,1)S(1)} %get-tuple-element.53.side_ref, bf16[128,1024]{1,0:T(8,128)(2,1)S(1)} %collective-permute-done.3.other_ref, bf16[2305,1024]{1,0:T(8,128)(2,1)S(1)} %get-tuple-element.55.pool_ref, f32[1,2432]{1,0:T(1,128)S(1)} %get-tuple-element.59.square_ref, ...), custom_call_target="tpu_custom_call" | custom-call | flops 1024 | bytes 1024 | tf_op jit(solution)/shard_map/pallas_call | solution.py:45
  20.4 0.1 collective-permute-start.4
  20.5 1.6 %shard_map.81 = (bf16[256,1024]{1,0:T(8,128)(2,1)S(1)}, f32[1,256]{1,0:T(1,128)S(1)}) custom-call(s32[1,2048]{1,0:T(1,128)S(1)} %bitcast.8, bf16[2305,1024]{1,0:T(8,128)(2,1)S(1)} %get-tuple-element.55.pool_ref), custom_call_target="tpu_custom_call" | custom-call | flops 1024 | bytes 1024 | tf_op jit(solution)/shard_map/pallas_call | solution.py:45
  22.1 0.0 collective-permute-done.4
  22.1 0.7 %collective-permute-start.5 = (f32[301,128]{1,0:T(8,128)S(1)}, f32[301,128]{1,0:T(8,128)S(1)}, u32[]{:S(2)}, u32[]{:S(2)}) collective-permute-start(f32[301,128]{1,0:T(8,128)S(1)} %subtract_add_fusion), channel_id=1, source_target_pairs={{0,2},{1,3},{2,0},{3,1},{4,6},{5,7},{6,4},{7,5},{8,10},{9,11},{10,... | collective-permute-start | bytes 462344 | tf_op jit(solution)/shard_map/ppermute | solution.py:16
  22.8 1.2 %collective-permute-start.7 = (bf16[128,1024]{1,0:T(8,128)(2,1)S(1)}, bf16[128,1024]{1,0:T(8,128)(2,1)S(1)}, u32[]{:S(2)}, u32[]{:S(2)}) collective-permute-start(bf16[128,1024]{1,0:T(8,128)(2,1)S(1)} %get-tuple-element.53.side_ref), channel_id=1, source_target_pairs={{0,8},{8,0},{16,24},{24,16},{1,9},{9,1},{17,25},{25,17},{2,10},{10... | collective-permute-start | bytes 786440 | tf_op jit(solution)/shard_map/ppermute | solution.py:16
  24.0 1.2 %collective-permute-start.8 = (bf16[128,1024]{1,0:T(8,128)(2,1)S(1)}, bf16[128,1024]{1,0:T(8,128)(2,1)S(1)}, u32[]{:S(2)}, u32[]{:S(2)}) collective-permute-start(bf16[128,1024]{1,0:T(8,128)(2,1)S(1)} %get-tuple-element.53.side_ref), channel_id=1, source_target_pairs={{0,16},{8,24},{16,0},{24,8},{1,17},{9,25},{17,1},{25,9},{2,18},{10... | collective-permute-start | bytes 786440 | tf_op jit(solution)/shard_map/ppermute | solution.py:16
  25.2 0.2 collective-permute-start.9
  25.4 3.7 %shard_map.82 = (bf16[512,1024]{1,0:T(8,128)(2,1)S(1)}, f32[1,512]{1,0:T(1,128)S(1)}, bf16[256,1024]{1,0:T(8,128)(2,1)S(1)}) custom-call(s32[1,2048]{1,0:T(1,128)S(1)} %bitcast.9, bf16[2305,1024]{1,0:T(8,128)(2,1)S(1)} %get-tuple-element.55.pool_ref, bf16[128,1024]{1,0:T(8,128)(2,1)S(1)} %get-tuple-element.53.side_ref, ...), custom_call_target="tpu_custom_call" | custom-call | flops 1024 | bytes 1024 | tf_op jit(solution)/shard_map/pallas_call | solution.py:45
  29.1 0.0 collective-permute-done.5
  29.1 3.3 %collective-permute-start.6 = (f32[301,128]{1,0:T(8,128)S(1)}, f32[301,128]{1,0:T(8,128)S(1)}, u32[]{:S(2)}, u32[]{:S(2)}) collective-permute-start(f32[301,128]{1,0:T(8,128)S(1)} %add.14), channel_id=1, source_target_pairs={{0,4},{1,5},{2,6},{3,7},{4,0},{5,1},{6,2},{7,3},{8,12},{9,13},{10,... | collective-permute-start | bytes 462344 | tf_op jit(solution)/shard_map/ppermute | solution.py:16
  32.4 6.3 %shard_map.83 = (bf16[1024,1024]{1,0:T(8,128)(2,1)S(1)}, f32[1,1024]{1,0:T(1,128)S(1)}, bf16[256,1024]{1,0:T(8,128)(2,1)S(1)}) custom-call(s32[1,2048]{1,0:T(1,128)S(1)} %bitcast.10, bf16[2305,1024]{1,0:T(8,128)(2,1)S(1)} %get-tuple-element.55.pool_ref, bf16[128,1024]{1,0:T(8,128)(2,1)S(1)} %get-tuple-element.53.side_ref, ...), custom_call_target="tpu_custom_call" | custom-call | flops 1024 | bytes 1024 | tf_op jit(solution)/shard_map/pallas_call | solution.py:45
  38.7 1.1 %collective-permute-done.6 = f32[301,128]{1,0:T(8,128)S(1)} collective-permute-done((f32[301,128]{1,0:T(8,128)S(1)}, f32[301,128]{1,0:T(8,128)S(1)}, u32[]{:S(2)}, u32[]{:S(2)}) %collective-permute-start.6) | collective-permute-done | bytes 154144 | tf_op jit(solution)/shard_map/ppermute | solution.py:16
  39.8 0.0 collective-permute-done.7
  39.8 0.0 collective-permute-done.8
  39.8 0.0 collective-permute-done.9
  39.9 0.9 %collective-permute-start.10 = (bf16[384,1024]{1,0:T(8,128)(2,1)S(1)}, bf16[384,1024]{1,0:T(8,128)(2,1)S(1)}, u32[]{:S(2)}, u32[]{:S(2)}) collective-permute-start(bf16[384,1024]{1,0:T(8,128)(2,1)S(1)} %constant_dynamic-update-slice_fusion.refs_0_), channel_id=1, source_target_pairs={{0,1},{1,0},{2,3},{3,2},{4,5},{5,4},{6,7},{7,6},{8,9},{9,8},{10,11... | collective-permute-start | bytes 2359304 | tf_op jit(solution)/shard_map/ppermute | solution.py:16
  40.8 1.3 %collective-permute-start.11 = (bf16[301,128]{1,0:T(8,128)(2,1)S(1)}, bf16[301,128]{1,0:T(8,128)(2,1)S(1)}, u32[]{:S(2)}, u32[]{:S(2)}) collective-permute-start(bf16[301,128]{1,0:T(8,128)(2,1)S(1)} %convert_element_type.8), channel_id=1, source_target_pairs={{0,8},{8,0},{16,24},{24,16},{1,9},{9,1},{17,25},{25,17},{2,10},{10... | collective-permute-start | bytes 231176 | tf_op jit(solution)/shard_map/ppermute | solution.py:16
  42.2 1.2 %collective-permute-start.12 = (bf16[301,128]{1,0:T(8,128)(2,1)S(1)}, bf16[301,128]{1,0:T(8,128)(2,1)S(1)}, u32[]{:S(2)}, u32[]{:S(2)}) collective-permute-start(bf16[301,128]{1,0:T(8,128)(2,1)S(1)} %convert_element_type.8), channel_id=1, source_target_pairs={{0,16},{8,24},{16,0},{24,8},{1,17},{9,25},{17,1},{25,9},{2,18},{10... | collective-permute-start | bytes 231176 | tf_op jit(solution)/shard_map/ppermute | solution.py:16
  43.4 0.1 collective-permute-start.13
  43.5 2.3 %shard_map.84.refs_2_ = bf16[384,2048]{1,0:T(8,128)(2,1)S(1)} custom-call(bf16[384,1024]{1,0:T(8,128)(2,1)S(1)} %constant_dynamic-update-slice_fusion.refs_0_, bf16[256,1024]{1,0:T(8,128)(2,1)S(1)} %get-tuple-element.56.refs_0_.refs_1_, f32[1,256]{1,0:T(1,128)S(1)} %get-tuple-element.57.refs_1_.refs_2_, ...), custom_call_target="tpu_custom_call" | custom-call | flops 1024 | bytes 1024 | tf_op jit(solution)/shard_map/pallas_call | solution.py:45
  45.8 0.0 collective-permute-done.10.refs_0_
  45.8 2.3 %shard_map.85.refs_2_ = bf16[384,2048]{1,0:T(8,128)(2,1)S(1)} custom-call(bf16[384,1024]{1,0:T(8,128)(2,1)S(1)} %collective-permute-done.10.refs_0_, bf16[256,1024]{1,0:T(8,128)(2,1)S(1)} %get-tuple-element.56.refs_0_.refs_1_, f32[1,256]{1,0:T(1,128)S(1)} %get-tuple-element.57.refs_1_.refs_2_, bf16[256,1024]{1,0:T(8,128)(2,1)S(1)} %get-tuple-element.65.refs_2_.refs_3_, ...), custom_call_target="tpu_custom_call" | custom-call | flops 1024 | bytes 1024 | tf_op jit(solution)/shard_map/pallas_call | solution.py:45
  48.1 0.0 collective-permute-done.11
  48.1 0.0 collective-permute-done.12
  48.1 0.0 collective-permute-done.13
  48.2 1.2 %collective-permute-start.14 = (bf16[301,512]{1,0:T(8,128)(2,1)S(1)}, bf16[301,512]{1,0:T(8,128)(2,1)S(1)}, u32[]{:S(2)}, u32[]{:S(2)}) collective-permute-start(bf16[301,512]{1,0:T(8,128)(2,1)S(1)} %constant_dynamic-update-slice_fusion.3.residual_ref), channel_id=1, source_target_pairs={{0,1},{1,0},{2,3},{3,2},{4,5},{5,4},{6,7},{7,6},{8,9},{9,8},{10,11... | collective-permute-start | bytes 924680 | tf_op jit(solution)/shard_map/ppermute | solution.py:16
  49.4 1.7 %shard_map.86 = (f32[301,2048]{1,0:T(8,128)S(1)}, f32[32,301]{1,0:T(8,128)}) custom-call(s32[1]{0:T(128)} %bitcast.1.place_ref, f32[301,128]{1,0:T(8,128)S(1)} %add.15.total_ref, bf16[301,512]{1,0:T(8,128)(2,1)S(1)} %constant_dynamic-update-slice_fusion.3.residual_ref, f32[301,2048]{1,0:T(8,128)S(1)} %get-tuple-element.83.base_ref, ...), custom_call_target="tpu_custom_call" | custom-call | flops 1024 | bytes 1024 | tf_op jit(solution)/shard_map/pallas_call | solution.py:45
  51.1 0.0 collective-permute-done.14.residual_ref
  51.1 2.0 %shard_map.87 = f32[301,2048]{1,0:T(8,128)} custom-call(bf16[301,512]{1,0:T(8,128)(2,1)S(1)} %collective-permute-done.14.residual_ref, f32[301,2048]{1,0:T(8,128)S(1)} %get-tuple-element.87.base_ref, bf16[256,1024]{1,0:T(8,128)(2,1)S(1)} %get-tuple-element.84.refs_0_, bf16[256,1024]{1,0:T(8,128)(2,1)S(1)} %get-tuple-element.85.refs_1_, ...), custom_call_target="tpu_custom_call" | custom-call | flops 1024 | bytes 1024 | tf_op jit(solution)/shard_map/pallas_call | solution.py:45
  (16 shorter events, 0.3 us)
Async XLA Ops:
  0.6 1.4 %copy-start = (bf16[41,1024]{1,0:T(8,128)(2,1)S(1)}, bf16[41,1024]{1,0:T(8,128)(2,1)}, u32[]{:S(2)}) copy-start(bf16[41,1024]{1,0:T(8,128)(2,1)} %param.6) | copy-start | bytes 251908
  2.3 12.1 %collective-permute-start = (bf16[32,1024]{1,0:T(8,128)(2,1)S(1)}, bf16[32,1024]{1,0:T(8,128)(2,1)S(1)}, u32[]{:S(2)}, u32[]{:S(2)}) collective-permute-start(bf16[32,1024]{1,0:T(8,128)(2,1)S(1)} %convolution_convert_fusion.refs_0_), channel_id=1, source_target_pairs={{0,2},{1,3},{2,0},{3,1},{4,6},{5,7},{6,4},{7,5},{8,10},{9,11},{10,... | collective-permute-start | bytes 196616 | tf_op jit(solution)/shard_map/ppermute | solution.py:16
  4.5 9.9 %collective-permute-start.1 = (bf16[32,1024]{1,0:T(8,128)(2,1)S(1)}, bf16[32,1024]{1,0:T(8,128)(2,1)S(1)}, u32[]{:S(2)}, u32[]{:S(2)}) collective-permute-start(bf16[32,1024]{1,0:T(8,128)(2,1)S(1)} %convolution_convert_fusion.refs_0_), channel_id=1, source_target_pairs={{0,4},{1,5},{2,6},{3,7},{4,0},{5,1},{6,2},{7,3},{8,12},{9,13},{10,... | collective-permute-start | bytes 196616 | tf_op jit(solution)/shard_map/ppermute | solution.py:16
  6.8 7.6 %collective-permute-start.2 = (bf16[32,1024]{1,0:T(8,128)(2,1)S(1)}, bf16[32,1024]{1,0:T(8,128)(2,1)S(1)}, u32[]{:S(2)}, u32[]{:S(2)}) collective-permute-start(bf16[32,1024]{1,0:T(8,128)(2,1)S(1)} %convolution_convert_fusion.refs_0_), channel_id=1, source_target_pairs={{0,6},{1,7},{2,4},{3,5},{4,2},{5,3},{6,0},{7,1},{8,14},{9,15},{10,... | collective-permute-start | bytes 196616 | tf_op jit(solution)/shard_map/ppermute | solution.py:16
  6.8 1.7 %copy-start.1 = (f32[2048,301]{0,1:T(8,128)S(1)}, f32[2048,301]{0,1:T(8,128)}, u32[]{:S(2)}) copy-start(f32[2048,301]{0,1:T(8,128)} %param.11) | copy-start | bytes 7397380
  8.5 5.9 %copy-start.2 = (f32[32,301]{1,0:T(8,128)S(1)}, f32[32,301]{1,0:T(8,128)}, u32[]{:S(2)}) copy-start(f32[32,301]{1,0:T(8,128)} %targets_ref.1) | copy-start | bytes 115588
  14.5 2.9 %collective-permute-start.3 = (bf16[128,1024]{1,0:T(8,128)(2,1)S(1)}, bf16[128,1024]{1,0:T(8,128)(2,1)S(1)}, u32[]{:S(2)}, u32[]{:S(2)}) collective-permute-start(bf16[128,1024]{1,0:T(8,128)(2,1)S(1)} %get-tuple-element.53.side_ref), channel_id=1, source_target_pairs={{0,1},{1,0},{2,3},{3,2},{4,5},{5,4},{6,7},{7,6},{8,9},{9,8},{10,11... | collective-permute-start | bytes 786440 | tf_op jit(solution)/shard_map/ppermute | solution.py:16
  20.4 1.7 %collective-permute-start.4 = (f32[301,128]{1,0:T(8,128)S(1)}, f32[301,128]{1,0:T(8,128)S(1)}, u32[]{:S(2)}, u32[]{:S(2)}) collective-permute-start(f32[301,128]{1,0:T(8,128)S(1)} %get-tuple-element.63), channel_id=1, source_target_pairs={{0,1},{1,0},{2,3},{3,2},{4,5},{5,4},{6,7},{7,6},{8,9},{9,8},{10,11... | collective-permute-start | bytes 462344 | tf_op jit(solution)/shard_map/ppermute | solution.py:16
  22.1 7.0 %collective-permute-start.5 = (f32[301,128]{1,0:T(8,128)S(1)}, f32[301,128]{1,0:T(8,128)S(1)}, u32[]{:S(2)}, u32[]{:S(2)}) collective-permute-start(f32[301,128]{1,0:T(8,128)S(1)} %subtract_add_fusion), channel_id=1, source_target_pairs={{0,2},{1,3},{2,0},{3,1},{4,6},{5,7},{6,4},{7,5},{8,10},{9,11},{10,... | collective-permute-start | bytes 462344 | tf_op jit(solution)/shard_map/ppermute | solution.py:16
  22.8 17.0 %collective-permute-start.7 = (bf16[128,1024]{1,0:T(8,128)(2,1)S(1)}, bf16[128,1024]{1,0:T(8,128)(2,1)S(1)}, u32[]{:S(2)}, u32[]{:S(2)}) collective-permute-start(bf16[128,1024]{1,0:T(8,128)(2,1)S(1)} %get-tuple-element.53.side_ref), channel_id=1, source_target_pairs={{0,8},{8,0},{16,24},{24,16},{1,9},{9,1},{17,25},{25,17},{2,10},{10... | collective-permute-start | bytes 786440 | tf_op jit(solution)/shard_map/ppermute | solution.py:16
  24.0 15.8 %collective-permute-start.8 = (bf16[128,1024]{1,0:T(8,128)(2,1)S(1)}, bf16[128,1024]{1,0:T(8,128)(2,1)S(1)}, u32[]{:S(2)}, u32[]{:S(2)}) collective-permute-start(bf16[128,1024]{1,0:T(8,128)(2,1)S(1)} %get-tuple-element.53.side_ref), channel_id=1, source_target_pairs={{0,16},{8,24},{16,0},{24,8},{1,17},{9,25},{17,1},{25,9},{2,18},{10... | collective-permute-start | bytes 786440 | tf_op jit(solution)/shard_map/ppermute | solution.py:16
  25.2 14.6 %collective-permute-start.9 = (bf16[128,1024]{1,0:T(8,128)(2,1)S(1)}, bf16[128,1024]{1,0:T(8,128)(2,1)S(1)}, u32[]{:S(2)}, u32[]{:S(2)}) collective-permute-start(bf16[128,1024]{1,0:T(8,128)(2,1)S(1)} %get-tuple-element.53.side_ref), channel_id=1, source_target_pairs={{0,24},{8,16},{16,8},{24,0},{1,25},{9,17},{17,9},{25,1},{2,26},{10... | collective-permute-start | bytes 786440 | tf_op jit(solution)/shard_map/ppermute | solution.py:16
  29.1 10.7 %collective-permute-start.6 = (f32[301,128]{1,0:T(8,128)S(1)}, f32[301,128]{1,0:T(8,128)S(1)}, u32[]{:S(2)}, u32[]{:S(2)}) collective-permute-start(f32[301,128]{1,0:T(8,128)S(1)} %add.14), channel_id=1, source_target_pairs={{0,4},{1,5},{2,6},{3,7},{4,0},{5,1},{6,2},{7,3},{8,12},{9,13},{10,... | collective-permute-start | bytes 462344 | tf_op jit(solution)/shard_map/ppermute | solution.py:16
  39.9 5.9 %collective-permute-start.10 = (bf16[384,1024]{1,0:T(8,128)(2,1)S(1)}, bf16[384,1024]{1,0:T(8,128)(2,1)S(1)}, u32[]{:S(2)}, u32[]{:S(2)}) collective-permute-start(bf16[384,1024]{1,0:T(8,128)(2,1)S(1)} %constant_dynamic-update-slice_fusion.refs_0_), channel_id=1, source_target_pairs={{0,1},{1,0},{2,3},{3,2},{4,5},{5,4},{6,7},{7,6},{8,9},{9,8},{10,11... | collective-permute-start | bytes 2359304 | tf_op jit(solution)/shard_map/ppermute | solution.py:16
  40.8 7.3 %collective-permute-start.11 = (bf16[301,128]{1,0:T(8,128)(2,1)S(1)}, bf16[301,128]{1,0:T(8,128)(2,1)S(1)}, u32[]{:S(2)}, u32[]{:S(2)}) collective-permute-start(bf16[301,128]{1,0:T(8,128)(2,1)S(1)} %convert_element_type.8), channel_id=1, source_target_pairs={{0,8},{8,0},{16,24},{24,16},{1,9},{9,1},{17,25},{25,17},{2,10},{10... | collective-permute-start | bytes 231176 | tf_op jit(solution)/shard_map/ppermute | solution.py:16
  42.2 5.9 %collective-permute-start.12 = (bf16[301,128]{1,0:T(8,128)(2,1)S(1)}, bf16[301,128]{1,0:T(8,128)(2,1)S(1)}, u32[]{:S(2)}, u32[]{:S(2)}) collective-permute-start(bf16[301,128]{1,0:T(8,128)(2,1)S(1)} %convert_element_type.8), channel_id=1, source_target_pairs={{0,16},{8,24},{16,0},{24,8},{1,17},{9,25},{17,1},{25,9},{2,18},{10... | collective-permute-start | bytes 231176 | tf_op jit(solution)/shard_map/ppermute | solution.py:16
  43.4 4.7 %collective-permute-start.13 = (bf16[301,128]{1,0:T(8,128)(2,1)S(1)}, bf16[301,128]{1,0:T(8,128)(2,1)S(1)}, u32[]{:S(2)}, u32[]{:S(2)}) collective-permute-start(bf16[301,128]{1,0:T(8,128)(2,1)S(1)} %convert_element_type.8), channel_id=1, source_target_pairs={{0,24},{8,16},{16,8},{24,0},{1,25},{9,17},{17,9},{25,1},{2,26},{10... | collective-permute-start | bytes 231176 | tf_op jit(solution)/shard_map/ppermute | solution.py:16
  48.2 2.9 %collective-permute-start.14 = (bf16[301,512]{1,0:T(8,128)(2,1)S(1)}, bf16[301,512]{1,0:T(8,128)(2,1)S(1)}, u32[]{:S(2)}, u32[]{:S(2)}) collective-permute-start(bf16[301,512]{1,0:T(8,128)(2,1)S(1)} %constant_dynamic-update-slice_fusion.3.residual_ref), channel_id=1, source_target_pairs={{0,1},{1,0},{2,3},{3,2},{4,5},{5,4},{6,7},{7,6},{8,9},{9,8},{10,11... | collective-permute-start | bytes 924680 | tf_op jit(solution)/shard_map/ppermute | solution.py:16

commit v2 on v1

--- a/solution.py
+++ b/solution.py
@@ -53,10 +53,18 @@
     )(*arrays)
 
 
+def narrow(index, pool_ref):
+    return index.astype(jnp.int16 if pool_ref.shape[0] < 1 << 15 else jnp.int32)
+
+
+def one_hot(hit):
+    return jnp.where(hit, jnp.bfloat16(1.0), jnp.bfloat16(0.0))
+
+
 def turned(column):
     return jnp.concatenate(
         [
-            jnp.broadcast_to(column[at : at + LANES], (LANES, LANES)).T[:1]
+            jnp.broadcast_to(column[at : at + LANES], (LANES, 8)).T[:1]
             for at in range(0, column.shape[0], LANES)
         ],
         axis=1,
@@ -76,23 +84,23 @@
 def place_body(index_ref, base_ref, pool_far, placed_ref, square_ref, kept_ref, pool_ref, done_ref):
     fetch = pltpu.make_async_copy(pool_far, pool_ref, done_ref)
     fetch.start()
-    index = index_ref[...]
+    index = narrow(index_ref[...], pool_ref)
     base = base_ref[...]
     kept_ref[...] = base
     half = base.astype(jnp.bfloat16)
     cuts = spans(placed_ref.shape[1], 2 * LANES)
     left, arrival = list(cuts), min(3, len(cuts) - 1)
     for turn, (at, size) in enumerate(cuts):
-        place = lax.broadcasted_iota(jnp.int32, (size, index.shape[1]), 0) + at
-        chosen = jnp.where(index == place, 1.0, 0.0).astype(jnp.bfloat16)
+        place = lax.broadcasted_iota(index.dtype, (size, index.shape[1]), 0)
+        chosen = one_hot(index - jnp.asarray(at, index.dtype) == place)
         placed_ref[:, at : at + size] = contract_last(half, chosen).astype(jnp.bfloat16)
         if turn == arrival:
             fetch.wait()
         share = -(-len(left) // (len(cuts) - turn)) if turn >= arrival else 0
         for from_row, count in left[:share]:
             rows = pool_rows(pool_ref, from_row, count).astype(jnp.float32)
-            square_ref[:, from_row : from_row + count] = turned(
-                jnp.sum(rows * rows, axis=1, keepdims=True)
+            square_ref[from_row : from_row + count, :] = jnp.broadcast_to(
+                jnp.sum(rows * rows, axis=1, keepdims=True), (count, LANES)
             )
         left = left[share:]
 
@@ -104,12 +112,12 @@
         [(index, WHOLE), (base, WHOLE), (pool, FAR)],
         [
             ((base.shape[0], width), jnp.bfloat16, WHOLE),
-            ((1, width), jnp.float32, WHOLE),
+            ((width, LANES), jnp.float32, WHOLE),
             (base.shape, jnp.float32, WHOLE),
             (pool.shape, jnp.bfloat16, WHOLE),
         ],
         [pltpu.SemaphoreType.DMA(())],
-        limit=41,
+        limit=40,
     )
 
 
@@ -176,8 +184,10 @@
     own_square = turned(own_square)
     for at, size in spans(placed_ref.shape[1], 4 * LANES):
         cross = contract_last(pool_rows(pool_ref, at, size), samples)
-        pool_square = column_of(square_ref[:, at : at + size])[:, :1]
-        kernel_ref[at : at + size, :] = kernel_of(pool_square + own_square + cross)
+        for lane in range(0, samples.shape[0], LANES):
+            lanes = slice(lane, lane + LANES)
+            squared = square_ref[at : at + size, :] + own_square[:, lanes] + cross[:, lanes]
+            kernel_ref[at : at + size, lanes] = kernel_of(squared)
     terms = jnp.dot(placed_ref[...], kernel_ref[...], preferred_element_type=jnp.float32)
     rows = side_ref.shape[0]
     terms_ref[...] = terms[:, :rows]
@@ -197,10 +207,11 @@
 def pick_span(index_ref, pool_ref, rows_ref, square_ref, first, at, size):
     whole = pool_ref.shape[0] // LANES * LANES
     wanted = column_of(index_ref[:, first + at : first + at + size])
-    lane = lax.broadcasted_iota(jnp.int32, (size, LANES), 1)
+    place = narrow(wanted, pool_ref)
+    lane = lax.broadcasted_iota(place.dtype, (size, LANES), 1)
     chosen = jnp.concatenate(
         [
-            jnp.where(wanted == lane + part, 1.0, 0.0).astype(jnp.bfloat16)
+            one_hot(place - jnp.asarray(part, place.dtype) == lane)
             for part in range(0, whole, LANES)
         ],
         axis=1,

time: 53.6 us -> 52.6 us (0.981)
  Pallas kernels: 30.4 us -> 29.1 us
    pallas_call x11, Pallas kernels: 30.4 us -> 29.1 us  [call(): pl.pallas_call(body, in_specs=[place for _, place in operands], out_specs...]
  transfers between devices with their start and end apart: 15 -> 15, of which waited for: 1 -> 1; matrix products, arithmetic and copies ran while one was open for 0% -> 0% of each run, Pallas kernels for 47% -> 46%
where the time goes in v2:
time: 52.6 us; the launch traced here: 52.4 us
  Pallas kernels  29.1 us (55%)
  starting transfers between devices  17.4 us (33%)
  local copies, waits for them, and re-layouts  1.86 us (4%)
  other arithmetic  1.49 us (3%)
  waiting for transfers between devices  1.26 us (2%)
  between operations  1.05 us (2%)
    pallas_call x11, Pallas kernels, call(): pl.pallas_call(body, in_specs=[place for _, place in operands], out_specs...  29.1 us
    ppermute x15, starting transfers between devices, flip(): return lax.ppermute(value, axis, [(i, i ^ distance) for i in range(count)])  17.4 us
    unnamed x11, local copies, waits for them, and re-layouts  1.81 us
    ppermute x15, waiting for transfers between devices, flip(): return lax.ppermute(value, axis, [(i, i ^ distance) for i in range(count)])  1.26 us
  transfers between devices with their start and end apart: 15, of which 1 were waited for; matrix products, arithmetic and copies ran while one was open for 0% of the time, Pallas kernels for 46%

profile of v2, /device:TPU:1, one launch (start us, length us, event | category | flops | bytes accessed | tf_op | source)
XLA Modules:
  0.0 52.4 jit_solution(8426438443832153565)
XLA Ops:
  0.6 0.0 copy-start
  0.7 0.7 %broadcast_subtract_fusion.1 = s32[32]{0:T(128)S(1)} fusion(s32[32]{0:T(128)} %param.7, s32[]{:T(128)S(6)} %mul.11), kind=kLoop, calls=%fused_computation.13 | loop fusion | flops 32 | bytes 260 | tf_op jit(solution)/shard_map/sub | solution.py:393
  1.3 0.7 %broadcast_subtract_fusion = s32[2048]{0:T(1024)S(1)} fusion(s32[2048]{0:T(1024)} %param.9, s32[]{:T(128)S(6)} %mul.9), kind=kLoop, calls=%fused_computation.12 | loop fusion | flops 2048 | bytes 16388 | tf_op jit(solution)/shard_map/sub | solution.py:392
  2.1 0.0 copy-done
  2.1 0.2 convolution_convert_fusion.refs_0_
  2.3 2.2 %collective-permute-start = (bf16[32,1024]{1,0:T(8,128)(2,1)S(1)}, bf16[32,1024]{1,0:T(8,128)(2,1)S(1)}, u32[]{:S(2)}, u32[]{:S(2)}) collective-permute-start(bf16[32,1024]{1,0:T(8,128)(2,1)S(1)} %convolution_convert_fusion.refs_0_), channel_id=1, source_target_pairs={{0,2},{1,3},{2,0},{3,1},{4,6},{5,7},{6,4},{7,5},{8,10},{9,11},{10,... | collective-permute-start | bytes 196616 | tf_op jit(solution)/shard_map/ppermute | solution.py:16
  4.5 2.3 %collective-permute-start.1 = (bf16[32,1024]{1,0:T(8,128)(2,1)S(1)}, bf16[32,1024]{1,0:T(8,128)(2,1)S(1)}, u32[]{:S(2)}, u32[]{:S(2)}) collective-permute-start(bf16[32,1024]{1,0:T(8,128)(2,1)S(1)} %convolution_convert_fusion.refs_0_), channel_id=1, source_target_pairs={{0,4},{1,5},{2,6},{3,7},{4,0},{5,1},{6,2},{7,3},{8,12},{9,13},{10,... | collective-permute-start | bytes 196616 | tf_op jit(solution)/shard_map/ppermute | solution.py:16
  6.8 0.0 collective-permute-start.2
  6.8 1.7 %copy-done.1 = f32[2048,301]{0,1:T(8,128)S(1)} copy-done((f32[2048,301]{0,1:T(8,128)S(1)}, f32[2048,301]{0,1:T(8,128)}, u32[]{:S(2)}) %copy-start.1) | copy-done | bytes 2465816
  8.5 5.1 %shard_map.77 = (bf16[301,2432]{1,0:T(8,128)(2,1)S(1)}, f32[2432,128]{1,0:T(8,128)S(1)}, f32[301,2048]{1,0:T(8,128)S(1)}, bf16[2305,1024]{1,0:T(8,128)(2,1)S(1)}) custom-call(s32[1,2048]{1,0:T(1,128)S(1)} %bitcast.6, f32[301,2048]{1,0:T(8,128)S(1)} %bitcast.5, bf16[2305,1024]{1,0:T(8,128)(2,1)} %pool_far.1), custom_call_target="tpu_custom_call" | custom-call | flops 1024 | bytes 1024 | tf_op jit(solution)/shard_map/pallas_call | solution.py:45
  13.6 0.0 collective-permute-done.refs_1_
  13.6 0.0 collective-permute-done.1.refs_2_
  13.6 0.0 collective-permute-done.2.refs_3_
  13.6 0.0 copy-done.2
  13.6 0.2 shard_map.78
  13.8 1.3 %collective-permute-start.3 = (bf16[128,1024]{1,0:T(8,128)(2,1)S(1)}, bf16[128,1024]{1,0:T(8,128)(2,1)S(1)}, u32[]{:S(2)}, u32[]{:S(2)}) collective-permute-start(bf16[128,1024]{1,0:T(8,128)(2,1)S(1)} %get-tuple-element.53.side_ref), channel_id=1, source_target_pairs={{0,1},{1,0},{2,3},{3,2},{4,5},{5,4},{6,7},{7,6},{8,9},{9,8},{10,11... | collective-permute-start | bytes 786440 | tf_op jit(solution)/shard_map/ppermute | solution.py:16
  15.1 1.6 %shard_map.79 = (bf16[256,1024]{1,0:T(8,128)(2,1)S(1)}, f32[1,256]{1,0:T(1,128)S(1)}) custom-call(s32[1,2048]{1,0:T(1,128)S(1)} %bitcast.7, bf16[2305,1024]{1,0:T(8,128)(2,1)S(1)} %get-tuple-element.55.pool_ref), custom_call_target="tpu_custom_call" | custom-call | flops 1024 | bytes 1024 | tf_op jit(solution)/shard_map/pallas_call | solution.py:45
  16.6 0.0 collective-permute-done.3.other_ref
  16.6 2.9 %shard_map.80 = (f32[301,128]{1,0:T(8,128)S(1)}, f32[301,128]{1,0:T(8,128)S(1)}) custom-call(bf16[128,1024]{1,0:T(8,128)(2,1)S(1)} %get-tuple-element.53.side_ref, bf16[128,1024]{1,0:T(8,128)(2,1)S(1)} %collective-permute-done.3.other_ref, bf16[2305,1024]{1,0:T(8,128)(2,1)S(1)} %get-tuple-element.55.pool_ref, f32[2432,128]{1,0:T(8,128)S(1)} %get-tuple-element.59.square_ref, ...), custom_call_target="tpu_custom_call" | custom-call | flops 1024 | bytes 1024 | tf_op jit(solution)/shard_map/pallas_call | solution.py:45
  19.6 0.1 collective-permute-start.4
  19.6 1.6 %shard_map.81 = (bf16[256,1024]{1,0:T(8,128)(2,1)S(1)}, f32[1,256]{1,0:T(1,128)S(1)}) custom-call(s32[1,2048]{1,0:T(1,128)S(1)} %bitcast.8, bf16[2305,1024]{1,0:T(8,128)(2,1)S(1)} %get-tuple-element.55.pool_ref), custom_call_target="tpu_custom_call" | custom-call | flops 1024 | bytes 1024 | tf_op jit(solution)/shard_map/pallas_call | solution.py:45
  21.2 0.0 collective-permute-done.4
  21.3 0.7 %collective-permute-start.5 = (f32[301,128]{1,0:T(8,128)S(1)}, f32[301,128]{1,0:T(8,128)S(1)}, u32[]{:S(2)}, u32[]{:S(2)}) collective-permute-start(f32[301,128]{1,0:T(8,128)S(1)} %subtract_add_fusion), channel_id=1, source_target_pairs={{0,2},{1,3},{2,0},{3,1},{4,6},{5,7},{6,4},{7,5},{8,10},{9,11},{10,... | collective-permute-start | bytes 462344 | tf_op jit(solution)/shard_map/ppermute | solution.py:16
  21.9 1.2 %collective-permute-start.7 = (bf16[128,1024]{1,0:T(8,128)(2,1)S(1)}, bf16[128,1024]{1,0:T(8,128)(2,1)S(1)}, u32[]{:S(2)}, u32[]{:S(2)}) collective-permute-start(bf16[128,1024]{1,0:T(8,128)(2,1)S(1)} %get-tuple-element.53.side_ref), channel_id=1, source_target_pairs={{0,8},{8,0},{16,24},{24,16},{1,9},{9,1},{17,25},{25,17},{2,10},{10... | collective-permute-start | bytes 786440 | tf_op jit(solution)/shard_map/ppermute | solution.py:16
  23.2 1.2 %collective-permute-start.8 = (bf16[128,1024]{1,0:T(8,128)(2,1)S(1)}, bf16[128,1024]{1,0:T(8,128)(2,1)S(1)}, u32[]{:S(2)}, u32[]{:S(2)}) collective-permute-start(bf16[128,1024]{1,0:T(8,128)(2,1)S(1)} %get-tuple-element.53.side_ref), channel_id=1, source_target_pairs={{0,16},{8,24},{16,0},{24,8},{1,17},{9,25},{17,1},{25,9},{2,18},{10... | collective-permute-start | bytes 786440 | tf_op jit(solution)/shard_map/ppermute | solution.py:16
  24.4 0.2 collective-permute-start.9
  24.6 3.4 %shard_map.82 = (bf16[512,1024]{1,0:T(8,128)(2,1)S(1)}, f32[1,512]{1,0:T(1,128)S(1)}, bf16[256,1024]{1,0:T(8,128)(2,1)S(1)}) custom-call(s32[1,2048]{1,0:T(1,128)S(1)} %bitcast.9, bf16[2305,1024]{1,0:T(8,128)(2,1)S(1)} %get-tuple-element.55.pool_ref, bf16[128,1024]{1,0:T(8,128)(2,1)S(1)} %get-tuple-element.53.side_ref, ...), custom_call_target="tpu_custom_call" | custom-call | flops 1024 | bytes 1024 | tf_op jit(solution)/shard_map/pallas_call | solution.py:45
  28.0 0.0 collective-permute-done.5
  28.1 3.4 %collective-permute-start.6 = (f32[301,128]{1,0:T(8,128)S(1)}, f32[301,128]{1,0:T(8,128)S(1)}, u32[]{:S(2)}, u32[]{:S(2)}) collective-permute-start(f32[301,128]{1,0:T(8,128)S(1)} %add.14), channel_id=1, source_target_pairs={{0,4},{1,5},{2,6},{3,7},{4,0},{5,1},{6,2},{7,3},{8,12},{9,13},{10,... | collective-permute-start | bytes 462344 | tf_op jit(solution)/shard_map/ppermute | solution.py:16
  31.5 6.1 %shard_map.83 = (bf16[1024,1024]{1,0:T(8,128)(2,1)S(1)}, f32[1,1024]{1,0:T(1,128)S(1)}, bf16[256,1024]{1,0:T(8,128)(2,1)S(1)}) custom-call(s32[1,2048]{1,0:T(1,128)S(1)} %bitcast.10, bf16[2305,1024]{1,0:T(8,128)(2,1)S(1)} %get-tuple-element.55.pool_ref, bf16[128,1024]{1,0:T(8,128)(2,1)S(1)} %get-tuple-element.53.side_ref, ...), custom_call_target="tpu_custom_call" | custom-call | flops 1024 | bytes 1024 | tf_op jit(solution)/shard_map/pallas_call | solution.py:45
  37.7 1.2 %collective-permute-done.6 = f32[301,128]{1,0:T(8,128)S(1)} collective-permute-done((f32[301,128]{1,0:T(8,128)S(1)}, f32[301,128]{1,0:T(8,128)S(1)}, u32[]{:S(2)}, u32[]{:S(2)}) %collective-permute-start.6) | collective-permute-done | bytes 154144 | tf_op jit(solution)/shard_map/ppermute | solution.py:16
  38.9 0.0 collective-permute-done.7
  38.9 0.0 collective-permute-done.8
  39.0 0.0 collective-permute-done.9
  39.0 0.8 %collective-permute-start.10 = (bf16[384,1024]{1,0:T(8,128)(2,1)S(1)}, bf16[384,1024]{1,0:T(8,128)(2,1)S(1)}, u32[]{:S(2)}, u32[]{:S(2)}) collective-permute-start(bf16[384,1024]{1,0:T(8,128)(2,1)S(1)} %constant_dynamic-update-slice_fusion.refs_0_), channel_id=1, source_target_pairs={{0,1},{1,0},{2,3},{3,2},{4,5},{5,4},{6,7},{7,6},{8,9},{9,8},{10,11... | collective-permute-start | bytes 2359304 | tf_op jit(solution)/shard_map/ppermute | solution.py:16
  39.9 1.4 %collective-permute-start.11 = (bf16[301,128]{1,0:T(8,128)(2,1)S(1)}, bf16[301,128]{1,0:T(8,128)(2,1)S(1)}, u32[]{:S(2)}, u32[]{:S(2)}) collective-permute-start(bf16[301,128]{1,0:T(8,128)(2,1)S(1)} %convert_element_type.8), channel_id=1, source_target_pairs={{0,8},{8,0},{16,24},{24,16},{1,9},{9,1},{17,25},{25,17},{2,10},{10... | collective-permute-start | bytes 231176 | tf_op jit(solution)/shard_map/ppermute | solution.py:16
  41.3 1.2 %collective-permute-start.12 = (bf16[301,128]{1,0:T(8,128)(2,1)S(1)}, bf16[301,128]{1,0:T(8,128)(2,1)S(1)}, u32[]{:S(2)}, u32[]{:S(2)}) collective-permute-start(bf16[301,128]{1,0:T(8,128)(2,1)S(1)} %convert_element_type.8), channel_id=1, source_target_pairs={{0,16},{8,24},{16,0},{24,8},{1,17},{9,25},{17,1},{25,9},{2,18},{10... | collective-permute-start | bytes 231176 | tf_op jit(solution)/shard_map/ppermute | solution.py:16
  42.5 0.0 collective-permute-start.13
  42.6 2.3 %shard_map.84.refs_2_ = bf16[384,2048]{1,0:T(8,128)(2,1)S(1)} custom-call(bf16[384,1024]{1,0:T(8,128)(2,1)S(1)} %constant_dynamic-update-slice_fusion.refs_0_, bf16[256,1024]{1,0:T(8,128)(2,1)S(1)} %get-tuple-element.56.refs_0_.refs_1_, f32[1,256]{1,0:T(1,128)S(1)} %get-tuple-element.57.refs_1_.refs_2_, ...), custom_call_target="tpu_custom_call" | custom-call | flops 1024 | bytes 1024 | tf_op jit(solution)/shard_map/pallas_call | solution.py:45
  44.8 0.0 collective-permute-done.10.refs_0_
  44.9 2.3 %shard_map.85.refs_2_ = bf16[384,2048]{1,0:T(8,128)(2,1)S(1)} custom-call(bf16[384,1024]{1,0:T(8,128)(2,1)S(1)} %collective-permute-done.10.refs_0_, bf16[256,1024]{1,0:T(8,128)(2,1)S(1)} %get-tuple-element.56.refs_0_.refs_1_, f32[1,256]{1,0:T(1,128)S(1)} %get-tuple-element.57.refs_1_.refs_2_, bf16[256,1024]{1,0:T(8,128)(2,1)S(1)} %get-tuple-element.65.refs_2_.refs_3_, ...), custom_call_target="tpu_custom_call" | custom-call | flops 1024 | bytes 1024 | tf_op jit(solution)/shard_map/pallas_call | solution.py:45
  47.2 0.0 collective-permute-done.11
  47.2 0.0 collective-permute-done.12
  47.2 0.0 collective-permute-done.13
  47.3 1.3 %collective-permute-start.14 = (bf16[301,512]{1,0:T(8,128)(2,1)S(1)}, bf16[301,512]{1,0:T(8,128)(2,1)S(1)}, u32[]{:S(2)}, u32[]{:S(2)}) collective-permute-start(bf16[301,512]{1,0:T(8,128)(2,1)S(1)} %constant_dynamic-update-slice_fusion.3.residual_ref), channel_id=1, source_target_pairs={{0,1},{1,0},{2,3},{3,2},{4,5},{5,4},{6,7},{7,6},{8,9},{9,8},{10,11... | collective-permute-start | bytes 924680 | tf_op jit(solution)/shard_map/ppermute | solution.py:16
  48.6 1.6 %shard_map.86 = (f32[301,2048]{1,0:T(8,128)S(1)}, f32[32,301]{1,0:T(8,128)}) custom-call(s32[1]{0:T(128)} %bitcast.1.place_ref, f32[301,128]{1,0:T(8,128)S(1)} %add.15.total_ref, bf16[301,512]{1,0:T(8,128)(2,1)S(1)} %constant_dynamic-update-slice_fusion.3.residual_ref, f32[301,2048]{1,0:T(8,128)S(1)} %get-tuple-element.83.base_ref, ...), custom_call_target="tpu_custom_call" | custom-call | flops 1024 | bytes 1024 | tf_op jit(solution)/shard_map/pallas_call | solution.py:45
  50.2 0.0 collective-permute-done.14.residual_ref
  50.2 2.0 %shard_map.87 = f32[301,2048]{1,0:T(8,128)} custom-call(bf16[301,512]{1,0:T(8,128)(2,1)S(1)} %collective-permute-done.14.residual_ref, f32[301,2048]{1,0:T(8,128)S(1)} %get-tuple-element.87.base_ref, bf16[256,1024]{1,0:T(8,128)(2,1)S(1)} %get-tuple-element.84.refs_0_, bf16[256,1024]{1,0:T(8,128)(2,1)S(1)} %get-tuple-element.85.refs_1_, ...), custom_call_target="tpu_custom_call" | custom-call | flops 1024 | bytes 1024 | tf_op jit(solution)/shard_map/pallas_call | solution.py:45
  (16 shorter events, 0.2 us)
Async XLA Ops:
  0.6 1.4 %copy-start = (bf16[41,1024]{1,0:T(8,128)(2,1)S(1)}, bf16[41,1024]{1,0:T(8,128)(2,1)}, u32[]{:S(2)}) copy-start(bf16[41,1024]{1,0:T(8,128)(2,1)} %param.6) | copy-start | bytes 251908
  2.3 11.3 %collective-permute-start = (bf16[32,1024]{1,0:T(8,128)(2,1)S(1)}, bf16[32,1024]{1,0:T(8,128)(2,1)S(1)}, u32[]{:S(2)}, u32[]{:S(2)}) collective-permute-start(bf16[32,1024]{1,0:T(8,128)(2,1)S(1)} %convolution_convert_fusion.refs_0_), channel_id=1, source_target_pairs={{0,2},{1,3},{2,0},{3,1},{4,6},{5,7},{6,4},{7,5},{8,10},{9,11},{10,... | collective-permute-start | bytes 196616 | tf_op jit(solution)/shard_map/ppermute | solution.py:16
  4.5 9.1 %collective-permute-start.1 = (bf16[32,1024]{1,0:T(8,128)(2,1)S(1)}, bf16[32,1024]{1,0:T(8,128)(2,1)S(1)}, u32[]{:S(2)}, u32[]{:S(2)}) collective-permute-start(bf16[32,1024]{1,0:T(8,128)(2,1)S(1)} %convolution_convert_fusion.refs_0_), channel_id=1, source_target_pairs={{0,4},{1,5},{2,6},{3,7},{4,0},{5,1},{6,2},{7,3},{8,12},{9,13},{10,... | collective-permute-start | bytes 196616 | tf_op jit(solution)/shard_map/ppermute | solution.py:16
  6.8 6.8 %collective-permute-start.2 = (bf16[32,1024]{1,0:T(8,128)(2,1)S(1)}, bf16[32,1024]{1,0:T(8,128)(2,1)S(1)}, u32[]{:S(2)}, u32[]{:S(2)}) collective-permute-start(bf16[32,1024]{1,0:T(8,128)(2,1)S(1)} %convolution_convert_fusion.refs_0_), channel_id=1, source_target_pairs={{0,6},{1,7},{2,4},{3,5},{4,2},{5,3},{6,0},{7,1},{8,14},{9,15},{10,... | collective-permute-start | bytes 196616 | tf_op jit(solution)/shard_map/ppermute | solution.py:16
  6.8 1.7 %copy-start.1 = (f32[2048,301]{0,1:T(8,128)S(1)}, f32[2048,301]{0,1:T(8,128)}, u32[]{:S(2)}) copy-start(f32[2048,301]{0,1:T(8,128)} %param.11) | copy-start | bytes 7397380
  8.5 5.1 %copy-start.2 = (f32[32,301]{1,0:T(8,128)S(1)}, f32[32,301]{1,0:T(8,128)}, u32[]{:S(2)}) copy-start(f32[32,301]{1,0:T(8,128)} %targets_ref.1) | copy-start | bytes 115588
  13.8 2.9 %collective-permute-start.3 = (bf16[128,1024]{1,0:T(8,128)(2,1)S(1)}, bf16[128,1024]{1,0:T(8,128)(2,1)S(1)}, u32[]{:S(2)}, u32[]{:S(2)}) collective-permute-start(bf16[128,1024]{1,0:T(8,128)(2,1)S(1)} %get-tuple-element.53.side_ref), channel_id=1, source_target_pairs={{0,1},{1,0},{2,3},{3,2},{4,5},{5,4},{6,7},{7,6},{8,9},{9,8},{10,11... | collective-permute-start | bytes 786440 | tf_op jit(solution)/shard_map/ppermute | solution.py:16
  19.6 1.7 %collective-permute-start.4 = (f32[301,128]{1,0:T(8,128)S(1)}, f32[301,128]{1,0:T(8,128)S(1)}, u32[]{:S(2)}, u32[]{:S(2)}) collective-permute-start(f32[301,128]{1,0:T(8,128)S(1)} %get-tuple-element.63), channel_id=1, source_target_pairs={{0,1},{1,0},{2,3},{3,2},{4,5},{5,4},{6,7},{7,6},{8,9},{9,8},{10,11... | collective-permute-start | bytes 462344 | tf_op jit(solution)/shard_map/ppermute | solution.py:16
  21.3 6.8 %collective-permute-start.5 = (f32[301,128]{1,0:T(8,128)S(1)}, f32[301,128]{1,0:T(8,128)S(1)}, u32[]{:S(2)}, u32[]{:S(2)}) collective-permute-start(f32[301,128]{1,0:T(8,128)S(1)} %subtract_add_fusion), channel_id=1, source_target_pairs={{0,2},{1,3},{2,0},{3,1},{4,6},{5,7},{6,4},{7,5},{8,10},{9,11},{10,... | collective-permute-start | bytes 462344 | tf_op jit(solution)/shard_map/ppermute | solution.py:16
  21.9 17.0 %collective-permute-start.7 = (bf16[128,1024]{1,0:T(8,128)(2,1)S(1)}, bf16[128,1024]{1,0:T(8,128)(2,1)S(1)}, u32[]{:S(2)}, u32[]{:S(2)}) collective-permute-start(bf16[128,1024]{1,0:T(8,128)(2,1)S(1)} %get-tuple-element.53.side_ref), channel_id=1, source_target_pairs={{0,8},{8,0},{16,24},{24,16},{1,9},{9,1},{17,25},{25,17},{2,10},{10... | collective-permute-start | bytes 786440 | tf_op jit(solution)/shard_map/ppermute | solution.py:16
  23.2 15.8 %collective-permute-start.8 = (bf16[128,1024]{1,0:T(8,128)(2,1)S(1)}, bf16[128,1024]{1,0:T(8,128)(2,1)S(1)}, u32[]{:S(2)}, u32[]{:S(2)}) collective-permute-start(bf16[128,1024]{1,0:T(8,128)(2,1)S(1)} %get-tuple-element.53.side_ref), channel_id=1, source_target_pairs={{0,16},{8,24},{16,0},{24,8},{1,17},{9,25},{17,1},{25,9},{2,18},{10... | collective-permute-start | bytes 786440 | tf_op jit(solution)/shard_map/ppermute | solution.py:16
  24.4 14.6 %collective-permute-start.9 = (bf16[128,1024]{1,0:T(8,128)(2,1)S(1)}, bf16[128,1024]{1,0:T(8,128)(2,1)S(1)}, u32[]{:S(2)}, u32[]{:S(2)}) collective-permute-start(bf16[128,1024]{1,0:T(8,128)(2,1)S(1)} %get-tuple-element.53.side_ref), channel_id=1, source_target_pairs={{0,24},{8,16},{16,8},{24,0},{1,25},{9,17},{17,9},{25,1},{2,26},{10... | collective-permute-start | bytes 786440 | tf_op jit(solution)/shard_map/ppermute | solution.py:16
  28.1 10.8 %collective-permute-start.6 = (f32[301,128]{1,0:T(8,128)S(1)}, f32[301,128]{1,0:T(8,128)S(1)}, u32[]{:S(2)}, u32[]{:S(2)}) collective-permute-start(f32[301,128]{1,0:T(8,128)S(1)} %add.14), channel_id=1, source_target_pairs={{0,4},{1,5},{2,6},{3,7},{4,0},{5,1},{6,2},{7,3},{8,12},{9,13},{10,... | collective-permute-start | bytes 462344 | tf_op jit(solution)/shard_map/ppermute | solution.py:16
  39.0 5.8 %collective-permute-start.10 = (bf16[384,1024]{1,0:T(8,128)(2,1)S(1)}, bf16[384,1024]{1,0:T(8,128)(2,1)S(1)}, u32[]{:S(2)}, u32[]{:S(2)}) collective-permute-start(bf16[384,1024]{1,0:T(8,128)(2,1)S(1)} %constant_dynamic-update-slice_fusion.refs_0_), channel_id=1, source_target_pairs={{0,1},{1,0},{2,3},{3,2},{4,5},{5,4},{6,7},{7,6},{8,9},{9,8},{10,11... | collective-permute-start | bytes 2359304 | tf_op jit(solution)/shard_map/ppermute | solution.py:16
  39.9 7.3 %collective-permute-start.11 = (bf16[301,128]{1,0:T(8,128)(2,1)S(1)}, bf16[301,128]{1,0:T(8,128)(2,1)S(1)}, u32[]{:S(2)}, u32[]{:S(2)}) collective-permute-start(bf16[301,128]{1,0:T(8,128)(2,1)S(1)} %convert_element_type.8), channel_id=1, source_target_pairs={{0,8},{8,0},{16,24},{24,16},{1,9},{9,1},{17,25},{25,17},{2,10},{10... | collective-permute-start | bytes 231176 | tf_op jit(solution)/shard_map/ppermute | solution.py:16
  41.3 5.9 %collective-permute-start.12 = (bf16[301,128]{1,0:T(8,128)(2,1)S(1)}, bf16[301,128]{1,0:T(8,128)(2,1)S(1)}, u32[]{:S(2)}, u32[]{:S(2)}) collective-permute-start(bf16[301,128]{1,0:T(8,128)(2,1)S(1)} %convert_element_type.8), channel_id=1, source_target_pairs={{0,16},{8,24},{16,0},{24,8},{1,17},{9,25},{17,1},{25,9},{2,18},{10... | collective-permute-start | bytes 231176 | tf_op jit(solution)/shard_map/ppermute | solution.py:16
  42.5 4.7 %collective-permute-start.13 = (bf16[301,128]{1,0:T(8,128)(2,1)S(1)}, bf16[301,128]{1,0:T(8,128)(2,1)S(1)}, u32[]{:S(2)}, u32[]{:S(2)}) collective-permute-start(bf16[301,128]{1,0:T(8,128)(2,1)S(1)} %convert_element_type.8), channel_id=1, source_target_pairs={{0,24},{8,16},{16,8},{24,0},{1,25},{9,17},{17,9},{25,1},{2,26},{10... | collective-permute-start | bytes 231176 | tf_op jit(solution)/shard_map/ppermute | solution.py:16
  47.3 2.9 %collective-permute-start.14 = (bf16[301,512]{1,0:T(8,128)(2,1)S(1)}, bf16[301,512]{1,0:T(8,128)(2,1)S(1)}, u32[]{:S(2)}, u32[]{:S(2)}) collective-permute-start(bf16[301,512]{1,0:T(8,128)(2,1)S(1)} %constant_dynamic-update-slice_fusion.3.residual_ref), channel_id=1, source_target_pairs={{0,1},{1,0},{2,3},{3,2},{4,5},{5,4},{6,7},{7,6},{8,9},{9,8},{10,11... | collective-permute-start | bytes 924680 | tf_op jit(solution)/shard_map/ppermute | solution.py:16

commit v3 on v2

--- a/solution.py
+++ b/solution.py
@@ -74,11 +74,16 @@
 def pool_rows(pool_ref, at, size):
     if at + size <= pool_ref.shape[0]:
         return pool_ref[at : at + size, :]
-    place = lax.broadcasted_iota(jnp.int32, (size, pool_ref.shape[1]), 0)
+    whole = (pool_ref.shape[0] - at) // LANES * LANES
+    place = lax.broadcasted_iota(jnp.int32, (size - whole, pool_ref.shape[1]), 0)
     rows = jnp.zeros(place.shape, jnp.float32)
-    for row in range(at, pool_ref.shape[0]):
-        rows = jnp.where(place == row - at, pool_ref[row : row + 1, :].astype(jnp.float32), rows)
-    return rows.astype(jnp.bfloat16)
+    for row in range(at + whole, pool_ref.shape[0]):
+        wide = pool_ref[row : row + 1, :].astype(jnp.float32)
+        rows = jnp.where(place == row - at - whole, wide, rows)
+    rows = rows.astype(jnp.bfloat16)
+    if whole == 0:
+        return rows
+    return jnp.concatenate([pool_ref[at : at + whole, :], rows], axis=0)
 
 
 def place_body(index_ref, base_ref, pool_far, placed_ref, square_ref, kept_ref, pool_ref, done_ref):
@@ -182,7 +187,7 @@
     samples = jnp.concatenate([side_ref[...], other_ref[...]], axis=0)
     samples, own_square = halves_and_squares(samples)
     own_square = turned(own_square)
-    for at, size in spans(placed_ref.shape[1], 4 * LANES):
+    for at, size in spans(placed_ref.shape[1], 8 * LANES):
         cross = contract_last(pool_rows(pool_ref, at, size), samples)
         for lane in range(0, samples.shape[0], LANES):
             lanes = slice(lane, lane + LANES)

time: 52.6 us -> 52 us (0.989)
  transfers between devices with their start and end apart: 15 -> 15, of which waited for: 1 -> 1; matrix products, arithmetic and copies ran while one was open for 0% -> 0% of each run, Pallas kernels for 46% -> 47%
where the time goes in v3:
time: 52 us; the launch traced here: 51.8 us
  Pallas kernels  28.9 us (56%)
  starting transfers between devices  17.2 us (33%)
  local copies, waits for them, and re-layouts  1.86 us (4%)
  other arithmetic  1.49 us (3%)
  waiting for transfers between devices  1.08 us (2%)
  between operations  1.06 us (2%)
    pallas_call x11, Pallas kernels, call(): pl.pallas_call(body, in_specs=[place for _, place in operands], out_specs...  28.9 us
    ppermute x15, starting transfers between devices, flip(): return lax.ppermute(value, axis, [(i, i ^ distance) for i in range(count)])  17.2 us
    unnamed x11, local copies, waits for them, and re-layouts  1.81 us
    ppermute x15, waiting for transfers between devices, flip(): return lax.ppermute(value, axis, [(i, i ^ distance) for i in range(count)])  1.08 us
  transfers between devices with their start and end apart: 15, of which 1 were waited for; matrix products, arithmetic and copies ran while one was open for 0% of the time, Pallas kernels for 47%

profile of v3, /device:TPU:1, one launch (start us, length us, event | category | flops | bytes accessed | tf_op | source)
XLA Modules:
  0.0 51.8 jit_solution(15977271815421975471)
XLA Ops:
  0.6 0.0 copy-start
  0.7 0.7 %broadcast_subtract_fusion.1 = s32[32]{0:T(128)S(1)} fusion(s32[32]{0:T(128)} %param.7, s32[]{:T(128)S(6)} %mul.11), kind=kLoop, calls=%fused_computation.13 | loop fusion | flops 32 | bytes 260 | tf_op jit(solution)/shard_map/sub | solution.py:398
  1.3 0.7 %broadcast_subtract_fusion = s32[2048]{0:T(1024)S(1)} fusion(s32[2048]{0:T(1024)} %param.9, s32[]{:T(128)S(6)} %mul.9), kind=kLoop, calls=%fused_computation.12 | loop fusion | flops 2048 | bytes 16388 | tf_op jit(solution)/shard_map/sub | solution.py:397
  2.1 0.0 copy-done
  2.1 0.2 convolution_convert_fusion.refs_0_
  2.3 2.2 %collective-permute-start = (bf16[32,1024]{1,0:T(8,128)(2,1)S(1)}, bf16[32,1024]{1,0:T(8,128)(2,1)S(1)}, u32[]{:S(2)}, u32[]{:S(2)}) collective-permute-start(bf16[32,1024]{1,0:T(8,128)(2,1)S(1)} %convolution_convert_fusion.refs_0_), channel_id=1, source_target_pairs={{0,2},{1,3},{2,0},{3,1},{4,6},{5,7},{6,4},{7,5},{8,10},{9,11},{10,... | collective-permute-start | bytes 196616 | tf_op jit(solution)/shard_map/ppermute | solution.py:16
  4.5 2.3 %collective-permute-start.1 = (bf16[32,1024]{1,0:T(8,128)(2,1)S(1)}, bf16[32,1024]{1,0:T(8,128)(2,1)S(1)}, u32[]{:S(2)}, u32[]{:S(2)}) collective-permute-start(bf16[32,1024]{1,0:T(8,128)(2,1)S(1)} %convolution_convert_fusion.refs_0_), channel_id=1, source_target_pairs={{0,4},{1,5},{2,6},{3,7},{4,0},{5,1},{6,2},{7,3},{8,12},{9,13},{10,... | collective-permute-start | bytes 196616 | tf_op jit(solution)/shard_map/ppermute | solution.py:16
  6.8 0.0 collective-permute-start.2
  6.8 1.7 %copy-done.1 = f32[2048,301]{0,1:T(8,128)S(1)} copy-done((f32[2048,301]{0,1:T(8,128)S(1)}, f32[2048,301]{0,1:T(8,128)}, u32[]{:S(2)}) %copy-start.1) | copy-done | bytes 2465816
  8.5 5.1 %shard_map.77 = (bf16[301,2432]{1,0:T(8,128)(2,1)S(1)}, f32[2432,128]{1,0:T(8,128)S(1)}, f32[301,2048]{1,0:T(8,128)S(1)}, bf16[2305,1024]{1,0:T(8,128)(2,1)S(1)}) custom-call(s32[1,2048]{1,0:T(1,128)S(1)} %bitcast.6, f32[301,2048]{1,0:T(8,128)S(1)} %bitcast.5, bf16[2305,1024]{1,0:T(8,128)(2,1)} %pool_far.1), custom_call_target="tpu_custom_call" | custom-call | flops 1024 | bytes 1024 | tf_op jit(solution)/shard_map/pallas_call | solution.py:45
  13.6 0.0 collective-permute-done.refs_1_
  13.6 0.0 collective-permute-done.1.refs_2_
  13.6 0.0 collective-permute-done.2.refs_3_
  13.6 0.0 copy-done.2
  13.6 0.2 shard_map.78
  13.8 1.3 %collective-permute-start.3 = (bf16[128,1024]{1,0:T(8,128)(2,1)S(1)}, bf16[128,1024]{1,0:T(8,128)(2,1)S(1)}, u32[]{:S(2)}, u32[]{:S(2)}) collective-permute-start(bf16[128,1024]{1,0:T(8,128)(2,1)S(1)} %get-tuple-element.53.side_ref), channel_id=1, source_target_pairs={{0,1},{1,0},{2,3},{3,2},{4,5},{5,4},{6,7},{7,6},{8,9},{9,8},{10,11... | collective-permute-start | bytes 786440 | tf_op jit(solution)/shard_map/ppermute | solution.py:16
  15.1 1.6 %shard_map.79 = (bf16[256,1024]{1,0:T(8,128)(2,1)S(1)}, f32[1,256]{1,0:T(1,128)S(1)}) custom-call(s32[1,2048]{1,0:T(1,128)S(1)} %bitcast.7, bf16[2305,1024]{1,0:T(8,128)(2,1)S(1)} %get-tuple-element.55.pool_ref), custom_call_target="tpu_custom_call" | custom-call | flops 1024 | bytes 1024 | tf_op jit(solution)/shard_map/pallas_call | solution.py:45
  16.6 0.0 collective-permute-done.3.other_ref
  16.6 2.5 %shard_map.80 = (f32[301,128]{1,0:T(8,128)S(1)}, f32[301,128]{1,0:T(8,128)S(1)}) custom-call(bf16[128,1024]{1,0:T(8,128)(2,1)S(1)} %get-tuple-element.53.side_ref, bf16[128,1024]{1,0:T(8,128)(2,1)S(1)} %collective-permute-done.3.other_ref, bf16[2305,1024]{1,0:T(8,128)(2,1)S(1)} %get-tuple-element.55.pool_ref, f32[2432,128]{1,0:T(8,128)S(1)} %get-tuple-element.59.square_ref, ...), custom_call_target="tpu_custom_call" | custom-call | flops 1024 | bytes 1024 | tf_op jit(solution)/shard_map/pallas_call | solution.py:45
  19.1 0.1 collective-permute-start.4
  19.2 1.6 %shard_map.81 = (bf16[256,1024]{1,0:T(8,128)(2,1)S(1)}, f32[1,256]{1,0:T(1,128)S(1)}) custom-call(s32[1,2048]{1,0:T(1,128)S(1)} %bitcast.8, bf16[2305,1024]{1,0:T(8,128)(2,1)S(1)} %get-tuple-element.55.pool_ref), custom_call_target="tpu_custom_call" | custom-call | flops 1024 | bytes 1024 | tf_op jit(solution)/shard_map/pallas_call | solution.py:45
  20.8 0.0 collective-permute-done.4
  20.8 0.7 %collective-permute-start.5 = (f32[301,128]{1,0:T(8,128)S(1)}, f32[301,128]{1,0:T(8,128)S(1)}, u32[]{:S(2)}, u32[]{:S(2)}) collective-permute-start(f32[301,128]{1,0:T(8,128)S(1)} %subtract_add_fusion), channel_id=1, source_target_pairs={{0,2},{1,3},{2,0},{3,1},{4,6},{5,7},{6,4},{7,5},{8,10},{9,11},{10,... | collective-permute-start | bytes 462344 | tf_op jit(solution)/shard_map/ppermute | solution.py:16
  21.5 1.2 %collective-permute-start.7 = (bf16[128,1024]{1,0:T(8,128)(2,1)S(1)}, bf16[128,1024]{1,0:T(8,128)(2,1)S(1)}, u32[]{:S(2)}, u32[]{:S(2)}) collective-permute-start(bf16[128,1024]{1,0:T(8,128)(2,1)S(1)} %get-tuple-element.53.side_ref), channel_id=1, source_target_pairs={{0,8},{8,0},{16,24},{24,16},{1,9},{9,1},{17,25},{25,17},{2,10},{10... | collective-permute-start | bytes 786440 | tf_op jit(solution)/shard_map/ppermute | solution.py:16
  22.7 1.2 %collective-permute-start.8 = (bf16[128,1024]{1,0:T(8,128)(2,1)S(1)}, bf16[128,1024]{1,0:T(8,128)(2,1)S(1)}, u32[]{:S(2)}, u32[]{:S(2)}) collective-permute-start(bf16[128,1024]{1,0:T(8,128)(2,1)S(1)} %get-tuple-element.53.side_ref), channel_id=1, source_target_pairs={{0,16},{8,24},{16,0},{24,8},{1,17},{9,25},{17,1},{25,9},{2,18},{10... | collective-permute-start | bytes 786440 | tf_op jit(solution)/shard_map/ppermute | solution.py:16
  24.0 0.2 collective-permute-start.9
  24.2 3.5 %shard_map.82 = (bf16[512,1024]{1,0:T(8,128)(2,1)S(1)}, f32[1,512]{1,0:T(1,128)S(1)}, bf16[256,1024]{1,0:T(8,128)(2,1)S(1)}) custom-call(s32[1,2048]{1,0:T(1,128)S(1)} %bitcast.9, bf16[2305,1024]{1,0:T(8,128)(2,1)S(1)} %get-tuple-element.55.pool_ref, bf16[128,1024]{1,0:T(8,128)(2,1)S(1)} %get-tuple-element.53.side_ref, ...), custom_call_target="tpu_custom_call" | custom-call | flops 1024 | bytes 1024 | tf_op jit(solution)/shard_map/pallas_call | solution.py:45
  27.6 0.0 collective-permute-done.5
  27.7 3.3 %collective-permute-start.6 = (f32[301,128]{1,0:T(8,128)S(1)}, f32[301,128]{1,0:T(8,128)S(1)}, u32[]{:S(2)}, u32[]{:S(2)}) collective-permute-start(f32[301,128]{1,0:T(8,128)S(1)} %add.14), channel_id=1, source_target_pairs={{0,4},{1,5},{2,6},{3,7},{4,0},{5,1},{6,2},{7,3},{8,12},{9,13},{10,... | collective-permute-start | bytes 462344 | tf_op jit(solution)/shard_map/ppermute | solution.py:16
  30.9 6.3 %shard_map.83 = (bf16[1024,1024]{1,0:T(8,128)(2,1)S(1)}, f32[1,1024]{1,0:T(1,128)S(1)}, bf16[256,1024]{1,0:T(8,128)(2,1)S(1)}) custom-call(s32[1,2048]{1,0:T(1,128)S(1)} %bitcast.10, bf16[2305,1024]{1,0:T(8,128)(2,1)S(1)} %get-tuple-element.55.pool_ref, bf16[128,1024]{1,0:T(8,128)(2,1)S(1)} %get-tuple-element.53.side_ref, ...), custom_call_target="tpu_custom_call" | custom-call | flops 1024 | bytes 1024 | tf_op jit(solution)/shard_map/pallas_call | solution.py:45
  37.3 1.0 %collective-permute-done.6 = f32[301,128]{1,0:T(8,128)S(1)} collective-permute-done((f32[301,128]{1,0:T(8,128)S(1)}, f32[301,128]{1,0:T(8,128)S(1)}, u32[]{:S(2)}, u32[]{:S(2)}) %collective-permute-start.6) | collective-permute-done | bytes 154144 | tf_op jit(solution)/shard_map/ppermute | solution.py:16
  38.3 0.0 collective-permute-done.7
  38.3 0.0 collective-permute-done.8
  38.3 0.0 collective-permute-done.9
  38.4 0.9 %collective-permute-start.10 = (bf16[384,1024]{1,0:T(8,128)(2,1)S(1)}, bf16[384,1024]{1,0:T(8,128)(2,1)S(1)}, u32[]{:S(2)}, u32[]{:S(2)}) collective-permute-start(bf16[384,1024]{1,0:T(8,128)(2,1)S(1)} %constant_dynamic-update-slice_fusion.refs_0_), channel_id=1, source_target_pairs={{0,1},{1,0},{2,3},{3,2},{4,5},{5,4},{6,7},{7,6},{8,9},{9,8},{10,11... | collective-permute-start | bytes 2359304 | tf_op jit(solution)/shard_map/ppermute | solution.py:16
  39.4 1.3 %collective-permute-start.11 = (bf16[301,128]{1,0:T(8,128)(2,1)S(1)}, bf16[301,128]{1,0:T(8,128)(2,1)S(1)}, u32[]{:S(2)}, u32[]{:S(2)}) collective-permute-start(bf16[301,128]{1,0:T(8,128)(2,1)S(1)} %convert_element_type.8), channel_id=1, source_target_pairs={{0,8},{8,0},{16,24},{24,16},{1,9},{9,1},{17,25},{25,17},{2,10},{10... | collective-permute-start | bytes 231176 | tf_op jit(solution)/shard_map/ppermute | solution.py:16
  40.7 1.2 %collective-permute-start.12 = (bf16[301,128]{1,0:T(8,128)(2,1)S(1)}, bf16[301,128]{1,0:T(8,128)(2,1)S(1)}, u32[]{:S(2)}, u32[]{:S(2)}) collective-permute-start(bf16[301,128]{1,0:T(8,128)(2,1)S(1)} %convert_element_type.8), channel_id=1, source_target_pairs={{0,16},{8,24},{16,0},{24,8},{1,17},{9,25},{17,1},{25,9},{2,18},{10... | collective-permute-start | bytes 231176 | tf_op jit(solution)/shard_map/ppermute | solution.py:16
  41.9 0.2 collective-permute-start.13
  42.1 2.3 %shard_map.84.refs_2_ = bf16[384,2048]{1,0:T(8,128)(2,1)S(1)} custom-call(bf16[384,1024]{1,0:T(8,128)(2,1)S(1)} %constant_dynamic-update-slice_fusion.refs_0_, bf16[256,1024]{1,0:T(8,128)(2,1)S(1)} %get-tuple-element.56.refs_0_.refs_1_, f32[1,256]{1,0:T(1,128)S(1)} %get-tuple-element.57.refs_1_.refs_2_, ...), custom_call_target="tpu_custom_call" | custom-call | flops 1024 | bytes 1024 | tf_op jit(solution)/shard_map/pallas_call | solution.py:45
  44.4 0.0 collective-permute-done.10.refs_0_
  44.4 2.3 %shard_map.85.refs_2_ = bf16[384,2048]{1,0:T(8,128)(2,1)S(1)} custom-call(bf16[384,1024]{1,0:T(8,128)(2,1)S(1)} %collective-permute-done.10.refs_0_, bf16[256,1024]{1,0:T(8,128)(2,1)S(1)} %get-tuple-element.56.refs_0_.refs_1_, f32[1,256]{1,0:T(1,128)S(1)} %get-tuple-element.57.refs_1_.refs_2_, bf16[256,1024]{1,0:T(8,128)(2,1)S(1)} %get-tuple-element.65.refs_2_.refs_3_, ...), custom_call_target="tpu_custom_call" | custom-call | flops 1024 | bytes 1024 | tf_op jit(solution)/shard_map/pallas_call | solution.py:45
  46.7 0.0 collective-permute-done.11
  46.7 0.0 collective-permute-done.12
  46.7 0.0 collective-permute-done.13
  46.8 1.1 %collective-permute-start.14 = (bf16[301,512]{1,0:T(8,128)(2,1)S(1)}, bf16[301,512]{1,0:T(8,128)(2,1)S(1)}, u32[]{:S(2)}, u32[]{:S(2)}) collective-permute-start(bf16[301,512]{1,0:T(8,128)(2,1)S(1)} %constant_dynamic-update-slice_fusion.3.residual_ref), channel_id=1, source_target_pairs={{0,1},{1,0},{2,3},{3,2},{4,5},{5,4},{6,7},{7,6},{8,9},{9,8},{10,11... | collective-permute-start | bytes 924680 | tf_op jit(solution)/shard_map/ppermute | solution.py:16
  48.0 1.6 %shard_map.86 = (f32[301,2048]{1,0:T(8,128)S(1)}, f32[32,301]{1,0:T(8,128)}) custom-call(s32[1]{0:T(128)} %bitcast.1.place_ref, f32[301,128]{1,0:T(8,128)S(1)} %add.15.total_ref, bf16[301,512]{1,0:T(8,128)(2,1)S(1)} %constant_dynamic-update-slice_fusion.3.residual_ref, f32[301,2048]{1,0:T(8,128)S(1)} %get-tuple-element.83.base_ref, ...), custom_call_target="tpu_custom_call" | custom-call | flops 1024 | bytes 1024 | tf_op jit(solution)/shard_map/pallas_call | solution.py:45
  49.6 0.0 collective-permute-done.14.residual_ref
  49.6 2.0 %shard_map.87 = f32[301,2048]{1,0:T(8,128)} custom-call(bf16[301,512]{1,0:T(8,128)(2,1)S(1)} %collective-permute-done.14.residual_ref, f32[301,2048]{1,0:T(8,128)S(1)} %get-tuple-element.87.base_ref, bf16[256,1024]{1,0:T(8,128)(2,1)S(1)} %get-tuple-element.84.refs_0_, bf16[256,1024]{1,0:T(8,128)(2,1)S(1)} %get-tuple-element.85.refs_1_, ...), custom_call_target="tpu_custom_call" | custom-call | flops 1024 | bytes 1024 | tf_op jit(solution)/shard_map/pallas_call | solution.py:45
  (16 shorter events, 0.2 us)
Async XLA Ops:
  0.6 1.4 %copy-start = (bf16[41,1024]{1,0:T(8,128)(2,1)S(1)}, bf16[41,1024]{1,0:T(8,128)(2,1)}, u32[]{:S(2)}) copy-start(bf16[41,1024]{1,0:T(8,128)(2,1)} %param.6) | copy-start | bytes 251908
  2.3 11.3 %collective-permute-start = (bf16[32,1024]{1,0:T(8,128)(2,1)S(1)}, bf16[32,1024]{1,0:T(8,128)(2,1)S(1)}, u32[]{:S(2)}, u32[]{:S(2)}) collective-permute-start(bf16[32,1024]{1,0:T(8,128)(2,1)S(1)} %convolution_convert_fusion.refs_0_), channel_id=1, source_target_pairs={{0,2},{1,3},{2,0},{3,1},{4,6},{5,7},{6,4},{7,5},{8,10},{9,11},{10,... | collective-permute-start | bytes 196616 | tf_op jit(solution)/shard_map/ppermute | solution.py:16
  4.5 9.1 %collective-permute-start.1 = (bf16[32,1024]{1,0:T(8,128)(2,1)S(1)}, bf16[32,1024]{1,0:T(8,128)(2,1)S(1)}, u32[]{:S(2)}, u32[]{:S(2)}) collective-permute-start(bf16[32,1024]{1,0:T(8,128)(2,1)S(1)} %convolution_convert_fusion.refs_0_), channel_id=1, source_target_pairs={{0,4},{1,5},{2,6},{3,7},{4,0},{5,1},{6,2},{7,3},{8,12},{9,13},{10,... | collective-permute-start | bytes 196616 | tf_op jit(solution)/shard_map/ppermute | solution.py:16
  6.8 6.8 %collective-permute-start.2 = (bf16[32,1024]{1,0:T(8,128)(2,1)S(1)}, bf16[32,1024]{1,0:T(8,128)(2,1)S(1)}, u32[]{:S(2)}, u32[]{:S(2)}) collective-permute-start(bf16[32,1024]{1,0:T(8,128)(2,1)S(1)} %convolution_convert_fusion.refs_0_), channel_id=1, source_target_pairs={{0,6},{1,7},{2,4},{3,5},{4,2},{5,3},{6,0},{7,1},{8,14},{9,15},{10,... | collective-permute-start | bytes 196616 | tf_op jit(solution)/shard_map/ppermute | solution.py:16
  6.8 1.7 %copy-start.1 = (f32[2048,301]{0,1:T(8,128)S(1)}, f32[2048,301]{0,1:T(8,128)}, u32[]{:S(2)}) copy-start(f32[2048,301]{0,1:T(8,128)} %param.11) | copy-start | bytes 7397380
  8.5 5.1 %copy-start.2 = (f32[32,301]{1,0:T(8,128)S(1)}, f32[32,301]{1,0:T(8,128)}, u32[]{:S(2)}) copy-start(f32[32,301]{1,0:T(8,128)} %targets_ref.1) | copy-start | bytes 115588
  13.8 2.9 %collective-permute-start.3 = (bf16[128,1024]{1,0:T(8,128)(2,1)S(1)}, bf16[128,1024]{1,0:T(8,128)(2,1)S(1)}, u32[]{:S(2)}, u32[]{:S(2)}) collective-permute-start(bf16[128,1024]{1,0:T(8,128)(2,1)S(1)} %get-tuple-element.53.side_ref), channel_id=1, source_target_pairs={{0,1},{1,0},{2,3},{3,2},{4,5},{5,4},{6,7},{7,6},{8,9},{9,8},{10,11... | collective-permute-start | bytes 786440 | tf_op jit(solution)/shard_map/ppermute | solution.py:16
  19.1 1.7 %collective-permute-start.4 = (f32[301,128]{1,0:T(8,128)S(1)}, f32[301,128]{1,0:T(8,128)S(1)}, u32[]{:S(2)}, u32[]{:S(2)}) collective-permute-start(f32[301,128]{1,0:T(8,128)S(1)} %get-tuple-element.63), channel_id=1, source_target_pairs={{0,1},{1,0},{2,3},{3,2},{4,5},{5,4},{6,7},{7,6},{8,9},{9,8},{10,11... | collective-permute-start | bytes 462344 | tf_op jit(solution)/shard_map/ppermute | solution.py:16
  20.8 6.8 %collective-permute-start.5 = (f32[301,128]{1,0:T(8,128)S(1)}, f32[301,128]{1,0:T(8,128)S(1)}, u32[]{:S(2)}, u32[]{:S(2)}) collective-permute-start(f32[301,128]{1,0:T(8,128)S(1)} %subtract_add_fusion), channel_id=1, source_target_pairs={{0,2},{1,3},{2,0},{3,1},{4,6},{5,7},{6,4},{7,5},{8,10},{9,11},{10,... | collective-permute-start | bytes 462344 | tf_op jit(solution)/shard_map/ppermute | solution.py:16
  21.5 16.8 %collective-permute-start.7 = (bf16[128,1024]{1,0:T(8,128)(2,1)S(1)}, bf16[128,1024]{1,0:T(8,128)(2,1)S(1)}, u32[]{:S(2)}, u32[]{:S(2)}) collective-permute-start(bf16[128,1024]{1,0:T(8,128)(2,1)S(1)} %get-tuple-element.53.side_ref), channel_id=1, source_target_pairs={{0,8},{8,0},{16,24},{24,16},{1,9},{9,1},{17,25},{25,17},{2,10},{10... | collective-permute-start | bytes 786440 | tf_op jit(solution)/shard_map/ppermute | solution.py:16
  22.7 15.6 %collective-permute-start.8 = (bf16[128,1024]{1,0:T(8,128)(2,1)S(1)}, bf16[128,1024]{1,0:T(8,128)(2,1)S(1)}, u32[]{:S(2)}, u32[]{:S(2)}) collective-permute-start(bf16[128,1024]{1,0:T(8,128)(2,1)S(1)} %get-tuple-element.53.side_ref), channel_id=1, source_target_pairs={{0,16},{8,24},{16,0},{24,8},{1,17},{9,25},{17,1},{25,9},{2,18},{10... | collective-permute-start | bytes 786440 | tf_op jit(solution)/shard_map/ppermute | solution.py:16
  24.0 14.4 %collective-permute-start.9 = (bf16[128,1024]{1,0:T(8,128)(2,1)S(1)}, bf16[128,1024]{1,0:T(8,128)(2,1)S(1)}, u32[]{:S(2)}, u32[]{:S(2)}) collective-permute-start(bf16[128,1024]{1,0:T(8,128)(2,1)S(1)} %get-tuple-element.53.side_ref), channel_id=1, source_target_pairs={{0,24},{8,16},{16,8},{24,0},{1,25},{9,17},{17,9},{25,1},{2,26},{10... | collective-permute-start | bytes 786440 | tf_op jit(solution)/shard_map/ppermute | solution.py:16
  27.7 10.6 %collective-permute-start.6 = (f32[301,128]{1,0:T(8,128)S(1)}, f32[301,128]{1,0:T(8,128)S(1)}, u32[]{:S(2)}, u32[]{:S(2)}) collective-permute-start(f32[301,128]{1,0:T(8,128)S(1)} %add.14), channel_id=1, source_target_pairs={{0,4},{1,5},{2,6},{3,7},{4,0},{5,1},{6,2},{7,3},{8,12},{9,13},{10,... | collective-permute-start | bytes 462344 | tf_op jit(solution)/shard_map/ppermute | solution.py:16
  38.4 5.9 %collective-permute-start.10 = (bf16[384,1024]{1,0:T(8,128)(2,1)S(1)}, bf16[384,1024]{1,0:T(8,128)(2,1)S(1)}, u32[]{:S(2)}, u32[]{:S(2)}) collective-permute-start(bf16[384,1024]{1,0:T(8,128)(2,1)S(1)} %constant_dynamic-update-slice_fusion.refs_0_), channel_id=1, source_target_pairs={{0,1},{1,0},{2,3},{3,2},{4,5},{5,4},{6,7},{7,6},{8,9},{9,8},{10,11... | collective-permute-start | bytes 2359304 | tf_op jit(solution)/shard_map/ppermute | solution.py:16
  39.4 7.3 %collective-permute-start.11 = (bf16[301,128]{1,0:T(8,128)(2,1)S(1)}, bf16[301,128]{1,0:T(8,128)(2,1)S(1)}, u32[]{:S(2)}, u32[]{:S(2)}) collective-permute-start(bf16[301,128]{1,0:T(8,128)(2,1)S(1)} %convert_element_type.8), channel_id=1, source_target_pairs={{0,8},{8,0},{16,24},{24,16},{1,9},{9,1},{17,25},{25,17},{2,10},{10... | collective-permute-start | bytes 231176 | tf_op jit(solution)/shard_map/ppermute | solution.py:16
  40.7 6.0 %collective-permute-start.12 = (bf16[301,128]{1,0:T(8,128)(2,1)S(1)}, bf16[301,128]{1,0:T(8,128)(2,1)S(1)}, u32[]{:S(2)}, u32[]{:S(2)}) collective-permute-start(bf16[301,128]{1,0:T(8,128)(2,1)S(1)} %convert_element_type.8), channel_id=1, source_target_pairs={{0,16},{8,24},{16,0},{24,8},{1,17},{9,25},{17,1},{25,9},{2,18},{10... | collective-permute-start | bytes 231176 | tf_op jit(solution)/shard_map/ppermute | solution.py:16
  41.9 4.8 %collective-permute-start.13 = (bf16[301,128]{1,0:T(8,128)(2,1)S(1)}, bf16[301,128]{1,0:T(8,128)(2,1)S(1)}, u32[]{:S(2)}, u32[]{:S(2)}) collective-permute-start(bf16[301,128]{1,0:T(8,128)(2,1)S(1)} %convert_element_type.8), channel_id=1, source_target_pairs={{0,24},{8,16},{16,8},{24,0},{1,25},{9,17},{17,9},{25,1},{2,26},{10... | collective-permute-start | bytes 231176 | tf_op jit(solution)/shard_map/ppermute | solution.py:16
  46.8 2.8 %collective-permute-start.14 = (bf16[301,512]{1,0:T(8,128)(2,1)S(1)}, bf16[301,512]{1,0:T(8,128)(2,1)S(1)}, u32[]{:S(2)}, u32[]{:S(2)}) collective-permute-start(bf16[301,512]{1,0:T(8,128)(2,1)S(1)} %constant_dynamic-update-slice_fusion.3.residual_ref), channel_id=1, source_target_pairs={{0,1},{1,0},{2,3},{3,2},{4,5},{5,4},{6,7},{7,6},{8,9},{9,8},{10,11... | collective-permute-start | bytes 924680 | tf_op jit(solution)/shard_map/ppermute | solution.py:16

commit v4 on v3

--- a/solution.py
+++ b/solution.py
@@ -51,6 +51,16 @@
         cost_estimate=pl.CostEstimate(flops=1024, bytes_accessed=1024, transcendentals=0),
         compiler_params=pltpu.CompilerParams(vmem_limit_bytes=limit << 20),
     )(*arrays)
+
+
+def staggered(steps):
+    held = None
+    for first, then in steps:
+        result = first()
+        if held is not None:
+            held()
+        held = functools.partial(then, result)
+    held()
 
 
 def narrow(index, pool_ref):
@@ -187,12 +197,20 @@
     samples = jnp.concatenate([side_ref[...], other_ref[...]], axis=0)
     samples, own_square = halves_and_squares(samples)
     own_square = turned(own_square)
-    for at, size in spans(placed_ref.shape[1], 8 * LANES):
-        cross = contract_last(pool_rows(pool_ref, at, size), samples)
+
+    def product(at, size):
+        return contract_last(pool_rows(pool_ref, at, size), samples)
+
+    def values(at, size, cross):
         for lane in range(0, samples.shape[0], LANES):
             lanes = slice(lane, lane + LANES)
             squared = square_ref[at : at + size, :] + own_square[:, lanes] + cross[:, lanes]
             kernel_ref[at : at + size, lanes] = kernel_of(squared)
+
+    staggered(
+        (functools.partial(product, at, size), functools.partial(values, at, size))
+        for at, size in spans(placed_ref.shape[1], 4 * LANES)
+    )
     terms = jnp.dot(placed_ref[...], kernel_ref[...], preferred_element_type=jnp.float32)
     rows = side_ref.shape[0]
     terms_ref[...] = terms[:, :rows]
@@ -209,30 +227,42 @@
     )
 
 
-def pick_span(index_ref, pool_ref, rows_ref, square_ref, first, at, size):
+def pick_steps(index_ref, pool_ref, rows_ref, square_ref, first, then=None):
     whole = pool_ref.shape[0] // LANES * LANES
-    wanted = column_of(index_ref[:, first + at : first + at + size])
-    place = narrow(wanted, pool_ref)
-    lane = lax.broadcasted_iota(place.dtype, (size, LANES), 1)
-    chosen = jnp.concatenate(
-        [
-            one_hot(place - jnp.asarray(part, place.dtype) == lane)
-            for part in range(0, whole, LANES)
-        ],
-        axis=1,
-    )
-    rows = jnp.dot(chosen, pool_ref[:whole, :], preferred_element_type=jnp.float32)
-    for row in range(whole, pool_ref.shape[0]):
-        rows = rows + jnp.where(
-            wanted[:, :1] == row, pool_ref[row : row + 1, :].astype(jnp.float32), 0.0
+
+    def product(at, size):
+        wanted = column_of(index_ref[:, first + at : first + at + size])
+        place = narrow(wanted, pool_ref)
+        lane = lax.broadcasted_iota(place.dtype, (size, LANES), 1)
+        chosen = jnp.concatenate(
+            [
+                one_hot(place - jnp.asarray(part, place.dtype) == lane)
+                for part in range(0, whole, LANES)
+            ],
+            axis=1,
         )
-    rows_ref[at : at + size, :] = rows.astype(jnp.bfloat16)
-    square_ref[:, at : at + size] = turned(jnp.sum(rows * rows, axis=1, keepdims=True))
+        rows = jnp.dot(chosen, pool_ref[:whole, :], preferred_element_type=jnp.float32)
+        return wanted, rows
+
+    def values(at, size, result):
+        wanted, rows = result
+        for row in range(whole, pool_ref.shape[0]):
+            rows = rows + jnp.where(
+                wanted[:, :1] == row, pool_ref[row : row + 1, :].astype(jnp.float32), 0.0
+            )
+        rows_ref[at : at + size, :] = rows.astype(jnp.bfloat16)
+        square_ref[:, at : at + size] = turned(jnp.sum(rows * rows, axis=1, keepdims=True))
+        if then is not None:
+            then(at, size)
+
+    return [
+        (functools.partial(product, at, size), functools.partial(values, at, size))
+        for at, size in spans(rows_ref.shape[0], 4 * LANES)
+    ]
 
 
 def pick_body(first, index_ref, pool_ref, rows_ref, square_ref):
-    for at, size in spans(rows_ref.shape[0], 8 * LANES):
-        pick_span(index_ref, pool_ref, rows_ref, square_ref, first, at, size)
+    staggered(pick_steps(index_ref, pool_ref, rows_ref, square_ref, first))
 
 
 def pick_rows(index, pool, first, count):
@@ -247,20 +277,27 @@
     *before, rows_ref, square_ref, kernel_ref = refs
     samples = jnp.concatenate([side_ref[...], other_ref[...]], axis=0)
     samples, own_square = halves_and_squares(samples)
-    start = 0
+
+    def early_product(early_ref, early_square_ref, start):
+        return contract_last(samples, early_ref[...])
+
+    def early_values(early_ref, early_square_ref, start, cross):
+        kernel = kernel_of(own_square + early_square_ref[...] + cross)
+        kernel_ref[:, start : start + early_ref.shape[0]] = kernel
+
+    def own_values(at, size):
+        cross = contract_last(samples, rows_ref[at : at + size, :])
+        kernel = kernel_of(own_square + square_ref[:, at : at + size] + cross)
+        kernel_ref[:, start + at : start + at + size] = kernel
+
+    steps, start = [], 0
     for early_ref, early_square_ref in zip(before[::2], before[1::2]):
-        span = early_ref.shape[0]
-        kernel_ref[:, start : start + span] = kernel_of(
-            own_square + early_square_ref[...] + contract_last(samples, early_ref[...])
+        place = (early_ref, early_square_ref, start)
+        steps.append(
+            (functools.partial(early_product, *place), functools.partial(early_values, *place))
         )
-        start += span
-    for at, size in spans(rows_ref.shape[0], 8 * LANES):
-        pick_span(index_ref, pool_ref, rows_ref, square_ref, first, at, size)
-        kernel_ref[:, start + at : start + at + size] = kernel_of(
-            own_square
-            + square_ref[:, at : at + size]
-            + contract_last(samples, rows_ref[at : at + size, :])
-        )
+        start += early_ref.shape[0]
+    staggered(steps + pick_steps(index_ref, pool_ref, rows_ref, square_ref, first, own_values))
 
 
 def pick_rows_and_own(index, pool, side, other, before, first, count):
@@ -282,13 +319,21 @@
     samples = jnp.concatenate([ref[...] for ref in refs[:parts]], axis=0)
     kernel_ref = refs[-1]
     samples, own_square = halves_and_squares(samples)
-    start = 0
+
+    def product(rows_ref, square_ref, start, at, size):
+        return contract_last(samples, rows_ref[at : at + size, :])
+
+    def values(rows_ref, square_ref, start, at, size, cross):
+        kernel = kernel_of(own_square + square_ref[:, at : at + size] + cross)
+        kernel_ref[:, start + at : start + at + size] = kernel
+
+    steps, start = [], 0
     for rows_ref, square_ref in zip(refs[parts:-1:2], refs[parts + 1 : -1 : 2]):
         for at, size in spans(rows_ref.shape[0], 2 * LANES):
-            cross = contract_last(samples, rows_ref[at : at + size, :])
-            kernel = kernel_of(own_square + square_ref[:, at : at + size] + cross)
-            kernel_ref[:, start + at : start + at + size] = kernel
+            place = (rows_ref, square_ref, start, at, size)
+            steps.append((functools.partial(product, *place), functools.partial(values, *place)))
         start += rows_ref.shape[0]
+    staggered(steps)
 
 
 def kernel_block(samples, picked):
@@ -357,7 +402,7 @@
 def finish_body(step, owns, kernels, first, residual_ref, base_ref, *refs):
     kernel_refs, (out_far, held_ref, done_ref) = refs[:kernels], refs[kernels:]
     stores = []
-    for turn, (at, size) in enumerate(spans(base_ref.shape[1], 4 * LANES)):
+    for turn, (at, size) in enumerate(spans(base_ref.shape[1], 2 * LANES)):
         gradient = gradient_span(residual_ref, kernel_refs, owns, first, at, size)
         held_ref[:, at : at + size] = base_ref[:, at : at + size] - step * gradient
         span = pl.ds(at, size)
@@ -370,7 +415,7 @@
 
 
 def finish(residual, base, owns, rests, first, step):
-    turns = len(spans(base.shape[1], 4 * LANES))
+    turns = len(spans(base.shape[1], 2 * LANES))
     kernels = [*owns, *rests]
     return call(
         functools.partial(finish_body, step, len(owns), len(kernels), first),

time: 52 us -> 51.9 us (level)
  no operation moved by 1% of the time
where the time goes in v4:
time: 51.9 us; the launch traced here: 51.7 us
  Pallas kernels  28.7 us (55%)
  starting transfers between devices  17.2 us (33%)
  local copies, waits for them, and re-layouts  1.86 us (4%)
  other arithmetic  1.49 us (3%)
  waiting for transfers between devices  1.17 us (2%)
  between operations  1.05 us (2%)
    pallas_call x11, Pallas kernels, call(): pl.pallas_call(body, in_specs=[place for _, place in operands], out_specs...  28.7 us
    ppermute x15, starting transfers between devices, flip(): return lax.ppermute(value, axis, [(i, i ^ distance) for i in range(count)])  17.2 us
    unnamed x11, local copies, waits for them, and re-layouts  1.81 us
    ppermute x15, waiting for transfers between devices, flip(): return lax.ppermute(value, axis, [(i, i ^ distance) for i in range(count)])  1.17 us
  transfers between devices with their start and end apart: 15, of which 1 were waited for; matrix products, arithmetic and copies ran while one was open for 0% of the time, Pallas kernels for 47%

profile of v4, /device:TPU:1, one launch (start us, length us, event | category | flops | bytes accessed | tf_op | source)
XLA Modules:
  0.0 51.7 jit_solution(8397401334014083437)
XLA Ops:
  0.6 0.0 copy-start
  0.7 0.7 %broadcast_subtract_fusion.1 = s32[32]{0:T(128)S(1)} fusion(s32[32]{0:T(128)} %param.7, s32[]{:T(128)S(6)} %mul.11), kind=kLoop, calls=%fused_computation.13 | loop fusion | flops 32 | bytes 260 | tf_op jit(solution)/shard_map/sub | solution.py:443
  1.3 0.7 %broadcast_subtract_fusion = s32[2048]{0:T(1024)S(1)} fusion(s32[2048]{0:T(1024)} %param.9, s32[]{:T(128)S(6)} %mul.9), kind=kLoop, calls=%fused_computation.12 | loop fusion | flops 2048 | bytes 16388 | tf_op jit(solution)/shard_map/sub | solution.py:442
  2.1 0.0 copy-done
  2.1 0.2 convolution_convert_fusion.refs_0_
  2.3 2.2 %collective-permute-start = (bf16[32,1024]{1,0:T(8,128)(2,1)S(1)}, bf16[32,1024]{1,0:T(8,128)(2,1)S(1)}, u32[]{:S(2)}, u32[]{:S(2)}) collective-permute-start(bf16[32,1024]{1,0:T(8,128)(2,1)S(1)} %convolution_convert_fusion.refs_0_), channel_id=1, source_target_pairs={{0,2},{1,3},{2,0},{3,1},{4,6},{5,7},{6,4},{7,5},{8,10},{9,11},{10,... | collective-permute-start | bytes 196616 | tf_op jit(solution)/shard_map/ppermute | solution.py:16
  4.5 2.3 %collective-permute-start.1 = (bf16[32,1024]{1,0:T(8,128)(2,1)S(1)}, bf16[32,1024]{1,0:T(8,128)(2,1)S(1)}, u32[]{:S(2)}, u32[]{:S(2)}) collective-permute-start(bf16[32,1024]{1,0:T(8,128)(2,1)S(1)} %convolution_convert_fusion.refs_0_), channel_id=1, source_target_pairs={{0,4},{1,5},{2,6},{3,7},{4,0},{5,1},{6,2},{7,3},{8,12},{9,13},{10,... | collective-permute-start | bytes 196616 | tf_op jit(solution)/shard_map/ppermute | solution.py:16
  6.8 0.0 collective-permute-start.2
  6.8 1.7 %copy-done.1 = f32[2048,301]{0,1:T(8,128)S(1)} copy-done((f32[2048,301]{0,1:T(8,128)S(1)}, f32[2048,301]{0,1:T(8,128)}, u32[]{:S(2)}) %copy-start.1) | copy-done | bytes 2465816
  8.5 5.1 %shard_map.77 = (bf16[301,2432]{1,0:T(8,128)(2,1)S(1)}, f32[2432,128]{1,0:T(8,128)S(1)}, f32[301,2048]{1,0:T(8,128)S(1)}, bf16[2305,1024]{1,0:T(8,128)(2,1)S(1)}) custom-call(s32[1,2048]{1,0:T(1,128)S(1)} %bitcast.6, f32[301,2048]{1,0:T(8,128)S(1)} %bitcast.5, bf16[2305,1024]{1,0:T(8,128)(2,1)} %pool_far.1), custom_call_target="tpu_custom_call" | custom-call | flops 1024 | bytes 1024 | tf_op jit(solution)/shard_map/pallas_call | solution.py:45
  13.6 0.0 collective-permute-done.refs_1_
  13.6 0.0 collective-permute-done.1.refs_2_
  13.6 0.0 collective-permute-done.2.refs_3_
  13.6 0.0 copy-done.2
  13.6 0.2 shard_map.78
  13.8 1.3 %collective-permute-start.3 = (bf16[128,1024]{1,0:T(8,128)(2,1)S(1)}, bf16[128,1024]{1,0:T(8,128)(2,1)S(1)}, u32[]{:S(2)}, u32[]{:S(2)}) collective-permute-start(bf16[128,1024]{1,0:T(8,128)(2,1)S(1)} %get-tuple-element.53.side_ref), channel_id=1, source_target_pairs={{0,1},{1,0},{2,3},{3,2},{4,5},{5,4},{6,7},{7,6},{8,9},{9,8},{10,11... | collective-permute-start | bytes 786440 | tf_op jit(solution)/shard_map/ppermute | solution.py:16
  15.1 1.6 %shard_map.79 = (bf16[256,1024]{1,0:T(8,128)(2,1)S(1)}, f32[1,256]{1,0:T(1,128)S(1)}) custom-call(s32[1,2048]{1,0:T(1,128)S(1)} %bitcast.7, bf16[2305,1024]{1,0:T(8,128)(2,1)S(1)} %get-tuple-element.55.pool_ref), custom_call_target="tpu_custom_call" | custom-call | flops 1024 | bytes 1024 | tf_op jit(solution)/shard_map/pallas_call | solution.py:45
  16.6 0.0 collective-permute-done.3.other_ref
  16.6 2.3 %shard_map.80 = (f32[301,128]{1,0:T(8,128)S(1)}, f32[301,128]{1,0:T(8,128)S(1)}) custom-call(bf16[128,1024]{1,0:T(8,128)(2,1)S(1)} %get-tuple-element.53.side_ref, bf16[128,1024]{1,0:T(8,128)(2,1)S(1)} %collective-permute-done.3.other_ref, bf16[2305,1024]{1,0:T(8,128)(2,1)S(1)} %get-tuple-element.55.pool_ref, f32[2432,128]{1,0:T(8,128)S(1)} %get-tuple-element.59.square_ref, ...), custom_call_target="tpu_custom_call" | custom-call | flops 1024 | bytes 1024 | tf_op jit(solution)/shard_map/pallas_call | solution.py:45
  18.9 0.1 collective-permute-start.4
  19.0 1.6 %shard_map.81 = (bf16[256,1024]{1,0:T(8,128)(2,1)S(1)}, f32[1,256]{1,0:T(1,128)S(1)}) custom-call(s32[1,2048]{1,0:T(1,128)S(1)} %bitcast.8, bf16[2305,1024]{1,0:T(8,128)(2,1)S(1)} %get-tuple-element.55.pool_ref), custom_call_target="tpu_custom_call" | custom-call | flops 1024 | bytes 1024 | tf_op jit(solution)/shard_map/pallas_call | solution.py:45
  20.6 0.0 collective-permute-done.4
  20.6 0.7 %collective-permute-start.5 = (f32[301,128]{1,0:T(8,128)S(1)}, f32[301,128]{1,0:T(8,128)S(1)}, u32[]{:S(2)}, u32[]{:S(2)}) collective-permute-start(f32[301,128]{1,0:T(8,128)S(1)} %subtract_add_fusion), channel_id=1, source_target_pairs={{0,2},{1,3},{2,0},{3,1},{4,6},{5,7},{6,4},{7,5},{8,10},{9,11},{10,... | collective-permute-start | bytes 462344 | tf_op jit(solution)/shard_map/ppermute | solution.py:16
  21.3 1.2 %collective-permute-start.7 = (bf16[128,1024]{1,0:T(8,128)(2,1)S(1)}, bf16[128,1024]{1,0:T(8,128)(2,1)S(1)}, u32[]{:S(2)}, u32[]{:S(2)}) collective-permute-start(bf16[128,1024]{1,0:T(8,128)(2,1)S(1)} %get-tuple-element.53.side_ref), channel_id=1, source_target_pairs={{0,8},{8,0},{16,24},{24,16},{1,9},{9,1},{17,25},{25,17},{2,10},{10... | collective-permute-start | bytes 786440 | tf_op jit(solution)/shard_map/ppermute | solution.py:16
  22.5 1.2 %collective-permute-start.8 = (bf16[128,1024]{1,0:T(8,128)(2,1)S(1)}, bf16[128,1024]{1,0:T(8,128)(2,1)S(1)}, u32[]{:S(2)}, u32[]{:S(2)}) collective-permute-start(bf16[128,1024]{1,0:T(8,128)(2,1)S(1)} %get-tuple-element.53.side_ref), channel_id=1, source_target_pairs={{0,16},{8,24},{16,0},{24,8},{1,17},{9,25},{17,1},{25,9},{2,18},{10... | collective-permute-start | bytes 786440 | tf_op jit(solution)/shard_map/ppermute | solution.py:16
  23.8 0.2 collective-permute-start.9
  24.0 3.4 %shard_map.82 = (bf16[512,1024]{1,0:T(8,128)(2,1)S(1)}, f32[1,512]{1,0:T(1,128)S(1)}, bf16[256,1024]{1,0:T(8,128)(2,1)S(1)}) custom-call(s32[1,2048]{1,0:T(1,128)S(1)} %bitcast.9, bf16[2305,1024]{1,0:T(8,128)(2,1)S(1)} %get-tuple-element.55.pool_ref, bf16[128,1024]{1,0:T(8,128)(2,1)S(1)} %get-tuple-element.53.side_ref, ...), custom_call_target="tpu_custom_call" | custom-call | flops 1024 | bytes 1024 | tf_op jit(solution)/shard_map/pallas_call | solution.py:45
  27.4 0.0 collective-permute-done.5
  27.5 3.3 %collective-permute-start.6 = (f32[301,128]{1,0:T(8,128)S(1)}, f32[301,128]{1,0:T(8,128)S(1)}, u32[]{:S(2)}, u32[]{:S(2)}) collective-permute-start(f32[301,128]{1,0:T(8,128)S(1)} %add.14), channel_id=1, source_target_pairs={{0,4},{1,5},{2,6},{3,7},{4,0},{5,1},{6,2},{7,3},{8,12},{9,13},{10,... | collective-permute-start | bytes 462344 | tf_op jit(solution)/shard_map/ppermute | solution.py:16
  30.7 6.2 %shard_map.83 = (bf16[1024,1024]{1,0:T(8,128)(2,1)S(1)}, f32[1,1024]{1,0:T(1,128)S(1)}, bf16[256,1024]{1,0:T(8,128)(2,1)S(1)}) custom-call(s32[1,2048]{1,0:T(1,128)S(1)} %bitcast.10, bf16[2305,1024]{1,0:T(8,128)(2,1)S(1)} %get-tuple-element.55.pool_ref, bf16[128,1024]{1,0:T(8,128)(2,1)S(1)} %get-tuple-element.53.side_ref, ...), custom_call_target="tpu_custom_call" | custom-call | flops 1024 | bytes 1024 | tf_op jit(solution)/shard_map/pallas_call | solution.py:45
  37.0 1.1 %collective-permute-done.6 = f32[301,128]{1,0:T(8,128)S(1)} collective-permute-done((f32[301,128]{1,0:T(8,128)S(1)}, f32[301,128]{1,0:T(8,128)S(1)}, u32[]{:S(2)}, u32[]{:S(2)}) %collective-permute-start.6) | collective-permute-done | bytes 154144 | tf_op jit(solution)/shard_map/ppermute | solution.py:16
  38.1 0.0 collective-permute-done.7
  38.1 0.0 collective-permute-done.8
  38.2 0.0 collective-permute-done.9
  38.2 0.8 %collective-permute-start.10 = (bf16[384,1024]{1,0:T(8,128)(2,1)S(1)}, bf16[384,1024]{1,0:T(8,128)(2,1)S(1)}, u32[]{:S(2)}, u32[]{:S(2)}) collective-permute-start(bf16[384,1024]{1,0:T(8,128)(2,1)S(1)} %constant_dynamic-update-slice_fusion.refs_0_), channel_id=1, source_target_pairs={{0,1},{1,0},{2,3},{3,2},{4,5},{5,4},{6,7},{7,6},{8,9},{9,8},{10,11... | collective-permute-start | bytes 2359304 | tf_op jit(solution)/shard_map/ppermute | solution.py:16
  39.1 1.4 %collective-permute-start.11 = (bf16[301,128]{1,0:T(8,128)(2,1)S(1)}, bf16[301,128]{1,0:T(8,128)(2,1)S(1)}, u32[]{:S(2)}, u32[]{:S(2)}) collective-permute-start(bf16[301,128]{1,0:T(8,128)(2,1)S(1)} %convert_element_type.8), channel_id=1, source_target_pairs={{0,8},{8,0},{16,24},{24,16},{1,9},{9,1},{17,25},{25,17},{2,10},{10... | collective-permute-start | bytes 231176 | tf_op jit(solution)/shard_map/ppermute | solution.py:16
  40.5 1.2 %collective-permute-start.12 = (bf16[301,128]{1,0:T(8,128)(2,1)S(1)}, bf16[301,128]{1,0:T(8,128)(2,1)S(1)}, u32[]{:S(2)}, u32[]{:S(2)}) collective-permute-start(bf16[301,128]{1,0:T(8,128)(2,1)S(1)} %convert_element_type.8), channel_id=1, source_target_pairs={{0,16},{8,24},{16,0},{24,8},{1,17},{9,25},{17,1},{25,9},{2,18},{10... | collective-permute-start | bytes 231176 | tf_op jit(solution)/shard_map/ppermute | solution.py:16
  41.7 0.1 collective-permute-start.13
  41.8 2.3 %shard_map.84.refs_2_ = bf16[384,2048]{1,0:T(8,128)(2,1)S(1)} custom-call(bf16[384,1024]{1,0:T(8,128)(2,1)S(1)} %constant_dynamic-update-slice_fusion.refs_0_, bf16[256,1024]{1,0:T(8,128)(2,1)S(1)} %get-tuple-element.56.refs_0_.refs_1_, f32[1,256]{1,0:T(1,128)S(1)} %get-tuple-element.57.refs_1_.refs_2_, ...), custom_call_target="tpu_custom_call" | custom-call | flops 1024 | bytes 1024 | tf_op jit(solution)/shard_map/pallas_call | solution.py:45
  44.1 0.0 collective-permute-done.10.refs_0_
  44.1 2.3 %shard_map.85.refs_2_ = bf16[384,2048]{1,0:T(8,128)(2,1)S(1)} custom-call(bf16[384,1024]{1,0:T(8,128)(2,1)S(1)} %collective-permute-done.10.refs_0_, bf16[256,1024]{1,0:T(8,128)(2,1)S(1)} %get-tuple-element.56.refs_0_.refs_1_, f32[1,256]{1,0:T(1,128)S(1)} %get-tuple-element.57.refs_1_.refs_2_, bf16[256,1024]{1,0:T(8,128)(2,1)S(1)} %get-tuple-element.65.refs_2_.refs_3_, ...), custom_call_target="tpu_custom_call" | custom-call | flops 1024 | bytes 1024 | tf_op jit(solution)/shard_map/pallas_call | solution.py:45
  46.4 0.0 collective-permute-done.11
  46.4 0.0 collective-permute-done.12
  46.4 0.0 collective-permute-done.13
  46.5 1.2 %collective-permute-start.14 = (bf16[301,512]{1,0:T(8,128)(2,1)S(1)}, bf16[301,512]{1,0:T(8,128)(2,1)S(1)}, u32[]{:S(2)}, u32[]{:S(2)}) collective-permute-start(bf16[301,512]{1,0:T(8,128)(2,1)S(1)} %constant_dynamic-update-slice_fusion.3.residual_ref), channel_id=1, source_target_pairs={{0,1},{1,0},{2,3},{3,2},{4,5},{5,4},{6,7},{7,6},{8,9},{9,8},{10,11... | collective-permute-start | bytes 924680 | tf_op jit(solution)/shard_map/ppermute | solution.py:16
  47.8 1.6 %shard_map.86 = (f32[301,2048]{1,0:T(8,128)S(1)}, f32[32,301]{1,0:T(8,128)}) custom-call(s32[1]{0:T(128)} %bitcast.1.place_ref, f32[301,128]{1,0:T(8,128)S(1)} %add.15.total_ref, bf16[301,512]{1,0:T(8,128)(2,1)S(1)} %constant_dynamic-update-slice_fusion.3.residual_ref, f32[301,2048]{1,0:T(8,128)S(1)} %get-tuple-element.83.base_ref, ...), custom_call_target="tpu_custom_call" | custom-call | flops 1024 | bytes 1024 | tf_op jit(solution)/shard_map/pallas_call | solution.py:45
  49.4 0.0 collective-permute-done.14.residual_ref
  49.4 2.1 %shard_map.87 = f32[301,2048]{1,0:T(8,128)} custom-call(bf16[301,512]{1,0:T(8,128)(2,1)S(1)} %collective-permute-done.14.residual_ref, f32[301,2048]{1,0:T(8,128)S(1)} %get-tuple-element.87.base_ref, bf16[256,1024]{1,0:T(8,128)(2,1)S(1)} %get-tuple-element.84.refs_0_, bf16[256,1024]{1,0:T(8,128)(2,1)S(1)} %get-tuple-element.85.refs_1_, ...), custom_call_target="tpu_custom_call" | custom-call | flops 1024 | bytes 1024 | tf_op jit(solution)/shard_map/pallas_call | solution.py:45
  (16 shorter events, 0.2 us)
Async XLA Ops:
  0.6 1.4 %copy-start = (bf16[41,1024]{1,0:T(8,128)(2,1)S(1)}, bf16[41,1024]{1,0:T(8,128)(2,1)}, u32[]{:S(2)}) copy-start(bf16[41,1024]{1,0:T(8,128)(2,1)} %param.6) | copy-start | bytes 251908
  2.3 11.3 %collective-permute-start = (bf16[32,1024]{1,0:T(8,128)(2,1)S(1)}, bf16[32,1024]{1,0:T(8,128)(2,1)S(1)}, u32[]{:S(2)}, u32[]{:S(2)}) collective-permute-start(bf16[32,1024]{1,0:T(8,128)(2,1)S(1)} %convolution_convert_fusion.refs_0_), channel_id=1, source_target_pairs={{0,2},{1,3},{2,0},{3,1},{4,6},{5,7},{6,4},{7,5},{8,10},{9,11},{10,... | collective-permute-start | bytes 196616 | tf_op jit(solution)/shard_map/ppermute | solution.py:16
  4.5 9.1 %collective-permute-start.1 = (bf16[32,1024]{1,0:T(8,128)(2,1)S(1)}, bf16[32,1024]{1,0:T(8,128)(2,1)S(1)}, u32[]{:S(2)}, u32[]{:S(2)}) collective-permute-start(bf16[32,1024]{1,0:T(8,128)(2,1)S(1)} %convolution_convert_fusion.refs_0_), channel_id=1, source_target_pairs={{0,4},{1,5},{2,6},{3,7},{4,0},{5,1},{6,2},{7,3},{8,12},{9,13},{10,... | collective-permute-start | bytes 196616 | tf_op jit(solution)/shard_map/ppermute | solution.py:16
  6.8 6.8 %collective-permute-start.2 = (bf16[32,1024]{1,0:T(8,128)(2,1)S(1)}, bf16[32,1024]{1,0:T(8,128)(2,1)S(1)}, u32[]{:S(2)}, u32[]{:S(2)}) collective-permute-start(bf16[32,1024]{1,0:T(8,128)(2,1)S(1)} %convolution_convert_fusion.refs_0_), channel_id=1, source_target_pairs={{0,6},{1,7},{2,4},{3,5},{4,2},{5,3},{6,0},{7,1},{8,14},{9,15},{10,... | collective-permute-start | bytes 196616 | tf_op jit(solution)/shard_map/ppermute | solution.py:16
  6.8 1.7 %copy-start.1 = (f32[2048,301]{0,1:T(8,128)S(1)}, f32[2048,301]{0,1:T(8,128)}, u32[]{:S(2)}) copy-start(f32[2048,301]{0,1:T(8,128)} %param.11) | copy-start | bytes 7397380
  8.5 5.1 %copy-start.2 = (f32[32,301]{1,0:T(8,128)S(1)}, f32[32,301]{1,0:T(8,128)}, u32[]{:S(2)}) copy-start(f32[32,301]{1,0:T(8,128)} %targets_ref.1) | copy-start | bytes 115588
  13.8 2.9 %collective-permute-start.3 = (bf16[128,1024]{1,0:T(8,128)(2,1)S(1)}, bf16[128,1024]{1,0:T(8,128)(2,1)S(1)}, u32[]{:S(2)}, u32[]{:S(2)}) collective-permute-start(bf16[128,1024]{1,0:T(8,128)(2,1)S(1)} %get-tuple-element.53.side_ref), channel_id=1, source_target_pairs={{0,1},{1,0},{2,3},{3,2},{4,5},{5,4},{6,7},{7,6},{8,9},{9,8},{10,11... | collective-permute-start | bytes 786440 | tf_op jit(solution)/shard_map/ppermute | solution.py:16
  18.9 1.7 %collective-permute-start.4 = (f32[301,128]{1,0:T(8,128)S(1)}, f32[301,128]{1,0:T(8,128)S(1)}, u32[]{:S(2)}, u32[]{:S(2)}) collective-permute-start(f32[301,128]{1,0:T(8,128)S(1)} %get-tuple-element.63), channel_id=1, source_target_pairs={{0,1},{1,0},{2,3},{3,2},{4,5},{5,4},{6,7},{7,6},{8,9},{9,8},{10,11... | collective-permute-start | bytes 462344 | tf_op jit(solution)/shard_map/ppermute | solution.py:16
  20.6 6.8 %collective-permute-start.5 = (f32[301,128]{1,0:T(8,128)S(1)}, f32[301,128]{1,0:T(8,128)S(1)}, u32[]{:S(2)}, u32[]{:S(2)}) collective-permute-start(f32[301,128]{1,0:T(8,128)S(1)} %subtract_add_fusion), channel_id=1, source_target_pairs={{0,2},{1,3},{2,0},{3,1},{4,6},{5,7},{6,4},{7,5},{8,10},{9,11},{10,... | collective-permute-start | bytes 462344 | tf_op jit(solution)/shard_map/ppermute | solution.py:16
  21.3 16.8 %collective-permute-start.7 = (bf16[128,1024]{1,0:T(8,128)(2,1)S(1)}, bf16[128,1024]{1,0:T(8,128)(2,1)S(1)}, u32[]{:S(2)}, u32[]{:S(2)}) collective-permute-start(bf16[128,1024]{1,0:T(8,128)(2,1)S(1)} %get-tuple-element.53.side_ref), channel_id=1, source_target_pairs={{0,8},{8,0},{16,24},{24,16},{1,9},{9,1},{17,25},{25,17},{2,10},{10... | collective-permute-start | bytes 786440 | tf_op jit(solution)/shard_map/ppermute | solution.py:16
  22.5 15.6 %collective-permute-start.8 = (bf16[128,1024]{1,0:T(8,128)(2,1)S(1)}, bf16[128,1024]{1,0:T(8,128)(2,1)S(1)}, u32[]{:S(2)}, u32[]{:S(2)}) collective-permute-start(bf16[128,1024]{1,0:T(8,128)(2,1)S(1)} %get-tuple-element.53.side_ref), channel_id=1, source_target_pairs={{0,16},{8,24},{16,0},{24,8},{1,17},{9,25},{17,1},{25,9},{2,18},{10... | collective-permute-start | bytes 786440 | tf_op jit(solution)/shard_map/ppermute | solution.py:16
  23.8 14.4 %collective-permute-start.9 = (bf16[128,1024]{1,0:T(8,128)(2,1)S(1)}, bf16[128,1024]{1,0:T(8,128)(2,1)S(1)}, u32[]{:S(2)}, u32[]{:S(2)}) collective-permute-start(bf16[128,1024]{1,0:T(8,128)(2,1)S(1)} %get-tuple-element.53.side_ref), channel_id=1, source_target_pairs={{0,24},{8,16},{16,8},{24,0},{1,25},{9,17},{17,9},{25,1},{2,26},{10... | collective-permute-start | bytes 786440 | tf_op jit(solution)/shard_map/ppermute | solution.py:16
  27.5 10.6 %collective-permute-start.6 = (f32[301,128]{1,0:T(8,128)S(1)}, f32[301,128]{1,0:T(8,128)S(1)}, u32[]{:S(2)}, u32[]{:S(2)}) collective-permute-start(f32[301,128]{1,0:T(8,128)S(1)} %add.14), channel_id=1, source_target_pairs={{0,4},{1,5},{2,6},{3,7},{4,0},{5,1},{6,2},{7,3},{8,12},{9,13},{10,... | collective-permute-start | bytes 462344 | tf_op jit(solution)/shard_map/ppermute | solution.py:16
  38.2 5.9 %collective-permute-start.10 = (bf16[384,1024]{1,0:T(8,128)(2,1)S(1)}, bf16[384,1024]{1,0:T(8,128)(2,1)S(1)}, u32[]{:S(2)}, u32[]{:S(2)}) collective-permute-start(bf16[384,1024]{1,0:T(8,128)(2,1)S(1)} %constant_dynamic-update-slice_fusion.refs_0_), channel_id=1, source_target_pairs={{0,1},{1,0},{2,3},{3,2},{4,5},{5,4},{6,7},{7,6},{8,9},{9,8},{10,11... | collective-permute-start | bytes 2359304 | tf_op jit(solution)/shard_map/ppermute | solution.py:16
  39.1 7.3 %collective-permute-start.11 = (bf16[301,128]{1,0:T(8,128)(2,1)S(1)}, bf16[301,128]{1,0:T(8,128)(2,1)S(1)}, u32[]{:S(2)}, u32[]{:S(2)}) collective-permute-start(bf16[301,128]{1,0:T(8,128)(2,1)S(1)} %convert_element_type.8), channel_id=1, source_target_pairs={{0,8},{8,0},{16,24},{24,16},{1,9},{9,1},{17,25},{25,17},{2,10},{10... | collective-permute-start | bytes 231176 | tf_op jit(solution)/shard_map/ppermute | solution.py:16
  40.5 5.9 %collective-permute-start.12 = (bf16[301,128]{1,0:T(8,128)(2,1)S(1)}, bf16[301,128]{1,0:T(8,128)(2,1)S(1)}, u32[]{:S(2)}, u32[]{:S(2)}) collective-permute-start(bf16[301,128]{1,0:T(8,128)(2,1)S(1)} %convert_element_type.8), channel_id=1, source_target_pairs={{0,16},{8,24},{16,0},{24,8},{1,17},{9,25},{17,1},{25,9},{2,18},{10... | collective-permute-start | bytes 231176 | tf_op jit(solution)/shard_map/ppermute | solution.py:16
  41.7 4.7 %collective-permute-start.13 = (bf16[301,128]{1,0:T(8,128)(2,1)S(1)}, bf16[301,128]{1,0:T(8,128)(2,1)S(1)}, u32[]{:S(2)}, u32[]{:S(2)}) collective-permute-start(bf16[301,128]{1,0:T(8,128)(2,1)S(1)} %convert_element_type.8), channel_id=1, source_target_pairs={{0,24},{8,16},{16,8},{24,0},{1,25},{9,17},{17,9},{25,1},{2,26},{10... | collective-permute-start | bytes 231176 | tf_op jit(solution)/shard_map/ppermute | solution.py:16
  46.5 2.9 %collective-permute-start.14 = (bf16[301,512]{1,0:T(8,128)(2,1)S(1)}, bf16[301,512]{1,0:T(8,128)(2,1)S(1)}, u32[]{:S(2)}, u32[]{:S(2)}) collective-permute-start(bf16[301,512]{1,0:T(8,128)(2,1)S(1)} %constant_dynamic-update-slice_fusion.3.residual_ref), channel_id=1, source_target_pairs={{0,1},{1,0},{2,3},{3,2},{4,5},{5,4},{6,7},{7,6},{8,9},{9,8},{10,11... | collective-permute-start | bytes 924680 | tf_op jit(solution)/shard_map/ppermute | solution.py:16

commit v5 on v4

--- a/solution.py
+++ b/solution.py
@@ -63,10 +63,6 @@
     held()
 
 
-def narrow(index, pool_ref):
-    return index.astype(jnp.int16 if pool_ref.shape[0] < 1 << 15 else jnp.int32)
-
-
 def one_hot(hit):
     return jnp.where(hit, jnp.bfloat16(1.0), jnp.bfloat16(0.0))
 
@@ -78,6 +74,16 @@
             for at in range(0, column.shape[0], LANES)
         ],
         axis=1,
+    )
+
+
+def column_of(row):
+    return jnp.concatenate(
+        [
+            jnp.broadcast_to(row[:, at : at + LANES], (LANES, LANES)).T
+            for at in range(0, row.shape[1], LANES)
+        ],
+        axis=0,
     )
 
 
@@ -96,19 +102,26 @@
     return jnp.concatenate([pool_ref[at : at + whole, :], rows], axis=0)
 
 
-def place_body(index_ref, base_ref, pool_far, placed_ref, square_ref, kept_ref, pool_ref, done_ref):
+def place_body(index_ref, base_ref, pool_far, *refs):
+    placed_ref, square_ref, column_ref, kept_ref, pool_ref, done_ref = refs
     fetch = pltpu.make_async_copy(pool_far, pool_ref, done_ref)
     fetch.start()
-    index = narrow(index_ref[...], pool_ref)
+    index = column_of(index_ref[...]).astype(column_ref.dtype)
+    column_ref[...] = index
     base = base_ref[...]
     kept_ref[...] = base
     half = base.astype(jnp.bfloat16)
+    lane = lax.broadcasted_iota(index.dtype, index.shape, 1)
     cuts = spans(placed_ref.shape[1], 2 * LANES)
     left, arrival = list(cuts), min(3, len(cuts) - 1)
     for turn, (at, size) in enumerate(cuts):
-        place = lax.broadcasted_iota(index.dtype, (size, index.shape[1]), 0)
-        chosen = one_hot(index - jnp.asarray(at, index.dtype) == place)
-        placed_ref[:, at : at + size] = contract_last(half, chosen).astype(jnp.bfloat16)
+        chosen = [
+            one_hot(index - jnp.asarray(part, index.dtype) == lane)
+            for part in range(at, at + size, LANES)
+        ]
+        placed_ref[:, at : at + size] = jnp.dot(
+            half, jnp.concatenate(chosen, axis=1), preferred_element_type=jnp.float32
+        ).astype(jnp.bfloat16)
         if turn == arrival:
             fetch.wait()
         share = -(-len(left) // (len(cuts) - turn)) if turn >= arrival else 0
@@ -122,17 +135,19 @@
 
 def place_coefficients(index, base, pool):
     width = tiles(pool.shape[0])
+    narrow = jnp.int16 if pool.shape[0] < 1 << 15 else jnp.int32
     return call(
         place_body,
         [(index, WHOLE), (base, WHOLE), (pool, FAR)],
         [
             ((base.shape[0], width), jnp.bfloat16, WHOLE),
             ((width, LANES), jnp.float32, WHOLE),
+            ((index.shape[1], LANES), narrow, WHOLE),
             (base.shape, jnp.float32, WHOLE),
             (pool.shape, jnp.bfloat16, WHOLE),
         ],
         [pltpu.SemaphoreType.DMA(())],
-        limit=40,
+        limit=39,
     )
 
 
@@ -182,16 +197,6 @@
     return (wide * -2.0).astype(jnp.bfloat16), jnp.sum(wide * wide, axis=1, keepdims=True)
 
 
-def column_of(row):
-    return jnp.concatenate(
-        [
-            jnp.broadcast_to(row[:, at : at + LANES], (LANES, LANES)).T
-            for at in range(0, row.shape[1], LANES)
-        ],
-        axis=0,
-    )
-
-
 def terms_body(side_ref, other_ref, pool_ref, square_ref, placed_ref, *refs):
     terms_ref, other_terms_ref, kernel_ref = refs
     samples = jnp.concatenate([side_ref[...], other_ref[...]], axis=0)
@@ -231,8 +236,7 @@
     whole = pool_ref.shape[0] // LANES * LANES
 
     def product(at, size):
-        wanted = column_of(index_ref[:, first + at : first + at + size])
-        place = narrow(wanted, pool_ref)
+        place = index_ref[first + at : first + at + size, :]
         lane = lax.broadcasted_iota(place.dtype, (size, LANES), 1)
         chosen = jnp.concatenate(
             [
@@ -242,7 +246,7 @@
             axis=1,
         )
         rows = jnp.dot(chosen, pool_ref[:whole, :], preferred_element_type=jnp.float32)
-        return wanted, rows
+        return place.astype(jnp.int32), rows
 
     def values(at, size, result):
         wanted, rows = result
@@ -402,7 +406,7 @@
 def finish_body(step, owns, kernels, first, residual_ref, base_ref, *refs):
     kernel_refs, (out_far, held_ref, done_ref) = refs[:kernels], refs[kernels:]
     stores = []
-    for turn, (at, size) in enumerate(spans(base_ref.shape[1], 2 * LANES)):
+    for turn, (at, size) in enumerate(spans(base_ref.shape[1], 4 * LANES)):
         gradient = gradient_span(residual_ref, kernel_refs, owns, first, at, size)
         held_ref[:, at : at + size] = base_ref[:, at : at + size] - step * gradient
         span = pl.ds(at, size)
@@ -415,7 +419,7 @@
 
 
 def finish(residual, base, owns, rests, first, step):
-    turns = len(spans(base.shape[1], 2 * LANES))
+    turns = len(spans(base.shape[1], 4 * LANES))
     kernels = [*owns, *rests]
     return call(
         functools.partial(finish_body, step, len(owns), len(kernels), first),
@@ -452,7 +456,9 @@
 
     place = jnp.reshape(far_place, (1,)).astype(jnp.int32)
     index, place = lax.optimization_barrier((indices[:count].reshape(1, -1), place))
-    placed, pool_square, base, pool = place_coefficients(index, coefficients.T, centre_pool)
+    placed, pool_square, index, base, pool = place_coefficients(
+        index, coefficients.T, centre_pool
+    )
     placed, *pieces = lax.optimization_barrier((placed, *pieces))
     side, placed_targets = arrange(place, targets, pieces)
     other = flip(side, "centre", 1)

time: 51.9 us -> 51.9 us (level)
  no operation moved by 1% of the time
where the time goes in v5:
time: 51.9 us; the launch traced here: 51.6 us
  Pallas kernels  28.5 us (55%)
  starting transfers between devices  17.2 us (33%)
  local copies, waits for them, and re-layouts  1.86 us (4%)
  other arithmetic  1.48 us (3%)
  waiting for transfers between devices  1.25 us (2%)
  between operations  1.05 us (2%)
    pallas_call x11, Pallas kernels, call(): pl.pallas_call(body, in_specs=[place for _, place in operands], out_specs...  28.5 us
    ppermute x15, starting transfers between devices, flip(): return lax.ppermute(value, axis, [(i, i ^ distance) for i in range(count)])  17.2 us
    unnamed x11, local copies, waits for them, and re-layouts  1.81 us
    ppermute x15, waiting for transfers between devices, flip(): return lax.ppermute(value, axis, [(i, i ^ distance) for i in range(count)])  1.25 us
  transfers between devices with their start and end apart: 15, of which 1 were waited for; matrix products, arithmetic and copies ran while one was open for 0% of the time, Pallas kernels for 47%

profile of v5, /device:TPU:1, one launch (start us, length us, event | category | flops | bytes accessed | tf_op | source)
XLA Modules:
  0.0 51.6 jit_solution(14227912594826212431)
XLA Ops:
  0.6 0.0 copy-start
  0.7 0.7 %broadcast_subtract_fusion.1 = s32[32]{0:T(128)S(1)} fusion(s32[32]{0:T(128)} %param.7, s32[]{:T(128)S(6)} %mul.11), kind=kLoop, calls=%fused_computation.13 | loop fusion | flops 32 | bytes 260 | tf_op jit(solution)/shard_map/sub | solution.py:447
  1.3 0.7 %broadcast_subtract_fusion = s32[2048]{0:T(1024)S(1)} fusion(s32[2048]{0:T(1024)} %param.9, s32[]{:T(128)S(6)} %mul.9), kind=kLoop, calls=%fused_computation.12 | loop fusion | flops 2048 | bytes 16388 | tf_op jit(solution)/shard_map/sub | solution.py:446
  2.1 0.0 copy-done
  2.1 0.2 convolution_convert_fusion.refs_0_
  2.3 2.2 %collective-permute-start = (bf16[32,1024]{1,0:T(8,128)(2,1)S(1)}, bf16[32,1024]{1,0:T(8,128)(2,1)S(1)}, u32[]{:S(2)}, u32[]{:S(2)}) collective-permute-start(bf16[32,1024]{1,0:T(8,128)(2,1)S(1)} %convolution_convert_fusion.refs_0_), channel_id=1, source_target_pairs={{0,2},{1,3},{2,0},{3,1},{4,6},{5,7},{6,4},{7,5},{8,10},{9,11},{10,... | collective-permute-start | bytes 196616 | tf_op jit(solution)/shard_map/ppermute | solution.py:16
  4.5 2.3 %collective-permute-start.1 = (bf16[32,1024]{1,0:T(8,128)(2,1)S(1)}, bf16[32,1024]{1,0:T(8,128)(2,1)S(1)}, u32[]{:S(2)}, u32[]{:S(2)}) collective-permute-start(bf16[32,1024]{1,0:T(8,128)(2,1)S(1)} %convolution_convert_fusion.refs_0_), channel_id=1, source_target_pairs={{0,4},{1,5},{2,6},{3,7},{4,0},{5,1},{6,2},{7,3},{8,12},{9,13},{10,... | collective-permute-start | bytes 196616 | tf_op jit(solution)/shard_map/ppermute | solution.py:16
  6.8 0.0 collective-permute-start.2
  6.8 1.7 %copy-done.1 = f32[2048,301]{0,1:T(8,128)S(1)} copy-done((f32[2048,301]{0,1:T(8,128)S(1)}, f32[2048,301]{0,1:T(8,128)}, u32[]{:S(2)}) %copy-start.1) | copy-done | bytes 2465816
  8.5 5.1 %shard_map.77 = (bf16[301,2432]{1,0:T(8,128)(2,1)S(1)}, f32[2432,128]{1,0:T(8,128)S(1)}, s16[2048,128]{1,0:T(8,128)(2,1)S(1)}, f32[301,2048]{1,0:T(8,128)S(1)}, bf16[2305,1024]{1,0:T(8,128)(2,1)S(1)}) custom-call(s32[1,2048]{1,0:T(1,128)S(1)} %bitcast.6, f32[301,2048]{1,0:T(8,128)S(1)} %bitcast.5, bf16[2305,1024]{1,0:T(8,128)(2,1)} %pool_far.1), custom_call_target="tpu_custom_call" | custom-call | flops 1024 | bytes 1024 | tf_op jit(solution)/shard_map/pallas_call | solution.py:45
  13.6 0.0 collective-permute-done.refs_1_
  13.6 0.0 collective-permute-done.1.refs_2_
  13.6 0.0 collective-permute-done.2.refs_3_
  13.6 0.0 copy-done.2
  13.6 0.2 shard_map.78
  13.8 1.3 %collective-permute-start.3 = (bf16[128,1024]{1,0:T(8,128)(2,1)S(1)}, bf16[128,1024]{1,0:T(8,128)(2,1)S(1)}, u32[]{:S(2)}, u32[]{:S(2)}) collective-permute-start(bf16[128,1024]{1,0:T(8,128)(2,1)S(1)} %get-tuple-element.54.side_ref), channel_id=1, source_target_pairs={{0,1},{1,0},{2,3},{3,2},{4,5},{5,4},{6,7},{7,6},{8,9},{9,8},{10,11... | collective-permute-start | bytes 786440 | tf_op jit(solution)/shard_map/ppermute | solution.py:16
  15.1 1.6 %shard_map.79 = (bf16[256,1024]{1,0:T(8,128)(2,1)S(1)}, f32[1,256]{1,0:T(1,128)S(1)}) custom-call(s16[2048,128]{1,0:T(8,128)(2,1)S(1)} %get-tuple-element.74.index_ref, bf16[2305,1024]{1,0:T(8,128)(2,1)S(1)} %get-tuple-element.57.pool_ref), custom_call_target="tpu_custom_call" | custom-call | flops 1024 | bytes 1024 | tf_op jit(solution)/shard_map/pallas_call | solution.py:45
  16.6 0.0 collective-permute-done.3.other_ref
  16.6 2.3 %shard_map.80 = (f32[301,128]{1,0:T(8,128)S(1)}, f32[301,128]{1,0:T(8,128)S(1)}) custom-call(bf16[128,1024]{1,0:T(8,128)(2,1)S(1)} %get-tuple-element.54.side_ref, bf16[128,1024]{1,0:T(8,128)(2,1)S(1)} %collective-permute-done.3.other_ref, bf16[2305,1024]{1,0:T(8,128)(2,1)S(1)} %get-tuple-element.57.pool_ref, f32[2432,128]{1,0:T(8,128)S(1)} %get-tuple-element.61.square_ref, ...), custom_call_target="tpu_custom_call" | custom-call | flops 1024 | bytes 1024 | tf_op jit(solution)/shard_map/pallas_call | solution.py:45
  19.0 0.1 collective-permute-start.4
  19.0 1.5 %shard_map.81 = (bf16[256,1024]{1,0:T(8,128)(2,1)S(1)}, f32[1,256]{1,0:T(1,128)S(1)}) custom-call(s16[2048,128]{1,0:T(8,128)(2,1)S(1)} %get-tuple-element.74.index_ref, bf16[2305,1024]{1,0:T(8,128)(2,1)S(1)} %get-tuple-element.57.pool_ref), custom_call_target="tpu_custom_call" | custom-call | flops 1024 | bytes 1024 | tf_op jit(solution)/shard_map/pallas_call | solution.py:45
  20.6 0.0 collective-permute-done.4
  20.6 0.7 %collective-permute-start.5 = (f32[301,128]{1,0:T(8,128)S(1)}, f32[301,128]{1,0:T(8,128)S(1)}, u32[]{:S(2)}, u32[]{:S(2)}) collective-permute-start(f32[301,128]{1,0:T(8,128)S(1)} %subtract_add_fusion), channel_id=1, source_target_pairs={{0,2},{1,3},{2,0},{3,1},{4,6},{5,7},{6,4},{7,5},{8,10},{9,11},{10,... | collective-permute-start | bytes 462344 | tf_op jit(solution)/shard_map/ppermute | solution.py:16
  21.3 1.2 %collective-permute-start.7 = (bf16[128,1024]{1,0:T(8,128)(2,1)S(1)}, bf16[128,1024]{1,0:T(8,128)(2,1)S(1)}, u32[]{:S(2)}, u32[]{:S(2)}) collective-permute-start(bf16[128,1024]{1,0:T(8,128)(2,1)S(1)} %get-tuple-element.54.side_ref), channel_id=1, source_target_pairs={{0,8},{8,0},{16,24},{24,16},{1,9},{9,1},{17,25},{25,17},{2,10},{10... | collective-permute-start | bytes 786440 | tf_op jit(solution)/shard_map/ppermute | solution.py:16
  22.5 1.2 %collective-permute-start.8 = (bf16[128,1024]{1,0:T(8,128)(2,1)S(1)}, bf16[128,1024]{1,0:T(8,128)(2,1)S(1)}, u32[]{:S(2)}, u32[]{:S(2)}) collective-permute-start(bf16[128,1024]{1,0:T(8,128)(2,1)S(1)} %get-tuple-element.54.side_ref), channel_id=1, source_target_pairs={{0,16},{8,24},{16,0},{24,8},{1,17},{9,25},{17,1},{25,9},{2,18},{10... | collective-permute-start | bytes 786440 | tf_op jit(solution)/shard_map/ppermute | solution.py:16
  23.7 0.2 collective-permute-start.9
  23.9 3.5 %shard_map.82 = (bf16[512,1024]{1,0:T(8,128)(2,1)S(1)}, f32[1,512]{1,0:T(1,128)S(1)}, bf16[256,1024]{1,0:T(8,128)(2,1)S(1)}) custom-call(s16[2048,128]{1,0:T(8,128)(2,1)S(1)} %get-tuple-element.74.index_ref, bf16[2305,1024]{1,0:T(8,128)(2,1)S(1)} %get-tuple-element.57.pool_ref, bf16[128,1024]{1,0:T(8,128)(2,1)S(1)} %get-tuple-element.54.side_ref, ...), custom_call_target="tpu_custom_call" | custom-call | flops 1024 | bytes 1024 | tf_op jit(solution)/shard_map/pallas_call | solution.py:45
  27.4 0.0 collective-permute-done.5
  27.5 3.3 %collective-permute-start.6 = (f32[301,128]{1,0:T(8,128)S(1)}, f32[301,128]{1,0:T(8,128)S(1)}, u32[]{:S(2)}, u32[]{:S(2)}) collective-permute-start(f32[301,128]{1,0:T(8,128)S(1)} %add.14), channel_id=1, source_target_pairs={{0,4},{1,5},{2,6},{3,7},{4,0},{5,1},{6,2},{7,3},{8,12},{9,13},{10,... | collective-permute-start | bytes 462344 | tf_op jit(solution)/shard_map/ppermute | solution.py:16
  30.7 6.2 %shard_map.83 = (bf16[1024,1024]{1,0:T(8,128)(2,1)S(1)}, f32[1,1024]{1,0:T(1,128)S(1)}, bf16[256,1024]{1,0:T(8,128)(2,1)S(1)}) custom-call(s16[2048,128]{1,0:T(8,128)(2,1)S(1)} %get-tuple-element.74.index_ref, bf16[2305,1024]{1,0:T(8,128)(2,1)S(1)} %get-tuple-element.57.pool_ref, bf16[128,1024]{1,0:T(8,128)(2,1)S(1)} %get-tuple-element.54.side_ref, ...), custom_call_target="tpu_custom_call" | custom-call | flops 1024 | bytes 1024 | tf_op jit(solution)/shard_map/pallas_call | solution.py:45
  36.9 1.2 %collective-permute-done.6 = f32[301,128]{1,0:T(8,128)S(1)} collective-permute-done((f32[301,128]{1,0:T(8,128)S(1)}, f32[301,128]{1,0:T(8,128)S(1)}, u32[]{:S(2)}, u32[]{:S(2)}) %collective-permute-start.6) | collective-permute-done | bytes 154144 | tf_op jit(solution)/shard_map/ppermute | solution.py:16
  38.2 0.0 collective-permute-done.7
  38.2 0.0 collective-permute-done.8
  38.2 0.0 collective-permute-done.9
  38.3 0.8 %collective-permute-start.10 = (bf16[384,1024]{1,0:T(8,128)(2,1)S(1)}, bf16[384,1024]{1,0:T(8,128)(2,1)S(1)}, u32[]{:S(2)}, u32[]{:S(2)}) collective-permute-start(bf16[384,1024]{1,0:T(8,128)(2,1)S(1)} %constant_dynamic-update-slice_fusion.refs_0_), channel_id=1, source_target_pairs={{0,1},{1,0},{2,3},{3,2},{4,5},{5,4},{6,7},{7,6},{8,9},{9,8},{10,11... | collective-permute-start | bytes 2359304 | tf_op jit(solution)/shard_map/ppermute | solution.py:16
  39.1 1.4 %collective-permute-start.11 = (bf16[301,128]{1,0:T(8,128)(2,1)S(1)}, bf16[301,128]{1,0:T(8,128)(2,1)S(1)}, u32[]{:S(2)}, u32[]{:S(2)}) collective-permute-start(bf16[301,128]{1,0:T(8,128)(2,1)S(1)} %convert_element_type.8), channel_id=1, source_target_pairs={{0,8},{8,0},{16,24},{24,16},{1,9},{9,1},{17,25},{25,17},{2,10},{10... | collective-permute-start | bytes 231176 | tf_op jit(solution)/shard_map/ppermute | solution.py:16
  40.5 1.2 %collective-permute-start.12 = (bf16[301,128]{1,0:T(8,128)(2,1)S(1)}, bf16[301,128]{1,0:T(8,128)(2,1)S(1)}, u32[]{:S(2)}, u32[]{:S(2)}) collective-permute-start(bf16[301,128]{1,0:T(8,128)(2,1)S(1)} %convert_element_type.8), channel_id=1, source_target_pairs={{0,16},{8,24},{16,0},{24,8},{1,17},{9,25},{17,1},{25,9},{2,18},{10... | collective-permute-start | bytes 231176 | tf_op jit(solution)/shard_map/ppermute | solution.py:16
  41.7 0.1 collective-permute-start.13
  41.8 2.3 %shard_map.84.refs_2_ = bf16[384,2048]{1,0:T(8,128)(2,1)S(1)} custom-call(bf16[384,1024]{1,0:T(8,128)(2,1)S(1)} %constant_dynamic-update-slice_fusion.refs_0_, bf16[256,1024]{1,0:T(8,128)(2,1)S(1)} %get-tuple-element.58.refs_0_.refs_1_, f32[1,256]{1,0:T(1,128)S(1)} %get-tuple-element.59.refs_1_.refs_2_, ...), custom_call_target="tpu_custom_call" | custom-call | flops 1024 | bytes 1024 | tf_op jit(solution)/shard_map/pallas_call | solution.py:45
  44.1 0.0 collective-permute-done.10.refs_0_
  44.1 2.3 %shard_map.85.refs_2_ = bf16[384,2048]{1,0:T(8,128)(2,1)S(1)} custom-call(bf16[384,1024]{1,0:T(8,128)(2,1)S(1)} %collective-permute-done.10.refs_0_, bf16[256,1024]{1,0:T(8,128)(2,1)S(1)} %get-tuple-element.58.refs_0_.refs_1_, f32[1,256]{1,0:T(1,128)S(1)} %get-tuple-element.59.refs_1_.refs_2_, bf16[256,1024]{1,0:T(8,128)(2,1)S(1)} %get-tuple-element.67.refs_2_.refs_3_, ...), custom_call_target="tpu_custom_call" | custom-call | flops 1024 | bytes 1024 | tf_op jit(solution)/shard_map/pallas_call | solution.py:45
  46.4 0.0 collective-permute-done.11
  46.4 0.0 collective-permute-done.12
  46.4 0.0 collective-permute-done.13
  46.5 1.3 %collective-permute-start.14 = (bf16[301,512]{1,0:T(8,128)(2,1)S(1)}, bf16[301,512]{1,0:T(8,128)(2,1)S(1)}, u32[]{:S(2)}, u32[]{:S(2)}) collective-permute-start(bf16[301,512]{1,0:T(8,128)(2,1)S(1)} %constant_dynamic-update-slice_fusion.3.residual_ref), channel_id=1, source_target_pairs={{0,1},{1,0},{2,3},{3,2},{4,5},{5,4},{6,7},{7,6},{8,9},{9,8},{10,11... | collective-permute-start | bytes 924680 | tf_op jit(solution)/shard_map/ppermute | solution.py:16
  47.8 1.7 %shard_map.86 = (f32[301,2048]{1,0:T(8,128)S(1)}, f32[32,301]{1,0:T(8,128)}) custom-call(s32[1]{0:T(128)} %bitcast.1.place_ref, f32[301,128]{1,0:T(8,128)S(1)} %add.15.total_ref, bf16[301,512]{1,0:T(8,128)(2,1)S(1)} %constant_dynamic-update-slice_fusion.3.residual_ref, f32[301,2048]{1,0:T(8,128)S(1)} %get-tuple-element.85.base_ref, ...), custom_call_target="tpu_custom_call" | custom-call | flops 1024 | bytes 1024 | tf_op jit(solution)/shard_map/pallas_call | solution.py:45
  49.5 0.0 collective-permute-done.14.residual_ref
  49.5 2.0 %shard_map.87 = f32[301,2048]{1,0:T(8,128)} custom-call(bf16[301,512]{1,0:T(8,128)(2,1)S(1)} %collective-permute-done.14.residual_ref, f32[301,2048]{1,0:T(8,128)S(1)} %get-tuple-element.89.base_ref, bf16[256,1024]{1,0:T(8,128)(2,1)S(1)} %get-tuple-element.86.refs_0_, bf16[256,1024]{1,0:T(8,128)(2,1)S(1)} %get-tuple-element.87.refs_1_, ...), custom_call_target="tpu_custom_call" | custom-call | flops 1024 | bytes 1024 | tf_op jit(solution)/shard_map/pallas_call | solution.py:45
  (16 shorter events, 0.2 us)
Async XLA Ops:
  0.6 1.4 %copy-start = (bf16[41,1024]{1,0:T(8,128)(2,1)S(1)}, bf16[41,1024]{1,0:T(8,128)(2,1)}, u32[]{:S(2)}) copy-start(bf16[41,1024]{1,0:T(8,128)(2,1)} %param.6) | copy-start | bytes 251908
  2.3 11.3 %collective-permute-start = (bf16[32,1024]{1,0:T(8,128)(2,1)S(1)}, bf16[32,1024]{1,0:T(8,128)(2,1)S(1)}, u32[]{:S(2)}, u32[]{:S(2)}) collective-permute-start(bf16[32,1024]{1,0:T(8,128)(2,1)S(1)} %convolution_convert_fusion.refs_0_), channel_id=1, source_target_pairs={{0,2},{1,3},{2,0},{3,1},{4,6},{5,7},{6,4},{7,5},{8,10},{9,11},{10,... | collective-permute-start | bytes 196616 | tf_op jit(solution)/shard_map/ppermute | solution.py:16
  4.5 9.1 %collective-permute-start.1 = (bf16[32,1024]{1,0:T(8,128)(2,1)S(1)}, bf16[32,1024]{1,0:T(8,128)(2,1)S(1)}, u32[]{:S(2)}, u32[]{:S(2)}) collective-permute-start(bf16[32,1024]{1,0:T(8,128)(2,1)S(1)} %convolution_convert_fusion.refs_0_), channel_id=1, source_target_pairs={{0,4},{1,5},{2,6},{3,7},{4,0},{5,1},{6,2},{7,3},{8,12},{9,13},{10,... | collective-permute-start | bytes 196616 | tf_op jit(solution)/shard_map/ppermute | solution.py:16
  6.8 6.8 %collective-permute-start.2 = (bf16[32,1024]{1,0:T(8,128)(2,1)S(1)}, bf16[32,1024]{1,0:T(8,128)(2,1)S(1)}, u32[]{:S(2)}, u32[]{:S(2)}) collective-permute-start(bf16[32,1024]{1,0:T(8,128)(2,1)S(1)} %convolution_convert_fusion.refs_0_), channel_id=1, source_target_pairs={{0,6},{1,7},{2,4},{3,5},{4,2},{5,3},{6,0},{7,1},{8,14},{9,15},{10,... | collective-permute-start | bytes 196616 | tf_op jit(solution)/shard_map/ppermute | solution.py:16
  6.8 1.7 %copy-start.1 = (f32[2048,301]{0,1:T(8,128)S(1)}, f32[2048,301]{0,1:T(8,128)}, u32[]{:S(2)}) copy-start(f32[2048,301]{0,1:T(8,128)} %param.11) | copy-start | bytes 7397380
  8.5 5.1 %copy-start.2 = (f32[32,301]{1,0:T(8,128)S(1)}, f32[32,301]{1,0:T(8,128)}, u32[]{:S(2)}) copy-start(f32[32,301]{1,0:T(8,128)} %targets_ref.1) | copy-start | bytes 115588
  13.8 2.9 %collective-permute-start.3 = (bf16[128,1024]{1,0:T(8,128)(2,1)S(1)}, bf16[128,1024]{1,0:T(8,128)(2,1)S(1)}, u32[]{:S(2)}, u32[]{:S(2)}) collective-permute-start(bf16[128,1024]{1,0:T(8,128)(2,1)S(1)} %get-tuple-element.54.side_ref), channel_id=1, source_target_pairs={{0,1},{1,0},{2,3},{3,2},{4,5},{5,4},{6,7},{7,6},{8,9},{9,8},{10,11... | collective-permute-start | bytes 786440 | tf_op jit(solution)/shard_map/ppermute | solution.py:16
  19.0 1.6 %collective-permute-start.4 = (f32[301,128]{1,0:T(8,128)S(1)}, f32[301,128]{1,0:T(8,128)S(1)}, u32[]{:S(2)}, u32[]{:S(2)}) collective-permute-start(f32[301,128]{1,0:T(8,128)S(1)} %get-tuple-element.65), channel_id=1, source_target_pairs={{0,1},{1,0},{2,3},{3,2},{4,5},{5,4},{6,7},{7,6},{8,9},{9,8},{10,11... | collective-permute-start | bytes 462344 | tf_op jit(solution)/shard_map/ppermute | solution.py:16
  20.6 6.8 %collective-permute-start.5 = (f32[301,128]{1,0:T(8,128)S(1)}, f32[301,128]{1,0:T(8,128)S(1)}, u32[]{:S(2)}, u32[]{:S(2)}) collective-permute-start(f32[301,128]{1,0:T(8,128)S(1)} %subtract_add_fusion), channel_id=1, source_target_pairs={{0,2},{1,3},{2,0},{3,1},{4,6},{5,7},{6,4},{7,5},{8,10},{9,11},{10,... | collective-permute-start | bytes 462344 | tf_op jit(solution)/shard_map/ppermute | solution.py:16
  21.3 16.9 %collective-permute-start.7 = (bf16[128,1024]{1,0:T(8,128)(2,1)S(1)}, bf16[128,1024]{1,0:T(8,128)(2,1)S(1)}, u32[]{:S(2)}, u32[]{:S(2)}) collective-permute-start(bf16[128,1024]{1,0:T(8,128)(2,1)S(1)} %get-tuple-element.54.side_ref), channel_id=1, source_target_pairs={{0,8},{8,0},{16,24},{24,16},{1,9},{9,1},{17,25},{25,17},{2,10},{10... | collective-permute-start | bytes 786440 | tf_op jit(solution)/shard_map/ppermute | solution.py:16
  22.5 15.7 %collective-permute-start.8 = (bf16[128,1024]{1,0:T(8,128)(2,1)S(1)}, bf16[128,1024]{1,0:T(8,128)(2,1)S(1)}, u32[]{:S(2)}, u32[]{:S(2)}) collective-permute-start(bf16[128,1024]{1,0:T(8,128)(2,1)S(1)} %get-tuple-element.54.side_ref), channel_id=1, source_target_pairs={{0,16},{8,24},{16,0},{24,8},{1,17},{9,25},{17,1},{25,9},{2,18},{10... | collective-permute-start | bytes 786440 | tf_op jit(solution)/shard_map/ppermute | solution.py:16
  23.7 14.4 %collective-permute-start.9 = (bf16[128,1024]{1,0:T(8,128)(2,1)S(1)}, bf16[128,1024]{1,0:T(8,128)(2,1)S(1)}, u32[]{:S(2)}, u32[]{:S(2)}) collective-permute-start(bf16[128,1024]{1,0:T(8,128)(2,1)S(1)} %get-tuple-element.54.side_ref), channel_id=1, source_target_pairs={{0,24},{8,16},{16,8},{24,0},{1,25},{9,17},{17,9},{25,1},{2,26},{10... | collective-permute-start | bytes 786440 | tf_op jit(solution)/shard_map/ppermute | solution.py:16
  27.5 10.7 %collective-permute-start.6 = (f32[301,128]{1,0:T(8,128)S(1)}, f32[301,128]{1,0:T(8,128)S(1)}, u32[]{:S(2)}, u32[]{:S(2)}) collective-permute-start(f32[301,128]{1,0:T(8,128)S(1)} %add.14), channel_id=1, source_target_pairs={{0,4},{1,5},{2,6},{3,7},{4,0},{5,1},{6,2},{7,3},{8,12},{9,13},{10,... | collective-permute-start | bytes 462344 | tf_op jit(solution)/shard_map/ppermute | solution.py:16
  38.3 5.8 %collective-permute-start.10 = (bf16[384,1024]{1,0:T(8,128)(2,1)S(1)}, bf16[384,1024]{1,0:T(8,128)(2,1)S(1)}, u32[]{:S(2)}, u32[]{:S(2)}) collective-permute-start(bf16[384,1024]{1,0:T(8,128)(2,1)S(1)} %constant_dynamic-update-slice_fusion.refs_0_), channel_id=1, source_target_pairs={{0,1},{1,0},{2,3},{3,2},{4,5},{5,4},{6,7},{7,6},{8,9},{9,8},{10,11... | collective-permute-start | bytes 2359304 | tf_op jit(solution)/shard_map/ppermute | solution.py:16
  39.1 7.3 %collective-permute-start.11 = (bf16[301,128]{1,0:T(8,128)(2,1)S(1)}, bf16[301,128]{1,0:T(8,128)(2,1)S(1)}, u32[]{:S(2)}, u32[]{:S(2)}) collective-permute-start(bf16[301,128]{1,0:T(8,128)(2,1)S(1)} %convert_element_type.8), channel_id=1, source_target_pairs={{0,8},{8,0},{16,24},{24,16},{1,9},{9,1},{17,25},{25,17},{2,10},{10... | collective-permute-start | bytes 231176 | tf_op jit(solution)/shard_map/ppermute | solution.py:16
  40.5 5.9 %collective-permute-start.12 = (bf16[301,128]{1,0:T(8,128)(2,1)S(1)}, bf16[301,128]{1,0:T(8,128)(2,1)S(1)}, u32[]{:S(2)}, u32[]{:S(2)}) collective-permute-start(bf16[301,128]{1,0:T(8,128)(2,1)S(1)} %convert_element_type.8), channel_id=1, source_target_pairs={{0,16},{8,24},{16,0},{24,8},{1,17},{9,25},{17,1},{25,9},{2,18},{10... | collective-permute-start | bytes 231176 | tf_op jit(solution)/shard_map/ppermute | solution.py:16
  41.7 4.7 %collective-permute-start.13 = (bf16[301,128]{1,0:T(8,128)(2,1)S(1)}, bf16[301,128]{1,0:T(8,128)(2,1)S(1)}, u32[]{:S(2)}, u32[]{:S(2)}) collective-permute-start(bf16[301,128]{1,0:T(8,128)(2,1)S(1)} %convert_element_type.8), channel_id=1, source_target_pairs={{0,24},{8,16},{16,8},{24,0},{1,25},{9,17},{17,9},{25,1},{2,26},{10... | collective-permute-start | bytes 231176 | tf_op jit(solution)/shard_map/ppermute | solution.py:16
  46.5 2.9 %collective-permute-start.14 = (bf16[301,512]{1,0:T(8,128)(2,1)S(1)}, bf16[301,512]{1,0:T(8,128)(2,1)S(1)}, u32[]{:S(2)}, u32[]{:S(2)}) collective-permute-start(bf16[301,512]{1,0:T(8,128)(2,1)S(1)} %constant_dynamic-update-slice_fusion.3.residual_ref), channel_id=1, source_target_pairs={{0,1},{1,0},{2,3},{3,2},{4,5},{5,4},{6,7},{7,6},{8,9},{9,8},{10,11... | collective-permute-start | bytes 924680 | tf_op jit(solution)/shard_map/ppermute | solution.py:16

commit v6 on v5

--- a/solution.py
+++ b/solution.py
@@ -440,14 +440,13 @@
     hold_all = batch_total * (centre_index.shape[0] + batch_pool.shape[1]) * 2 <= 1 << 24
 
     count = centre_index.shape[0]
-    indices = lax.optimization_barrier(
-        jnp.concatenate(
-            [
-                centre_index - centre_place * centre_pool.shape[0],
-                batch_index - device_place * batch_pool.shape[0],
-            ]
-        )
-    )
+    both = jnp.concatenate([centre_index, batch_index])
+    starts = jnp.where(
+        jnp.arange(both.shape[0]) < count,
+        centre_place * centre_pool.shape[0],
+        device_place * batch_pool.shape[0],
+    )
+    indices = lax.optimization_barrier(both - starts)
     chosen = indices[count:, None] == jnp.arange(batch_pool.shape[0])
     local_rows = jnp.dot(
         chosen.astype(jnp.bfloat16), batch_pool, preferred_element_type=jnp.float32

time: 51.9 us -> 51.3 us (0.988)
  other arithmetic: 1.48 us -> 0.84 us
    sub x2 -> x1, other arithmetic: 1.39 us -> 0.75 us  [on_device(): indices = lax.optimization_barrier(both - starts)]
where the time goes in v6:
time: 51.3 us; the launch traced here: 51.1 us
  Pallas kernels  28.5 us (56%)
  starting transfers between devices  17.3 us (34%)
  local copies, waits for them, and re-layouts  1.98 us (4%)
  waiting for transfers between devices  1.23 us (2%)
  between operations  1.05 us (2%)
  other arithmetic  0.84 us (2%)
    pallas_call x11, Pallas kernels, call(): pl.pallas_call(body, in_specs=[place for _, place in operands], out_specs...  28.5 us
    ppermute x15, starting transfers between devices, flip(): return lax.ppermute(value, axis, [(i, i ^ distance) for i in range(count)])  17.3 us
    unnamed x11, local copies, waits for them, and re-layouts  1.93 us
    ppermute x15, waiting for transfers between devices, flip(): return lax.ppermute(value, axis, [(i, i ^ distance) for i in range(count)])  1.23 us
  transfers between devices with their start and end apart: 15, of which 1 were waited for; matrix products, arithmetic and copies ran while one was open for 0% of the time, Pallas kernels for 47%

profile of v6, /device:TPU:1, one launch (start us, length us, event | category | flops | bytes accessed | tf_op | source)
XLA Modules:
  0.0 51.1 jit_solution(556040540337008466)
XLA Ops:
  0.6 0.0 copy-start
  0.7 0.8 %add_subtract_fusion = s32[2080]{0:T(1024)S(1)} fusion(s32[32]{0:T(128)} %param.7, s32[2048]{0:T(1024)} %param.9, s32[]{:T(128)S(6)} %mul.11, s32[]{:T(128)S(6)} %mul.9), kind=kLoop, calls=%fused_computation.10 | loop fusion | flops 8320 | bytes 16648 | tf_op jit(solution)/shard_map/sub | solution.py:449
  1.4 0.1 copy-done
  1.5 0.2 convolution_convert_fusion.refs_0_
  1.7 2.2 %collective-permute-start = (bf16[32,1024]{1,0:T(8,128)(2,1)S(1)}, bf16[32,1024]{1,0:T(8,128)(2,1)S(1)}, u32[]{:S(2)}, u32[]{:S(2)}) collective-permute-start(bf16[32,1024]{1,0:T(8,128)(2,1)S(1)} %convolution_convert_fusion.refs_0_), channel_id=1, source_target_pairs={{0,2},{1,3},{2,0},{3,1},{4,6},{5,7},{6,4},{7,5},{8,10},{9,11},{10,... | collective-permute-start | bytes 196616 | tf_op jit(solution)/shard_map/ppermute | solution.py:16
  3.9 2.3 %collective-permute-start.1 = (bf16[32,1024]{1,0:T(8,128)(2,1)S(1)}, bf16[32,1024]{1,0:T(8,128)(2,1)S(1)}, u32[]{:S(2)}, u32[]{:S(2)}) collective-permute-start(bf16[32,1024]{1,0:T(8,128)(2,1)S(1)} %convolution_convert_fusion.refs_0_), channel_id=1, source_target_pairs={{0,4},{1,5},{2,6},{3,7},{4,0},{5,1},{6,2},{7,3},{8,12},{9,13},{10,... | collective-permute-start | bytes 196616 | tf_op jit(solution)/shard_map/ppermute | solution.py:16
  6.2 0.0 collective-permute-start.2
  6.2 0.0 copy-start.1
  6.2 1.7 %copy-done.1 = f32[2048,301]{0,1:T(8,128)S(1)} copy-done((f32[2048,301]{0,1:T(8,128)S(1)}, f32[2048,301]{0,1:T(8,128)}, u32[]{:S(2)}) %copy-start.1) | copy-done | bytes 2465816
  7.9 5.1 %shard_map.77 = (bf16[301,2432]{1,0:T(8,128)(2,1)S(1)}, f32[2432,128]{1,0:T(8,128)S(1)}, s16[2048,128]{1,0:T(8,128)(2,1)S(1)}, f32[301,2048]{1,0:T(8,128)S(1)}, bf16[2305,1024]{1,0:T(8,128)(2,1)S(1)}) custom-call(s32[1,2048]{1,0:T(1,128)S(1)} %bitcast.6, f32[301,2048]{1,0:T(8,128)S(1)} %bitcast.5, bf16[2305,1024]{1,0:T(8,128)(2,1)} %pool_far.1), custom_call_target="tpu_custom_call" | custom-call | flops 1024 | bytes 1024 | tf_op jit(solution)/shard_map/pallas_call | solution.py:45
  13.0 0.0 collective-permute-done.refs_1_
  13.0 0.0 collective-permute-done.1.refs_2_
  13.1 0.0 collective-permute-done.2.refs_3_
  13.1 0.0 copy-done.2
  13.1 0.2 shard_map.78
  13.2 1.3 %collective-permute-start.3 = (bf16[128,1024]{1,0:T(8,128)(2,1)S(1)}, bf16[128,1024]{1,0:T(8,128)(2,1)S(1)}, u32[]{:S(2)}, u32[]{:S(2)}) collective-permute-start(bf16[128,1024]{1,0:T(8,128)(2,1)S(1)} %get-tuple-element.54.side_ref), channel_id=1, source_target_pairs={{0,1},{1,0},{2,3},{3,2},{4,5},{5,4},{6,7},{7,6},{8,9},{9,8},{10,11... | collective-permute-start | bytes 786440 | tf_op jit(solution)/shard_map/ppermute | solution.py:16
  14.5 1.6 %shard_map.79 = (bf16[256,1024]{1,0:T(8,128)(2,1)S(1)}, f32[1,256]{1,0:T(1,128)S(1)}) custom-call(s16[2048,128]{1,0:T(8,128)(2,1)S(1)} %get-tuple-element.74.index_ref, bf16[2305,1024]{1,0:T(8,128)(2,1)S(1)} %get-tuple-element.57.pool_ref), custom_call_target="tpu_custom_call" | custom-call | flops 1024 | bytes 1024 | tf_op jit(solution)/shard_map/pallas_call | solution.py:45
  16.1 0.0 collective-permute-done.3.other_ref
  16.1 2.3 %shard_map.80 = (f32[301,128]{1,0:T(8,128)S(1)}, f32[301,128]{1,0:T(8,128)S(1)}) custom-call(bf16[128,1024]{1,0:T(8,128)(2,1)S(1)} %get-tuple-element.54.side_ref, bf16[128,1024]{1,0:T(8,128)(2,1)S(1)} %collective-permute-done.3.other_ref, bf16[2305,1024]{1,0:T(8,128)(2,1)S(1)} %get-tuple-element.57.pool_ref, f32[2432,128]{1,0:T(8,128)S(1)} %get-tuple-element.61.square_ref, ...), custom_call_target="tpu_custom_call" | custom-call | flops 1024 | bytes 1024 | tf_op jit(solution)/shard_map/pallas_call | solution.py:45
  18.4 0.1 collective-permute-start.4
  18.5 1.5 %shard_map.81 = (bf16[256,1024]{1,0:T(8,128)(2,1)S(1)}, f32[1,256]{1,0:T(1,128)S(1)}) custom-call(s16[2048,128]{1,0:T(8,128)(2,1)S(1)} %get-tuple-element.74.index_ref, bf16[2305,1024]{1,0:T(8,128)(2,1)S(1)} %get-tuple-element.57.pool_ref), custom_call_target="tpu_custom_call" | custom-call | flops 1024 | bytes 1024 | tf_op jit(solution)/shard_map/pallas_call | solution.py:45
  20.0 0.0 collective-permute-done.4
  20.1 0.7 %collective-permute-start.5 = (f32[301,128]{1,0:T(8,128)S(1)}, f32[301,128]{1,0:T(8,128)S(1)}, u32[]{:S(2)}, u32[]{:S(2)}) collective-permute-start(f32[301,128]{1,0:T(8,128)S(1)} %subtract_add_fusion), channel_id=1, source_target_pairs={{0,2},{1,3},{2,0},{3,1},{4,6},{5,7},{6,4},{7,5},{8,10},{9,11},{10,... | collective-permute-start | bytes 462344 | tf_op jit(solution)/shard_map/ppermute | solution.py:16
  20.8 1.2 %collective-permute-start.7 = (bf16[128,1024]{1,0:T(8,128)(2,1)S(1)}, bf16[128,1024]{1,0:T(8,128)(2,1)S(1)}, u32[]{:S(2)}, u32[]{:S(2)}) collective-permute-start(bf16[128,1024]{1,0:T(8,128)(2,1)S(1)} %get-tuple-element.54.side_ref), channel_id=1, source_target_pairs={{0,8},{8,0},{16,24},{24,16},{1,9},{9,1},{17,25},{25,17},{2,10},{10... | collective-permute-start | bytes 786440 | tf_op jit(solution)/shard_map/ppermute | solution.py:16
  22.0 1.2 %collective-permute-start.8 = (bf16[128,1024]{1,0:T(8,128)(2,1)S(1)}, bf16[128,1024]{1,0:T(8,128)(2,1)S(1)}, u32[]{:S(2)}, u32[]{:S(2)}) collective-permute-start(bf16[128,1024]{1,0:T(8,128)(2,1)S(1)} %get-tuple-element.54.side_ref), channel_id=1, source_target_pairs={{0,16},{8,24},{16,0},{24,8},{1,17},{9,25},{17,1},{25,9},{2,18},{10... | collective-permute-start | bytes 786440 | tf_op jit(solution)/shard_map/ppermute | solution.py:16
  23.2 0.2 collective-permute-start.9
  23.4 3.5 %shard_map.82 = (bf16[512,1024]{1,0:T(8,128)(2,1)S(1)}, f32[1,512]{1,0:T(1,128)S(1)}, bf16[256,1024]{1,0:T(8,128)(2,1)S(1)}) custom-call(s16[2048,128]{1,0:T(8,128)(2,1)S(1)} %get-tuple-element.74.index_ref, bf16[2305,1024]{1,0:T(8,128)(2,1)S(1)} %get-tuple-element.57.pool_ref, bf16[128,1024]{1,0:T(8,128)(2,1)S(1)} %get-tuple-element.54.side_ref, ...), custom_call_target="tpu_custom_call" | custom-call | flops 1024 | bytes 1024 | tf_op jit(solution)/shard_map/pallas_call | solution.py:45
  26.9 0.0 collective-permute-done.5
  26.9 3.3 %collective-permute-start.6 = (f32[301,128]{1,0:T(8,128)S(1)}, f32[301,128]{1,0:T(8,128)S(1)}, u32[]{:S(2)}, u32[]{:S(2)}) collective-permute-start(f32[301,128]{1,0:T(8,128)S(1)} %add.14), channel_id=1, source_target_pairs={{0,4},{1,5},{2,6},{3,7},{4,0},{5,1},{6,2},{7,3},{8,12},{9,13},{10,... | collective-permute-start | bytes 462344 | tf_op jit(solution)/shard_map/ppermute | solution.py:16
  30.2 6.2 %shard_map.83 = (bf16[1024,1024]{1,0:T(8,128)(2,1)S(1)}, f32[1,1024]{1,0:T(1,128)S(1)}, bf16[256,1024]{1,0:T(8,128)(2,1)S(1)}) custom-call(s16[2048,128]{1,0:T(8,128)(2,1)S(1)} %get-tuple-element.74.index_ref, bf16[2305,1024]{1,0:T(8,128)(2,1)S(1)} %get-tuple-element.57.pool_ref, bf16[128,1024]{1,0:T(8,128)(2,1)S(1)} %get-tuple-element.54.side_ref, ...), custom_call_target="tpu_custom_call" | custom-call | flops 1024 | bytes 1024 | tf_op jit(solution)/shard_map/pallas_call | solution.py:45
  36.4 1.2 %collective-permute-done.6 = f32[301,128]{1,0:T(8,128)S(1)} collective-permute-done((f32[301,128]{1,0:T(8,128)S(1)}, f32[301,128]{1,0:T(8,128)S(1)}, u32[]{:S(2)}, u32[]{:S(2)}) %collective-permute-start.6) | collective-permute-done | bytes 154144 | tf_op jit(solution)/shard_map/ppermute | solution.py:16
  37.6 0.0 collective-permute-done.7
  37.6 0.0 collective-permute-done.8
  37.6 0.0 collective-permute-done.9
  37.7 0.8 %collective-permute-start.10 = (bf16[384,1024]{1,0:T(8,128)(2,1)S(1)}, bf16[384,1024]{1,0:T(8,128)(2,1)S(1)}, u32[]{:S(2)}, u32[]{:S(2)}) collective-permute-start(bf16[384,1024]{1,0:T(8,128)(2,1)S(1)} %constant_dynamic-update-slice_fusion.refs_0_), channel_id=1, source_target_pairs={{0,1},{1,0},{2,3},{3,2},{4,5},{5,4},{6,7},{7,6},{8,9},{9,8},{10,11... | collective-permute-start | bytes 2359304 | tf_op jit(solution)/shard_map/ppermute | solution.py:16
  38.5 1.4 %collective-permute-start.11 = (bf16[301,128]{1,0:T(8,128)(2,1)S(1)}, bf16[301,128]{1,0:T(8,128)(2,1)S(1)}, u32[]{:S(2)}, u32[]{:S(2)}) collective-permute-start(bf16[301,128]{1,0:T(8,128)(2,1)S(1)} %convert_element_type.8), channel_id=1, source_target_pairs={{0,8},{8,0},{16,24},{24,16},{1,9},{9,1},{17,25},{25,17},{2,10},{10... | collective-permute-start | bytes 231176 | tf_op jit(solution)/shard_map/ppermute | solution.py:16
  40.0 1.2 %collective-permute-start.12 = (bf16[301,128]{1,0:T(8,128)(2,1)S(1)}, bf16[301,128]{1,0:T(8,128)(2,1)S(1)}, u32[]{:S(2)}, u32[]{:S(2)}) collective-permute-start(bf16[301,128]{1,0:T(8,128)(2,1)S(1)} %convert_element_type.8), channel_id=1, source_target_pairs={{0,16},{8,24},{16,0},{24,8},{1,17},{9,25},{17,1},{25,9},{2,18},{10... | collective-permute-start | bytes 231176 | tf_op jit(solution)/shard_map/ppermute | solution.py:16
  41.2 0.0 collective-permute-start.13
  41.3 2.3 %shard_map.84.refs_2_ = bf16[384,2048]{1,0:T(8,128)(2,1)S(1)} custom-call(bf16[384,1024]{1,0:T(8,128)(2,1)S(1)} %constant_dynamic-update-slice_fusion.refs_0_, bf16[256,1024]{1,0:T(8,128)(2,1)S(1)} %get-tuple-element.58.refs_0_.refs_1_, f32[1,256]{1,0:T(1,128)S(1)} %get-tuple-element.59.refs_1_.refs_2_, ...), custom_call_target="tpu_custom_call" | custom-call | flops 1024 | bytes 1024 | tf_op jit(solution)/shard_map/pallas_call | solution.py:45
  43.5 0.0 collective-permute-done.10.refs_0_
  43.6 2.3 %shard_map.85.refs_2_ = bf16[384,2048]{1,0:T(8,128)(2,1)S(1)} custom-call(bf16[384,1024]{1,0:T(8,128)(2,1)S(1)} %collective-permute-done.10.refs_0_, bf16[256,1024]{1,0:T(8,128)(2,1)S(1)} %get-tuple-element.58.refs_0_.refs_1_, f32[1,256]{1,0:T(1,128)S(1)} %get-tuple-element.59.refs_1_.refs_2_, bf16[256,1024]{1,0:T(8,128)(2,1)S(1)} %get-tuple-element.67.refs_2_.refs_3_, ...), custom_call_target="tpu_custom_call" | custom-call | flops 1024 | bytes 1024 | tf_op jit(solution)/shard_map/pallas_call | solution.py:45
  45.8 0.0 collective-permute-done.11
  45.9 0.0 collective-permute-done.12
  45.9 0.0 collective-permute-done.13
  46.0 1.3 %collective-permute-start.14 = (bf16[301,512]{1,0:T(8,128)(2,1)S(1)}, bf16[301,512]{1,0:T(8,128)(2,1)S(1)}, u32[]{:S(2)}, u32[]{:S(2)}) collective-permute-start(bf16[301,512]{1,0:T(8,128)(2,1)S(1)} %constant_dynamic-update-slice_fusion.3.residual_ref), channel_id=1, source_target_pairs={{0,1},{1,0},{2,3},{3,2},{4,5},{5,4},{6,7},{7,6},{8,9},{9,8},{10,11... | collective-permute-start | bytes 924680 | tf_op jit(solution)/shard_map/ppermute | solution.py:16
  47.3 1.7 %shard_map.86 = (f32[301,2048]{1,0:T(8,128)S(1)}, f32[32,301]{1,0:T(8,128)}) custom-call(s32[1]{0:T(128)} %bitcast.1.place_ref, f32[301,128]{1,0:T(8,128)S(1)} %add.15.total_ref, bf16[301,512]{1,0:T(8,128)(2,1)S(1)} %constant_dynamic-update-slice_fusion.3.residual_ref, f32[301,2048]{1,0:T(8,128)S(1)} %get-tuple-element.85.base_ref, ...), custom_call_target="tpu_custom_call" | custom-call | flops 1024 | bytes 1024 | tf_op jit(solution)/shard_map/pallas_call | solution.py:45
  48.9 0.0 collective-permute-done.14.residual_ref
  48.9 2.0 %shard_map.87 = f32[301,2048]{1,0:T(8,128)} custom-call(bf16[301,512]{1,0:T(8,128)(2,1)S(1)} %collective-permute-done.14.residual_ref, f32[301,2048]{1,0:T(8,128)S(1)} %get-tuple-element.89.base_ref, bf16[256,1024]{1,0:T(8,128)(2,1)S(1)} %get-tuple-element.86.refs_0_, bf16[256,1024]{1,0:T(8,128)(2,1)S(1)} %get-tuple-element.87.refs_1_, ...), custom_call_target="tpu_custom_call" | custom-call | flops 1024 | bytes 1024 | tf_op jit(solution)/shard_map/pallas_call | solution.py:45
  (14 shorter events, 0.2 us)
Async XLA Ops:
  0.6 0.9 %copy-start = (bf16[41,1024]{1,0:T(8,128)(2,1)S(1)}, bf16[41,1024]{1,0:T(8,128)(2,1)}, u32[]{:S(2)}) copy-start(bf16[41,1024]{1,0:T(8,128)(2,1)} %param.6) | copy-start | bytes 251908
  1.7 11.3 %collective-permute-start = (bf16[32,1024]{1,0:T(8,128)(2,1)S(1)}, bf16[32,1024]{1,0:T(8,128)(2,1)S(1)}, u32[]{:S(2)}, u32[]{:S(2)}) collective-permute-start(bf16[32,1024]{1,0:T(8,128)(2,1)S(1)} %convolution_convert_fusion.refs_0_), channel_id=1, source_target_pairs={{0,2},{1,3},{2,0},{3,1},{4,6},{5,7},{6,4},{7,5},{8,10},{9,11},{10,... | collective-permute-start | bytes 196616 | tf_op jit(solution)/shard_map/ppermute | solution.py:16
  3.9 9.1 %collective-permute-start.1 = (bf16[32,1024]{1,0:T(8,128)(2,1)S(1)}, bf16[32,1024]{1,0:T(8,128)(2,1)S(1)}, u32[]{:S(2)}, u32[]{:S(2)}) collective-permute-start(bf16[32,1024]{1,0:T(8,128)(2,1)S(1)} %convolution_convert_fusion.refs_0_), channel_id=1, source_target_pairs={{0,4},{1,5},{2,6},{3,7},{4,0},{5,1},{6,2},{7,3},{8,12},{9,13},{10,... | collective-permute-start | bytes 196616 | tf_op jit(solution)/shard_map/ppermute | solution.py:16
  6.2 6.8 %collective-permute-start.2 = (bf16[32,1024]{1,0:T(8,128)(2,1)S(1)}, bf16[32,1024]{1,0:T(8,128)(2,1)S(1)}, u32[]{:S(2)}, u32[]{:S(2)}) collective-permute-start(bf16[32,1024]{1,0:T(8,128)(2,1)S(1)} %convolution_convert_fusion.refs_0_), channel_id=1, source_target_pairs={{0,6},{1,7},{2,4},{3,5},{4,2},{5,3},{6,0},{7,1},{8,14},{9,15},{10,... | collective-permute-start | bytes 196616 | tf_op jit(solution)/shard_map/ppermute | solution.py:16
  6.2 1.7 %copy-start.1 = (f32[2048,301]{0,1:T(8,128)S(1)}, f32[2048,301]{0,1:T(8,128)}, u32[]{:S(2)}) copy-start(f32[2048,301]{0,1:T(8,128)} %param.11) | copy-start | bytes 7397380
  7.9 5.1 %copy-start.2 = (f32[32,301]{1,0:T(8,128)S(1)}, f32[32,301]{1,0:T(8,128)}, u32[]{:S(2)}) copy-start(f32[32,301]{1,0:T(8,128)} %targets_ref.1) | copy-start | bytes 115588
  13.2 2.9 %collective-permute-start.3 = (bf16[128,1024]{1,0:T(8,128)(2,1)S(1)}, bf16[128,1024]{1,0:T(8,128)(2,1)S(1)}, u32[]{:S(2)}, u32[]{:S(2)}) collective-permute-start(bf16[128,1024]{1,0:T(8,128)(2,1)S(1)} %get-tuple-element.54.side_ref), channel_id=1, source_target_pairs={{0,1},{1,0},{2,3},{3,2},{4,5},{5,4},{6,7},{7,6},{8,9},{9,8},{10,11... | collective-permute-start | bytes 786440 | tf_op jit(solution)/shard_map/ppermute | solution.py:16
  18.4 1.6 %collective-permute-start.4 = (f32[301,128]{1,0:T(8,128)S(1)}, f32[301,128]{1,0:T(8,128)S(1)}, u32[]{:S(2)}, u32[]{:S(2)}) collective-permute-start(f32[301,128]{1,0:T(8,128)S(1)} %get-tuple-element.65), channel_id=1, source_target_pairs={{0,1},{1,0},{2,3},{3,2},{4,5},{5,4},{6,7},{7,6},{8,9},{9,8},{10,11... | collective-permute-start | bytes 462344 | tf_op jit(solution)/shard_map/ppermute | solution.py:16
  20.1 6.8 %collective-permute-start.5 = (f32[301,128]{1,0:T(8,128)S(1)}, f32[301,128]{1,0:T(8,128)S(1)}, u32[]{:S(2)}, u32[]{:S(2)}) collective-permute-start(f32[301,128]{1,0:T(8,128)S(1)} %subtract_add_fusion), channel_id=1, source_target_pairs={{0,2},{1,3},{2,0},{3,1},{4,6},{5,7},{6,4},{7,5},{8,10},{9,11},{10,... | collective-permute-start | bytes 462344 | tf_op jit(solution)/shard_map/ppermute | solution.py:16
  20.8 16.9 %collective-permute-start.7 = (bf16[128,1024]{1,0:T(8,128)(2,1)S(1)}, bf16[128,1024]{1,0:T(8,128)(2,1)S(1)}, u32[]{:S(2)}, u32[]{:S(2)}) collective-permute-start(bf16[128,1024]{1,0:T(8,128)(2,1)S(1)} %get-tuple-element.54.side_ref), channel_id=1, source_target_pairs={{0,8},{8,0},{16,24},{24,16},{1,9},{9,1},{17,25},{25,17},{2,10},{10... | collective-permute-start | bytes 786440 | tf_op jit(solution)/shard_map/ppermute | solution.py:16
  22.0 15.7 %collective-permute-start.8 = (bf16[128,1024]{1,0:T(8,128)(2,1)S(1)}, bf16[128,1024]{1,0:T(8,128)(2,1)S(1)}, u32[]{:S(2)}, u32[]{:S(2)}) collective-permute-start(bf16[128,1024]{1,0:T(8,128)(2,1)S(1)} %get-tuple-element.54.side_ref), channel_id=1, source_target_pairs={{0,16},{8,24},{16,0},{24,8},{1,17},{9,25},{17,1},{25,9},{2,18},{10... | collective-permute-start | bytes 786440 | tf_op jit(solution)/shard_map/ppermute | solution.py:16
  23.2 14.4 %collective-permute-start.9 = (bf16[128,1024]{1,0:T(8,128)(2,1)S(1)}, bf16[128,1024]{1,0:T(8,128)(2,1)S(1)}, u32[]{:S(2)}, u32[]{:S(2)}) collective-permute-start(bf16[128,1024]{1,0:T(8,128)(2,1)S(1)} %get-tuple-element.54.side_ref), channel_id=1, source_target_pairs={{0,24},{8,16},{16,8},{24,0},{1,25},{9,17},{17,9},{25,1},{2,26},{10... | collective-permute-start | bytes 786440 | tf_op jit(solution)/shard_map/ppermute | solution.py:16
  26.9 10.7 %collective-permute-start.6 = (f32[301,128]{1,0:T(8,128)S(1)}, f32[301,128]{1,0:T(8,128)S(1)}, u32[]{:S(2)}, u32[]{:S(2)}) collective-permute-start(f32[301,128]{1,0:T(8,128)S(1)} %add.14), channel_id=1, source_target_pairs={{0,4},{1,5},{2,6},{3,7},{4,0},{5,1},{6,2},{7,3},{8,12},{9,13},{10,... | collective-permute-start | bytes 462344 | tf_op jit(solution)/shard_map/ppermute | solution.py:16
  37.7 5.8 %collective-permute-start.10 = (bf16[384,1024]{1,0:T(8,128)(2,1)S(1)}, bf16[384,1024]{1,0:T(8,128)(2,1)S(1)}, u32[]{:S(2)}, u32[]{:S(2)}) collective-permute-start(bf16[384,1024]{1,0:T(8,128)(2,1)S(1)} %constant_dynamic-update-slice_fusion.refs_0_), channel_id=1, source_target_pairs={{0,1},{1,0},{2,3},{3,2},{4,5},{5,4},{6,7},{7,6},{8,9},{9,8},{10,11... | collective-permute-start | bytes 2359304 | tf_op jit(solution)/shard_map/ppermute | solution.py:16
  38.5 7.3 %collective-permute-start.11 = (bf16[301,128]{1,0:T(8,128)(2,1)S(1)}, bf16[301,128]{1,0:T(8,128)(2,1)S(1)}, u32[]{:S(2)}, u32[]{:S(2)}) collective-permute-start(bf16[301,128]{1,0:T(8,128)(2,1)S(1)} %convert_element_type.8), channel_id=1, source_target_pairs={{0,8},{8,0},{16,24},{24,16},{1,9},{9,1},{17,25},{25,17},{2,10},{10... | collective-permute-start | bytes 231176 | tf_op jit(solution)/shard_map/ppermute | solution.py:16
  40.0 5.9 %collective-permute-start.12 = (bf16[301,128]{1,0:T(8,128)(2,1)S(1)}, bf16[301,128]{1,0:T(8,128)(2,1)S(1)}, u32[]{:S(2)}, u32[]{:S(2)}) collective-permute-start(bf16[301,128]{1,0:T(8,128)(2,1)S(1)} %convert_element_type.8), channel_id=1, source_target_pairs={{0,16},{8,24},{16,0},{24,8},{1,17},{9,25},{17,1},{25,9},{2,18},{10... | collective-permute-start | bytes 231176 | tf_op jit(solution)/shard_map/ppermute | solution.py:16
  41.2 4.7 %collective-permute-start.13 = (bf16[301,128]{1,0:T(8,128)(2,1)S(1)}, bf16[301,128]{1,0:T(8,128)(2,1)S(1)}, u32[]{:S(2)}, u32[]{:S(2)}) collective-permute-start(bf16[301,128]{1,0:T(8,128)(2,1)S(1)} %convert_element_type.8), channel_id=1, source_target_pairs={{0,24},{8,16},{16,8},{24,0},{1,25},{9,17},{17,9},{25,1},{2,26},{10... | collective-permute-start | bytes 231176 | tf_op jit(solution)/shard_map/ppermute | solution.py:16
  46.0 2.9 %collective-permute-start.14 = (bf16[301,512]{1,0:T(8,128)(2,1)S(1)}, bf16[301,512]{1,0:T(8,128)(2,1)S(1)}, u32[]{:S(2)}, u32[]{:S(2)}) collective-permute-start(bf16[301,512]{1,0:T(8,128)(2,1)S(1)} %constant_dynamic-update-slice_fusion.3.residual_ref), channel_id=1, source_target_pairs={{0,1},{1,0},{2,3},{3,2},{4,5},{5,4},{6,7},{7,6},{8,9},{9,8},{10,11... | collective-permute-start | bytes 924680 | tf_op jit(solution)/shard_map/ppermute | solution.py:16

commit v7 on v6

--- a/solution.py
+++ b/solution.py
@@ -355,7 +355,9 @@
     own_refs, rest_refs = kernel_refs[:owns], kernel_refs[owns:]
     span = own_refs[0].shape[1]
     own_ref, own_at = own_refs[at // span], at % span
-    rows = residual_ref.shape[1] - sum(rest_ref.shape[0] for rest_ref in rest_refs)
+    rows = own_ref.shape[0] // 2
+    rest_rows = residual_ref.shape[1] - rows
+    rest_at = rest_rows if first else 0
     gradient = jnp.dot(
         residual_ref[:, :rows],
         own_ref[first : first + rows, own_at : own_at + size],
@@ -363,7 +365,9 @@
     )
     for rest_ref in rest_refs:
         gradient = gradient + jnp.dot(
-            residual_ref[:, rows:], rest_ref[:, at : at + size], preferred_element_type=jnp.float32
+            residual_ref[:, rows:],
+            rest_ref[rest_at : rest_at + rest_rows, at : at + size],
+            preferred_element_type=jnp.float32,
         )
     return gradient
 
@@ -494,11 +498,11 @@
         side_rows = jnp.concatenate(foreign, axis=0)
         other_rows = flip(side_rows, "centre", 1)
     residual_side = total.astype(jnp.bfloat16)
-    rests, other_rests = [], []
+    rests = []
     if hold_all:
-        rests, other_rests = [kernel_block([side_rows], picked)], [kernel_block([other_rows], picked)]
+        rests = [kernel_block([side_rows, other_rows], picked)]
         parts = [residual_side] + [flip(residual_side, "batch", k) for k in range(1, batch_size)]
-        rests, other_rests, parts = lax.optimization_barrier((rests, other_rests, parts))
+        rests, parts = lax.optimization_barrier((rests, parts))
         residual_side = jnp.concatenate(parts, axis=1)
     residual_other = flip(residual_side, "centre", 1)
 
@@ -507,7 +511,7 @@
     updated, residual = descend(
         place, total, own_count, residual_side, start, kernels, rests, step
     )
-    updated = finish(residual_other, updated, kernels, other_rests, rows, step)
+    updated = finish(residual_other, updated, kernels, rests, rows, step)
     if not hold_all:
         updated = base + lax.psum(updated, "batch")
     return (updated.T, residual)

time: 51.3 us -> 51.3 us (level)
    pallas_call x11 -> x10, Pallas kernels: 28.5 us -> 28.2 us  [call(): pl.pallas_call(body, in_specs=[place for _, place in operands], out_specs...]
  transfers between devices with their start and end apart: 15 -> 15, of which waited for: 1 -> 1; matrix products, arithmetic and copies ran while one was open for 0% -> 0% of each run, Pallas kernels for 47% -> 46%
where the time goes in v7:
time: 51.3 us; the launch traced here: 51.1 us
  Pallas kernels  28.2 us (55%)
  starting transfers between devices  17.6 us (34%)
  local copies, waits for them, and re-layouts  1.98 us (4%)
  waiting for transfers between devices  1.24 us (2%)
  between operations  1.04 us (2%)
  other arithmetic  0.84 us (2%)
    pallas_call x10, Pallas kernels, call(): pl.pallas_call(body, in_specs=[place for _, place in operands], out_specs...  28.2 us
    ppermute x15, starting transfers between devices, flip(): return lax.ppermute(value, axis, [(i, i ^ distance) for i in range(count)])  17.6 us
    unnamed x11, local copies, waits for them, and re-layouts  1.93 us
    ppermute x15, waiting for transfers between devices, flip(): return lax.ppermute(value, axis, [(i, i ^ distance) for i in range(count)])  1.24 us
  transfers between devices with their start and end apart: 15, of which 1 were waited for; matrix products, arithmetic and copies ran while one was open for 0% of the time, Pallas kernels for 46%

profile of v7, /device:TPU:1, one launch (start us, length us, event | category | flops | bytes accessed | tf_op | source)
XLA Modules:
  0.0 51.1 jit_solution(17642853492738398838)
XLA Ops:
  0.6 0.0 copy-start
  0.7 0.8 %add_subtract_fusion = s32[2080]{0:T(1024)S(1)} fusion(s32[32]{0:T(128)} %param.7, s32[2048]{0:T(1024)} %param.9, s32[]{:T(128)S(6)} %mul.11, s32[]{:T(128)S(6)} %mul.9), kind=kLoop, calls=%fused_computation.10 | loop fusion | flops 8320 | bytes 16648 | tf_op jit(solution)/shard_map/sub | solution.py:453
  1.4 0.1 copy-done
  1.5 0.2 convolution_convert_fusion.refs_0_
  1.7 2.2 %collective-permute-start = (bf16[32,1024]{1,0:T(8,128)(2,1)S(1)}, bf16[32,1024]{1,0:T(8,128)(2,1)S(1)}, u32[]{:S(2)}, u32[]{:S(2)}) collective-permute-start(bf16[32,1024]{1,0:T(8,128)(2,1)S(1)} %convolution_convert_fusion.refs_0_), channel_id=1, source_target_pairs={{0,2},{1,3},{2,0},{3,1},{4,6},{5,7},{6,4},{7,5},{8,10},{9,11},{10,... | collective-permute-start | bytes 196616 | tf_op jit(solution)/shard_map/ppermute | solution.py:16
  3.9 2.3 %collective-permute-start.1 = (bf16[32,1024]{1,0:T(8,128)(2,1)S(1)}, bf16[32,1024]{1,0:T(8,128)(2,1)S(1)}, u32[]{:S(2)}, u32[]{:S(2)}) collective-permute-start(bf16[32,1024]{1,0:T(8,128)(2,1)S(1)} %convolution_convert_fusion.refs_0_), channel_id=1, source_target_pairs={{0,4},{1,5},{2,6},{3,7},{4,0},{5,1},{6,2},{7,3},{8,12},{9,13},{10,... | collective-permute-start | bytes 196616 | tf_op jit(solution)/shard_map/ppermute | solution.py:16
  6.2 0.0 collective-permute-start.2
  6.2 0.0 copy-start.1
  6.2 1.7 %copy-done.1 = f32[2048,301]{0,1:T(8,128)S(1)} copy-done((f32[2048,301]{0,1:T(8,128)S(1)}, f32[2048,301]{0,1:T(8,128)}, u32[]{:S(2)}) %copy-start.1) | copy-done | bytes 2465816
  7.9 0.0 copy-start.2
  7.9 5.1 %shard_map.77 = (bf16[301,2432]{1,0:T(8,128)(2,1)S(1)}, f32[2432,128]{1,0:T(8,128)S(1)}, s16[2048,128]{1,0:T(8,128)(2,1)S(1)}, f32[301,2048]{1,0:T(8,128)S(1)}, bf16[2305,1024]{1,0:T(8,128)(2,1)S(1)}) custom-call(s32[1,2048]{1,0:T(1,128)S(1)} %bitcast.6, f32[301,2048]{1,0:T(8,128)S(1)} %bitcast.5, bf16[2305,1024]{1,0:T(8,128)(2,1)} %pool_far.1), custom_call_target="tpu_custom_call" | custom-call | flops 1024 | bytes 1024 | tf_op jit(solution)/shard_map/pallas_call | solution.py:45
  13.0 0.0 collective-permute-done.refs_1_
  13.0 0.0 collective-permute-done.1.refs_2_
  13.1 0.0 collective-permute-done.2.refs_3_
  13.1 0.0 copy-done.2
  13.1 0.2 shard_map.78
  13.2 1.3 %collective-permute-start.3 = (bf16[128,1024]{1,0:T(8,128)(2,1)S(1)}, bf16[128,1024]{1,0:T(8,128)(2,1)S(1)}, u32[]{:S(2)}, u32[]{:S(2)}) collective-permute-start(bf16[128,1024]{1,0:T(8,128)(2,1)S(1)} %get-tuple-element.53.side_ref), channel_id=1, source_target_pairs={{0,1},{1,0},{2,3},{3,2},{4,5},{5,4},{6,7},{7,6},{8,9},{9,8},{10,11... | collective-permute-start | bytes 786440 | tf_op jit(solution)/shard_map/ppermute | solution.py:16
  14.5 1.6 %shard_map.79 = (bf16[256,1024]{1,0:T(8,128)(2,1)S(1)}, f32[1,256]{1,0:T(1,128)S(1)}) custom-call(s16[2048,128]{1,0:T(8,128)(2,1)S(1)} %get-tuple-element.73.index_ref, bf16[2305,1024]{1,0:T(8,128)(2,1)S(1)} %get-tuple-element.56.pool_ref), custom_call_target="tpu_custom_call" | custom-call | flops 1024 | bytes 1024 | tf_op jit(solution)/shard_map/pallas_call | solution.py:45
  16.1 0.0 collective-permute-done.3.other_ref
  16.1 2.3 %shard_map.80 = (f32[301,128]{1,0:T(8,128)S(1)}, f32[301,128]{1,0:T(8,128)S(1)}) custom-call(bf16[128,1024]{1,0:T(8,128)(2,1)S(1)} %get-tuple-element.53.side_ref, bf16[128,1024]{1,0:T(8,128)(2,1)S(1)} %collective-permute-done.3.other_ref, bf16[2305,1024]{1,0:T(8,128)(2,1)S(1)} %get-tuple-element.56.pool_ref, f32[2432,128]{1,0:T(8,128)S(1)} %get-tuple-element.60.square_ref, ...), custom_call_target="tpu_custom_call" | custom-call | flops 1024 | bytes 1024 | tf_op jit(solution)/shard_map/pallas_call | solution.py:45
  18.4 0.1 collective-permute-start.4
  18.5 1.5 %shard_map.81 = (bf16[256,1024]{1,0:T(8,128)(2,1)S(1)}, f32[1,256]{1,0:T(1,128)S(1)}) custom-call(s16[2048,128]{1,0:T(8,128)(2,1)S(1)} %get-tuple-element.73.index_ref, bf16[2305,1024]{1,0:T(8,128)(2,1)S(1)} %get-tuple-element.56.pool_ref), custom_call_target="tpu_custom_call" | custom-call | flops 1024 | bytes 1024 | tf_op jit(solution)/shard_map/pallas_call | solution.py:45
  20.0 0.0 collective-permute-done.4
  20.1 0.7 %collective-permute-start.5 = (f32[301,128]{1,0:T(8,128)S(1)}, f32[301,128]{1,0:T(8,128)S(1)}, u32[]{:S(2)}, u32[]{:S(2)}) collective-permute-start(f32[301,128]{1,0:T(8,128)S(1)} %subtract_add_fusion), channel_id=1, source_target_pairs={{0,2},{1,3},{2,0},{3,1},{4,6},{5,7},{6,4},{7,5},{8,10},{9,11},{10,... | collective-permute-start | bytes 462344 | tf_op jit(solution)/shard_map/ppermute | solution.py:16
  20.8 1.2 %collective-permute-start.7 = (bf16[128,1024]{1,0:T(8,128)(2,1)S(1)}, bf16[128,1024]{1,0:T(8,128)(2,1)S(1)}, u32[]{:S(2)}, u32[]{:S(2)}) collective-permute-start(bf16[128,1024]{1,0:T(8,128)(2,1)S(1)} %get-tuple-element.53.side_ref), channel_id=1, source_target_pairs={{0,8},{8,0},{16,24},{24,16},{1,9},{9,1},{17,25},{25,17},{2,10},{10... | collective-permute-start | bytes 786440 | tf_op jit(solution)/shard_map/ppermute | solution.py:16
  22.0 1.2 %collective-permute-start.8 = (bf16[128,1024]{1,0:T(8,128)(2,1)S(1)}, bf16[128,1024]{1,0:T(8,128)(2,1)S(1)}, u32[]{:S(2)}, u32[]{:S(2)}) collective-permute-start(bf16[128,1024]{1,0:T(8,128)(2,1)S(1)} %get-tuple-element.53.side_ref), channel_id=1, source_target_pairs={{0,16},{8,24},{16,0},{24,8},{1,17},{9,25},{17,1},{25,9},{2,18},{10... | collective-permute-start | bytes 786440 | tf_op jit(solution)/shard_map/ppermute | solution.py:16
  23.2 0.2 collective-permute-start.9
  23.4 3.5 %shard_map.82 = (bf16[512,1024]{1,0:T(8,128)(2,1)S(1)}, f32[1,512]{1,0:T(1,128)S(1)}, bf16[256,1024]{1,0:T(8,128)(2,1)S(1)}) custom-call(s16[2048,128]{1,0:T(8,128)(2,1)S(1)} %get-tuple-element.73.index_ref, bf16[2305,1024]{1,0:T(8,128)(2,1)S(1)} %get-tuple-element.56.pool_ref, bf16[128,1024]{1,0:T(8,128)(2,1)S(1)} %get-tuple-element.53.side_ref, ...), custom_call_target="tpu_custom_call" | custom-call | flops 1024 | bytes 1024 | tf_op jit(solution)/shard_map/pallas_call | solution.py:45
  26.9 0.0 collective-permute-done.5
  27.0 3.3 %collective-permute-start.6 = (f32[301,128]{1,0:T(8,128)S(1)}, f32[301,128]{1,0:T(8,128)S(1)}, u32[]{:S(2)}, u32[]{:S(2)}) collective-permute-start(f32[301,128]{1,0:T(8,128)S(1)} %add.14), channel_id=1, source_target_pairs={{0,4},{1,5},{2,6},{3,7},{4,0},{5,1},{6,2},{7,3},{8,12},{9,13},{10,... | collective-permute-start | bytes 462344 | tf_op jit(solution)/shard_map/ppermute | solution.py:16
  30.2 6.2 %shard_map.83 = (bf16[1024,1024]{1,0:T(8,128)(2,1)S(1)}, f32[1,1024]{1,0:T(1,128)S(1)}, bf16[256,1024]{1,0:T(8,128)(2,1)S(1)}) custom-call(s16[2048,128]{1,0:T(8,128)(2,1)S(1)} %get-tuple-element.73.index_ref, bf16[2305,1024]{1,0:T(8,128)(2,1)S(1)} %get-tuple-element.56.pool_ref, bf16[128,1024]{1,0:T(8,128)(2,1)S(1)} %get-tuple-element.53.side_ref, ...), custom_call_target="tpu_custom_call" | custom-call | flops 1024 | bytes 1024 | tf_op jit(solution)/shard_map/pallas_call | solution.py:45
  36.4 1.2 %collective-permute-done.6 = f32[301,128]{1,0:T(8,128)S(1)} collective-permute-done((f32[301,128]{1,0:T(8,128)S(1)}, f32[301,128]{1,0:T(8,128)S(1)}, u32[]{:S(2)}, u32[]{:S(2)}) %collective-permute-start.6) | collective-permute-done | bytes 154144 | tf_op jit(solution)/shard_map/ppermute | solution.py:16
  37.6 0.0 collective-permute-done.7
  37.6 0.0 collective-permute-done.8
  37.6 0.0 collective-permute-done.9
  37.7 0.8 %collective-permute-start.10 = (bf16[384,1024]{1,0:T(8,128)(2,1)S(1)}, bf16[384,1024]{1,0:T(8,128)(2,1)S(1)}, u32[]{:S(2)}, u32[]{:S(2)}) collective-permute-start(bf16[384,1024]{1,0:T(8,128)(2,1)S(1)} %constant_dynamic-update-slice_fusion.refs_0_), channel_id=1, source_target_pairs={{0,1},{1,0},{2,3},{3,2},{4,5},{5,4},{6,7},{7,6},{8,9},{9,8},{10,11... | collective-permute-start | bytes 2359304 | tf_op jit(solution)/shard_map/ppermute | solution.py:16
  38.5 1.4 %collective-permute-start.11 = (bf16[301,128]{1,0:T(8,128)(2,1)S(1)}, bf16[301,128]{1,0:T(8,128)(2,1)S(1)}, u32[]{:S(2)}, u32[]{:S(2)}) collective-permute-start(bf16[301,128]{1,0:T(8,128)(2,1)S(1)} %convert_element_type.8), channel_id=1, source_target_pairs={{0,8},{8,0},{16,24},{24,16},{1,9},{9,1},{17,25},{25,17},{2,10},{10... | collective-permute-start | bytes 231176 | tf_op jit(solution)/shard_map/ppermute | solution.py:16
  40.0 1.2 %collective-permute-start.12 = (bf16[301,128]{1,0:T(8,128)(2,1)S(1)}, bf16[301,128]{1,0:T(8,128)(2,1)S(1)}, u32[]{:S(2)}, u32[]{:S(2)}) collective-permute-start(bf16[301,128]{1,0:T(8,128)(2,1)S(1)} %convert_element_type.8), channel_id=1, source_target_pairs={{0,16},{8,24},{16,0},{24,8},{1,17},{9,25},{17,1},{25,9},{2,18},{10... | collective-permute-start | bytes 231176 | tf_op jit(solution)/shard_map/ppermute | solution.py:16
  41.2 0.0 collective-permute-start.13
  41.3 0.0 collective-permute-done.10.refs_1_
  41.3 4.3 %shard_map.84.refs_2_ = bf16[768,2048]{1,0:T(8,128)(2,1)S(1)} custom-call(bf16[384,1024]{1,0:T(8,128)(2,1)S(1)} %constant_dynamic-update-slice_fusion.refs_0_, bf16[384,1024]{1,0:T(8,128)(2,1)S(1)} %collective-permute-done.10.refs_1_, bf16[256,1024]{1,0:T(8,128)(2,1)S(1)} %get-tuple-element.57.refs_0_.refs_2_, ...), custom_call_target="tpu_custom_call" | custom-call | flops 1024 | bytes 1024 | tf_op jit(solution)/shard_map/pallas_call | solution.py:45
  45.5 0.0 collective-permute-done.11
  45.5 0.0 collective-permute-done.12
  45.6 0.0 collective-permute-done.13
  45.7 1.6 %collective-permute-start.14 = (bf16[301,512]{1,0:T(8,128)(2,1)S(1)}, bf16[301,512]{1,0:T(8,128)(2,1)S(1)}, u32[]{:S(2)}, u32[]{:S(2)}) collective-permute-start(bf16[301,512]{1,0:T(8,128)(2,1)S(1)} %constant_dynamic-update-slice_fusion.3.residual_ref), channel_id=1, source_target_pairs={{0,1},{1,0},{2,3},{3,2},{4,5},{5,4},{6,7},{7,6},{8,9},{9,8},{10,11... | collective-permute-start | bytes 924680 | tf_op jit(solution)/shard_map/ppermute | solution.py:16
  47.3 1.6 %shard_map.85 = (f32[301,2048]{1,0:T(8,128)S(1)}, f32[32,301]{1,0:T(8,128)}) custom-call(s32[1]{0:T(128)} %bitcast.1.place_ref, f32[301,128]{1,0:T(8,128)S(1)} %add.15.total_ref, bf16[301,512]{1,0:T(8,128)(2,1)S(1)} %constant_dynamic-update-slice_fusion.3.residual_ref, f32[301,2048]{1,0:T(8,128)S(1)} %get-tuple-element.84.base_ref, ...), custom_call_target="tpu_custom_call" | custom-call | flops 1024 | bytes 1024 | tf_op jit(solution)/shard_map/pallas_call | solution.py:45
  48.9 0.0 collective-permute-done.14.residual_ref
  48.9 2.0 %shard_map.86 = f32[301,2048]{1,0:T(8,128)} custom-call(bf16[301,512]{1,0:T(8,128)(2,1)S(1)} %collective-permute-done.14.residual_ref, f32[301,2048]{1,0:T(8,128)S(1)} %get-tuple-element.88.base_ref, bf16[256,1024]{1,0:T(8,128)(2,1)S(1)} %get-tuple-element.85.refs_0_, bf16[256,1024]{1,0:T(8,128)(2,1)S(1)} %get-tuple-element.86.refs_1_, ...), custom_call_target="tpu_custom_call" | custom-call | flops 1024 | bytes 1024 | tf_op jit(solution)/shard_map/pallas_call | solution.py:45
  (13 shorter events, 0.2 us)
Async XLA Ops:
  0.6 0.9 %copy-start = (bf16[41,1024]{1,0:T(8,128)(2,1)S(1)}, bf16[41,1024]{1,0:T(8,128)(2,1)}, u32[]{:S(2)}) copy-start(bf16[41,1024]{1,0:T(8,128)(2,1)} %param.6) | copy-start | bytes 251908
  1.7 11.3 %collective-permute-start = (bf16[32,1024]{1,0:T(8,128)(2,1)S(1)}, bf16[32,1024]{1,0:T(8,128)(2,1)S(1)}, u32[]{:S(2)}, u32[]{:S(2)}) collective-permute-start(bf16[32,1024]{1,0:T(8,128)(2,1)S(1)} %convolution_convert_fusion.refs_0_), channel_id=1, source_target_pairs={{0,2},{1,3},{2,0},{3,1},{4,6},{5,7},{6,4},{7,5},{8,10},{9,11},{10,... | collective-permute-start | bytes 196616 | tf_op jit(solution)/shard_map/ppermute | solution.py:16
  3.9 9.1 %collective-permute-start.1 = (bf16[32,1024]{1,0:T(8,128)(2,1)S(1)}, bf16[32,1024]{1,0:T(8,128)(2,1)S(1)}, u32[]{:S(2)}, u32[]{:S(2)}) collective-permute-start(bf16[32,1024]{1,0:T(8,128)(2,1)S(1)} %convolution_convert_fusion.refs_0_), channel_id=1, source_target_pairs={{0,4},{1,5},{2,6},{3,7},{4,0},{5,1},{6,2},{7,3},{8,12},{9,13},{10,... | collective-permute-start | bytes 196616 | tf_op jit(solution)/shard_map/ppermute | solution.py:16
  6.2 6.8 %collective-permute-start.2 = (bf16[32,1024]{1,0:T(8,128)(2,1)S(1)}, bf16[32,1024]{1,0:T(8,128)(2,1)S(1)}, u32[]{:S(2)}, u32[]{:S(2)}) collective-permute-start(bf16[32,1024]{1,0:T(8,128)(2,1)S(1)} %convolution_convert_fusion.refs_0_), channel_id=1, source_target_pairs={{0,6},{1,7},{2,4},{3,5},{4,2},{5,3},{6,0},{7,1},{8,14},{9,15},{10,... | collective-permute-start | bytes 196616 | tf_op jit(solution)/shard_map/ppermute | solution.py:16
  6.2 1.7 %copy-start.1 = (f32[2048,301]{0,1:T(8,128)S(1)}, f32[2048,301]{0,1:T(8,128)}, u32[]{:S(2)}) copy-start(f32[2048,301]{0,1:T(8,128)} %param.11) | copy-start | bytes 7397380
  7.9 5.1 %copy-start.2 = (f32[32,301]{1,0:T(8,128)S(1)}, f32[32,301]{1,0:T(8,128)}, u32[]{:S(2)}) copy-start(f32[32,301]{1,0:T(8,128)} %targets_ref.1) | copy-start | bytes 115588
  13.2 2.9 %collective-permute-start.3 = (bf16[128,1024]{1,0:T(8,128)(2,1)S(1)}, bf16[128,1024]{1,0:T(8,128)(2,1)S(1)}, u32[]{:S(2)}, u32[]{:S(2)}) collective-permute-start(bf16[128,1024]{1,0:T(8,128)(2,1)S(1)} %get-tuple-element.53.side_ref), channel_id=1, source_target_pairs={{0,1},{1,0},{2,3},{3,2},{4,5},{5,4},{6,7},{7,6},{8,9},{9,8},{10,11... | collective-permute-start | bytes 786440 | tf_op jit(solution)/shard_map/ppermute | solution.py:16
  18.4 1.6 %collective-permute-start.4 = (f32[301,128]{1,0:T(8,128)S(1)}, f32[301,128]{1,0:T(8,128)S(1)}, u32[]{:S(2)}, u32[]{:S(2)}) collective-permute-start(f32[301,128]{1,0:T(8,128)S(1)} %get-tuple-element.64), channel_id=1, source_target_pairs={{0,1},{1,0},{2,3},{3,2},{4,5},{5,4},{6,7},{7,6},{8,9},{9,8},{10,11... | collective-permute-start | bytes 462344 | tf_op jit(solution)/shard_map/ppermute | solution.py:16
  20.1 6.8 %collective-permute-start.5 = (f32[301,128]{1,0:T(8,128)S(1)}, f32[301,128]{1,0:T(8,128)S(1)}, u32[]{:S(2)}, u32[]{:S(2)}) collective-permute-start(f32[301,128]{1,0:T(8,128)S(1)} %subtract_add_fusion), channel_id=1, source_target_pairs={{0,2},{1,3},{2,0},{3,1},{4,6},{5,7},{6,4},{7,5},{8,10},{9,11},{10,... | collective-permute-start | bytes 462344 | tf_op jit(solution)/shard_map/ppermute | solution.py:16
  20.8 16.8 %collective-permute-start.7 = (bf16[128,1024]{1,0:T(8,128)(2,1)S(1)}, bf16[128,1024]{1,0:T(8,128)(2,1)S(1)}, u32[]{:S(2)}, u32[]{:S(2)}) collective-permute-start(bf16[128,1024]{1,0:T(8,128)(2,1)S(1)} %get-tuple-element.53.side_ref), channel_id=1, source_target_pairs={{0,8},{8,0},{16,24},{24,16},{1,9},{9,1},{17,25},{25,17},{2,10},{10... | collective-permute-start | bytes 786440 | tf_op jit(solution)/shard_map/ppermute | solution.py:16
  22.0 15.7 %collective-permute-start.8 = (bf16[128,1024]{1,0:T(8,128)(2,1)S(1)}, bf16[128,1024]{1,0:T(8,128)(2,1)S(1)}, u32[]{:S(2)}, u32[]{:S(2)}) collective-permute-start(bf16[128,1024]{1,0:T(8,128)(2,1)S(1)} %get-tuple-element.53.side_ref), channel_id=1, source_target_pairs={{0,16},{8,24},{16,0},{24,8},{1,17},{9,25},{17,1},{25,9},{2,18},{10... | collective-permute-start | bytes 786440 | tf_op jit(solution)/shard_map/ppermute | solution.py:16
  23.2 14.4 %collective-permute-start.9 = (bf16[128,1024]{1,0:T(8,128)(2,1)S(1)}, bf16[128,1024]{1,0:T(8,128)(2,1)S(1)}, u32[]{:S(2)}, u32[]{:S(2)}) collective-permute-start(bf16[128,1024]{1,0:T(8,128)(2,1)S(1)} %get-tuple-element.53.side_ref), channel_id=1, source_target_pairs={{0,24},{8,16},{16,8},{24,0},{1,25},{9,17},{17,9},{25,1},{2,26},{10... | collective-permute-start | bytes 786440 | tf_op jit(solution)/shard_map/ppermute | solution.py:16
  27.0 10.6 %collective-permute-start.6 = (f32[301,128]{1,0:T(8,128)S(1)}, f32[301,128]{1,0:T(8,128)S(1)}, u32[]{:S(2)}, u32[]{:S(2)}) collective-permute-start(f32[301,128]{1,0:T(8,128)S(1)} %add.14), channel_id=1, source_target_pairs={{0,4},{1,5},{2,6},{3,7},{4,0},{5,1},{6,2},{7,3},{8,12},{9,13},{10,... | collective-permute-start | bytes 462344 | tf_op jit(solution)/shard_map/ppermute | solution.py:16
  37.7 3.5 %collective-permute-start.10 = (bf16[384,1024]{1,0:T(8,128)(2,1)S(1)}, bf16[384,1024]{1,0:T(8,128)(2,1)S(1)}, u32[]{:S(2)}, u32[]{:S(2)}) collective-permute-start(bf16[384,1024]{1,0:T(8,128)(2,1)S(1)} %constant_dynamic-update-slice_fusion.refs_0_), channel_id=1, source_target_pairs={{0,1},{1,0},{2,3},{3,2},{4,5},{5,4},{6,7},{7,6},{8,9},{9,8},{10,11... | collective-permute-start | bytes 2359304 | tf_op jit(solution)/shard_map/ppermute | solution.py:16
  38.5 7.0 %collective-permute-start.11 = (bf16[301,128]{1,0:T(8,128)(2,1)S(1)}, bf16[301,128]{1,0:T(8,128)(2,1)S(1)}, u32[]{:S(2)}, u32[]{:S(2)}) collective-permute-start(bf16[301,128]{1,0:T(8,128)(2,1)S(1)} %convert_element_type.8), channel_id=1, source_target_pairs={{0,8},{8,0},{16,24},{24,16},{1,9},{9,1},{17,25},{25,17},{2,10},{10... | collective-permute-start | bytes 231176 | tf_op jit(solution)/shard_map/ppermute | solution.py:16
  40.0 5.6 %collective-permute-start.12 = (bf16[301,128]{1,0:T(8,128)(2,1)S(1)}, bf16[301,128]{1,0:T(8,128)(2,1)S(1)}, u32[]{:S(2)}, u32[]{:S(2)}) collective-permute-start(bf16[301,128]{1,0:T(8,128)(2,1)S(1)} %convert_element_type.8), channel_id=1, source_target_pairs={{0,16},{8,24},{16,0},{24,8},{1,17},{9,25},{17,1},{25,9},{2,18},{10... | collective-permute-start | bytes 231176 | tf_op jit(solution)/shard_map/ppermute | solution.py:16
  41.2 4.3 %collective-permute-start.13 = (bf16[301,128]{1,0:T(8,128)(2,1)S(1)}, bf16[301,128]{1,0:T(8,128)(2,1)S(1)}, u32[]{:S(2)}, u32[]{:S(2)}) collective-permute-start(bf16[301,128]{1,0:T(8,128)(2,1)S(1)} %convert_element_type.8), channel_id=1, source_target_pairs={{0,24},{8,16},{16,8},{24,0},{1,25},{9,17},{17,9},{25,1},{2,26},{10... | collective-permute-start | bytes 231176 | tf_op jit(solution)/shard_map/ppermute | solution.py:16
  45.7 3.2 %collective-permute-start.14 = (bf16[301,512]{1,0:T(8,128)(2,1)S(1)}, bf16[301,512]{1,0:T(8,128)(2,1)S(1)}, u32[]{:S(2)}, u32[]{:S(2)}) collective-permute-start(bf16[301,512]{1,0:T(8,128)(2,1)S(1)} %constant_dynamic-update-slice_fusion.3.residual_ref), channel_id=1, source_target_pairs={{0,1},{1,0},{2,3},{3,2},{4,5},{5,4},{6,7},{7,6},{8,9},{9,8},{10,11... | collective-permute-start | bytes 924680 | tf_op jit(solution)/shard_map/ppermute | solution.py:16

commit v8 on v7

--- a/solution.py
+++ b/solution.py
@@ -491,7 +491,12 @@
                 after(index, total), pool, side, other, before, at, size
             )
             picked, kernels, at = [*picked, pair], [*kernels, kernel], at + size
-        total = after(total + flip(total, "centre", distance), *picked[-1])
+        if 2 * distance == centre_size:
+            half = total.astype(jnp.bfloat16)
+            summed = half.astype(jnp.float32) + flip(half, "centre", distance).astype(jnp.float32)
+        else:
+            summed = total + flip(total, "centre", distance)
+        total = after(summed, *picked[-1])
         distance *= 2
     if hold_all:
         foreign = lax.optimization_barrier((total, *foreign))[1:]

time: 51.3 us -> 55.8 us (1.088)
  waiting for transfers between devices: 1.24 us -> 5.26 us
    ppermute x15, waiting for transfers between devices: 1.24 us -> 5.26 us  [flip(): return lax.ppermute(value, axis, [(i, i ^ distance) for i in range(count)])]
  transfers between devices with their start and end apart: 15 -> 15, of which waited for: 1 -> 2; matrix products, arithmetic and copies ran while one was open for 0% -> 0% of each run, Pallas kernels for 46% -> 43%
where the time goes in v8:
time: 55.8 us; the launch traced here: 55.6 us
  Pallas kernels  28.2 us (51%)
  starting transfers between devices  18.1 us (32%)
  waiting for transfers between devices  5.26 us (9%)
  local copies, waits for them, and re-layouts  1.98 us (4%)
  between operations  1.03 us (2%)
  other arithmetic  0.84 us (2%)
    pallas_call x10, Pallas kernels, call(): pl.pallas_call(body, in_specs=[place for _, place in operands], out_specs...  28.2 us
    ppermute x15, starting transfers between devices, flip(): return lax.ppermute(value, axis, [(i, i ^ distance) for i in range(count)])  18.1 us
    ppermute x15, waiting for transfers between devices, flip(): return lax.ppermute(value, axis, [(i, i ^ distance) for i in range(count)])  5.26 us
    unnamed x11, local copies, waits for them, and re-layouts  1.93 us
  transfers between devices with their start and end apart: 15, of which 2 were waited for; matrix products, arithmetic and copies ran while one was open for 0% of the time, Pallas kernels for 43%

profile of v8, /device:TPU:1, one launch (start us, length us, event | category | flops | bytes accessed | tf_op | source)
XLA Modules:
  0.0 55.6 jit_solution(17994239786948414800)
XLA Ops:
  0.6 0.0 copy-start
  0.7 0.8 %add_subtract_fusion = s32[2080]{0:T(1024)S(1)} fusion(s32[32]{0:T(128)} %param.7, s32[2048]{0:T(1024)} %param.9, s32[]{:T(128)S(6)} %mul.11, s32[]{:T(128)S(6)} %mul.9), kind=kLoop, calls=%fused_computation.11 | loop fusion | flops 8320 | bytes 16648 | tf_op jit(solution)/shard_map/sub | solution.py:453
  1.4 0.1 copy-done
  1.5 0.2 convolution_convert_fusion.refs_0_
  1.7 2.2 %collective-permute-start = (bf16[32,1024]{1,0:T(8,128)(2,1)S(1)}, bf16[32,1024]{1,0:T(8,128)(2,1)S(1)}, u32[]{:S(2)}, u32[]{:S(2)}) collective-permute-start(bf16[32,1024]{1,0:T(8,128)(2,1)S(1)} %convolution_convert_fusion.refs_0_), channel_id=1, source_target_pairs={{0,2},{1,3},{2,0},{3,1},{4,6},{5,7},{6,4},{7,5},{8,10},{9,11},{10,... | collective-permute-start | bytes 196616 | tf_op jit(solution)/shard_map/ppermute | solution.py:16
  3.9 2.3 %collective-permute-start.1 = (bf16[32,1024]{1,0:T(8,128)(2,1)S(1)}, bf16[32,1024]{1,0:T(8,128)(2,1)S(1)}, u32[]{:S(2)}, u32[]{:S(2)}) collective-permute-start(bf16[32,1024]{1,0:T(8,128)(2,1)S(1)} %convolution_convert_fusion.refs_0_), channel_id=1, source_target_pairs={{0,4},{1,5},{2,6},{3,7},{4,0},{5,1},{6,2},{7,3},{8,12},{9,13},{10,... | collective-permute-start | bytes 196616 | tf_op jit(solution)/shard_map/ppermute | solution.py:16
  6.2 0.0 collective-permute-start.2
  6.2 0.0 copy-start.1
  6.2 1.7 %copy-done.1 = f32[2048,301]{0,1:T(8,128)S(1)} copy-done((f32[2048,301]{0,1:T(8,128)S(1)}, f32[2048,301]{0,1:T(8,128)}, u32[]{:S(2)}) %copy-start.1) | copy-done | bytes 2465816
  7.9 0.0 copy-start.2
  7.9 5.1 %shard_map.77 = (bf16[301,2432]{1,0:T(8,128)(2,1)S(1)}, f32[2432,128]{1,0:T(8,128)S(1)}, s16[2048,128]{1,0:T(8,128)(2,1)S(1)}, f32[301,2048]{1,0:T(8,128)S(1)}, bf16[2305,1024]{1,0:T(8,128)(2,1)S(1)}) custom-call(s32[1,2048]{1,0:T(1,128)S(1)} %bitcast.6, f32[301,2048]{1,0:T(8,128)S(1)} %bitcast.5, bf16[2305,1024]{1,0:T(8,128)(2,1)} %pool_far.1), custom_call_target="tpu_custom_call" | custom-call | flops 1024 | bytes 1024 | tf_op jit(solution)/shard_map/pallas_call | solution.py:45
  13.0 0.0 collective-permute-done.refs_1_
  13.0 0.0 collective-permute-done.1.refs_2_
  13.1 0.0 collective-permute-done.2.refs_3_
  13.1 0.0 copy-done.2
  13.1 0.2 shard_map.78
  13.2 1.3 %collective-permute-start.3 = (bf16[128,1024]{1,0:T(8,128)(2,1)S(1)}, bf16[128,1024]{1,0:T(8,128)(2,1)S(1)}, u32[]{:S(2)}, u32[]{:S(2)}) collective-permute-start(bf16[128,1024]{1,0:T(8,128)(2,1)S(1)} %get-tuple-element.53.side_ref), channel_id=1, source_target_pairs={{0,1},{1,0},{2,3},{3,2},{4,5},{5,4},{6,7},{7,6},{8,9},{9,8},{10,11... | collective-permute-start | bytes 786440 | tf_op jit(solution)/shard_map/ppermute | solution.py:16
  14.5 1.6 %shard_map.79 = (bf16[256,1024]{1,0:T(8,128)(2,1)S(1)}, f32[1,256]{1,0:T(1,128)S(1)}) custom-call(s16[2048,128]{1,0:T(8,128)(2,1)S(1)} %get-tuple-element.73.index_ref, bf16[2305,1024]{1,0:T(8,128)(2,1)S(1)} %get-tuple-element.56.pool_ref), custom_call_target="tpu_custom_call" | custom-call | flops 1024 | bytes 1024 | tf_op jit(solution)/shard_map/pallas_call | solution.py:45
  16.1 0.0 collective-permute-done.3.other_ref
  16.1 2.3 %shard_map.80 = (f32[301,128]{1,0:T(8,128)S(1)}, f32[301,128]{1,0:T(8,128)S(1)}) custom-call(bf16[128,1024]{1,0:T(8,128)(2,1)S(1)} %get-tuple-element.53.side_ref, bf16[128,1024]{1,0:T(8,128)(2,1)S(1)} %collective-permute-done.3.other_ref, bf16[2305,1024]{1,0:T(8,128)(2,1)S(1)} %get-tuple-element.56.pool_ref, f32[2432,128]{1,0:T(8,128)S(1)} %get-tuple-element.60.square_ref, ...), custom_call_target="tpu_custom_call" | custom-call | flops 1024 | bytes 1024 | tf_op jit(solution)/shard_map/pallas_call | solution.py:45
  18.4 0.1 collective-permute-start.4
  18.5 1.5 %shard_map.81 = (bf16[256,1024]{1,0:T(8,128)(2,1)S(1)}, f32[1,256]{1,0:T(1,128)S(1)}) custom-call(s16[2048,128]{1,0:T(8,128)(2,1)S(1)} %get-tuple-element.73.index_ref, bf16[2305,1024]{1,0:T(8,128)(2,1)S(1)} %get-tuple-element.56.pool_ref), custom_call_target="tpu_custom_call" | custom-call | flops 1024 | bytes 1024 | tf_op jit(solution)/shard_map/pallas_call | solution.py:45
  20.0 0.0 collective-permute-done.4
  20.1 0.7 %collective-permute-start.5 = (f32[301,128]{1,0:T(8,128)S(1)}, f32[301,128]{1,0:T(8,128)S(1)}, u32[]{:S(2)}, u32[]{:S(2)}) collective-permute-start(f32[301,128]{1,0:T(8,128)S(1)} %subtract_add_fusion), channel_id=1, source_target_pairs={{0,2},{1,3},{2,0},{3,1},{4,6},{5,7},{6,4},{7,5},{8,10},{9,11},{10,... | collective-permute-start | bytes 462344 | tf_op jit(solution)/shard_map/ppermute | solution.py:16
  20.8 3.5 %shard_map.82 = (bf16[512,1024]{1,0:T(8,128)(2,1)S(1)}, f32[1,512]{1,0:T(1,128)S(1)}, bf16[256,1024]{1,0:T(8,128)(2,1)S(1)}) custom-call(s16[2048,128]{1,0:T(8,128)(2,1)S(1)} %get-tuple-element.73.index_ref, bf16[2305,1024]{1,0:T(8,128)(2,1)S(1)} %get-tuple-element.56.pool_ref, bf16[128,1024]{1,0:T(8,128)(2,1)S(1)} %get-tuple-element.53.side_ref, ...), custom_call_target="tpu_custom_call" | custom-call | flops 1024 | bytes 1024 | tf_op jit(solution)/shard_map/pallas_call | solution.py:45
  24.3 1.0 %collective-permute-done.5 = f32[301,128]{1,0:T(8,128)S(1)} collective-permute-done((f32[301,128]{1,0:T(8,128)S(1)}, f32[301,128]{1,0:T(8,128)S(1)}, u32[]{:S(2)}, u32[]{:S(2)}) %collective-permute-start.5) | collective-permute-done | bytes 154144 | tf_op jit(solution)/shard_map/ppermute | solution.py:16
  25.3 2.7 %collective-permute-start.6 = (bf16[301,128]{1,0:T(8,128)(2,1)S(1)}, bf16[301,128]{1,0:T(8,128)(2,1)S(1)}, u32[]{:S(2)}, u32[]{:S(2)}) collective-permute-start(bf16[301,128]{1,0:T(8,128)(2,1)S(1)} %add.14), channel_id=1, source_target_pairs={{0,4},{1,5},{2,6},{3,7},{4,0},{5,1},{6,2},{7,3},{8,12},{9,13},{10,... | collective-permute-start | bytes 231176 | tf_op jit(solution)/shard_map/ppermute | solution.py:16
  28.0 1.2 %collective-permute-start.7 = (bf16[128,1024]{1,0:T(8,128)(2,1)S(1)}, bf16[128,1024]{1,0:T(8,128)(2,1)S(1)}, u32[]{:S(2)}, u32[]{:S(2)}) collective-permute-start(bf16[128,1024]{1,0:T(8,128)(2,1)S(1)} %get-tuple-element.53.side_ref), channel_id=1, source_target_pairs={{0,8},{8,0},{16,24},{24,16},{1,9},{9,1},{17,25},{25,17},{2,10},{10... | collective-permute-start | bytes 786440 | tf_op jit(solution)/shard_map/ppermute | solution.py:16
  29.2 1.3 %collective-permute-start.8 = (bf16[128,1024]{1,0:T(8,128)(2,1)S(1)}, bf16[128,1024]{1,0:T(8,128)(2,1)S(1)}, u32[]{:S(2)}, u32[]{:S(2)}) collective-permute-start(bf16[128,1024]{1,0:T(8,128)(2,1)S(1)} %get-tuple-element.53.side_ref), channel_id=1, source_target_pairs={{0,16},{8,24},{16,0},{24,8},{1,17},{9,25},{17,1},{25,9},{2,18},{10... | collective-permute-start | bytes 786440 | tf_op jit(solution)/shard_map/ppermute | solution.py:16
  30.5 0.2 collective-permute-start.9
  30.7 6.2 %shard_map.83 = (bf16[1024,1024]{1,0:T(8,128)(2,1)S(1)}, f32[1,1024]{1,0:T(1,128)S(1)}, bf16[256,1024]{1,0:T(8,128)(2,1)S(1)}) custom-call(s16[2048,128]{1,0:T(8,128)(2,1)S(1)} %get-tuple-element.73.index_ref, bf16[2305,1024]{1,0:T(8,128)(2,1)S(1)} %get-tuple-element.56.pool_ref, bf16[128,1024]{1,0:T(8,128)(2,1)S(1)} %get-tuple-element.53.side_ref, ...), custom_call_target="tpu_custom_call" | custom-call | flops 1024 | bytes 1024 | tf_op jit(solution)/shard_map/pallas_call | solution.py:45
  36.8 0.0 collective-permute-done.6
  36.9 0.0 collective-permute-done.7
  36.9 0.0 collective-permute-done.8
  36.9 4.2 %collective-permute-done.9 = bf16[128,1024]{1,0:T(8,128)(2,1)S(1)} collective-permute-done((bf16[128,1024]{1,0:T(8,128)(2,1)S(1)}, bf16[128,1024]{1,0:T(8,128)(2,1)S(1)}, u32[]{:S(2)}, u32[]{:S(2)}) %collective-permute-start.9) | collective-permute-done | bytes 262176 | tf_op jit(solution)/shard_map/ppermute | solution.py:16
  41.2 2.5 %collective-permute-start.10 = (bf16[384,1024]{1,0:T(8,128)(2,1)S(1)}, bf16[384,1024]{1,0:T(8,128)(2,1)S(1)}, u32[]{:S(2)}, u32[]{:S(2)}) collective-permute-start(bf16[384,1024]{1,0:T(8,128)(2,1)S(1)} %constant_dynamic-update-slice_fusion.refs_0_), channel_id=1, source_target_pairs={{0,1},{1,0},{2,3},{3,2},{4,5},{5,4},{6,7},{7,6},{8,9},{9,8},{10,11... | collective-permute-start | bytes 2359304 | tf_op jit(solution)/shard_map/ppermute | solution.py:16
  43.7 1.0 %collective-permute-start.11 = (bf16[301,128]{1,0:T(8,128)(2,1)S(1)}, bf16[301,128]{1,0:T(8,128)(2,1)S(1)}, u32[]{:S(2)}, u32[]{:S(2)}) collective-permute-start(bf16[301,128]{1,0:T(8,128)(2,1)S(1)} %convert_element_type.20), channel_id=1, source_target_pairs={{0,8},{8,0},{16,24},{24,16},{1,9},{9,1},{17,25},{25,17},{2,10},{10... | collective-permute-start | bytes 231176 | tf_op jit(solution)/shard_map/ppermute | solution.py:16
  44.8 0.5 collective-permute-start.12
  45.3 1.1 %collective-permute-start.13 = (bf16[301,128]{1,0:T(8,128)(2,1)S(1)}, bf16[301,128]{1,0:T(8,128)(2,1)S(1)}, u32[]{:S(2)}, u32[]{:S(2)}) collective-permute-start(bf16[301,128]{1,0:T(8,128)(2,1)S(1)} %convert_element_type.20), channel_id=1, source_target_pairs={{0,24},{8,16},{16,8},{24,0},{1,25},{9,17},{17,9},{25,1},{2,26},{10... | collective-permute-start | bytes 231176 | tf_op jit(solution)/shard_map/ppermute | solution.py:16
  46.4 0.0 collective-permute-done.10.refs_1_
  46.4 4.2 %shard_map.84.refs_2_ = bf16[768,2048]{1,0:T(8,128)(2,1)S(1)} custom-call(bf16[384,1024]{1,0:T(8,128)(2,1)S(1)} %constant_dynamic-update-slice_fusion.refs_0_, bf16[384,1024]{1,0:T(8,128)(2,1)S(1)} %collective-permute-done.10.refs_1_, bf16[256,1024]{1,0:T(8,128)(2,1)S(1)} %get-tuple-element.57.refs_0_.refs_2_, ...), custom_call_target="tpu_custom_call" | custom-call | flops 1024 | bytes 1024 | tf_op jit(solution)/shard_map/pallas_call | solution.py:45
  50.7 0.0 collective-permute-done.11
  50.7 0.0 collective-permute-done.12
  50.7 0.0 collective-permute-done.13
  50.8 0.9 %collective-permute-start.14 = (bf16[301,512]{1,0:T(8,128)(2,1)S(1)}, bf16[301,512]{1,0:T(8,128)(2,1)S(1)}, u32[]{:S(2)}, u32[]{:S(2)}) collective-permute-start(bf16[301,512]{1,0:T(8,128)(2,1)S(1)} %constant_dynamic-update-slice_fusion.3.residual_ref), channel_id=1, source_target_pairs={{0,1},{1,0},{2,3},{3,2},{4,5},{5,4},{6,7},{7,6},{8,9},{9,8},{10,11... | collective-permute-start | bytes 924680 | tf_op jit(solution)/shard_map/ppermute | solution.py:16
  51.8 1.6 %shard_map.85 = (f32[301,2048]{1,0:T(8,128)S(1)}, f32[32,301]{1,0:T(8,128)}) custom-call(s32[1]{0:T(128)} %bitcast.1.place_ref, f32[301,128]{1,0:T(8,128)S(1)} %convert_add_fusion.total_ref, bf16[301,512]{1,0:T(8,128)(2,1)S(1)} %constant_dynamic-update-slice_fusion.3.residual_ref, f32[301,2048]{1,0:T(8,128)S(1)} %get-tuple-element.84.base_ref, ...), custom_call_target="tpu_custom_call" | custom-call | flops 1024 | bytes 1024 | tf_op jit(solution)/shard_map/pallas_call | solution.py:45
  53.4 0.0 collective-permute-done.14.residual_ref
  53.4 2.0 %shard_map.86 = f32[301,2048]{1,0:T(8,128)} custom-call(bf16[301,512]{1,0:T(8,128)(2,1)S(1)} %collective-permute-done.14.residual_ref, f32[301,2048]{1,0:T(8,128)S(1)} %get-tuple-element.88.base_ref, bf16[256,1024]{1,0:T(8,128)(2,1)S(1)} %get-tuple-element.85.refs_0_, bf16[256,1024]{1,0:T(8,128)(2,1)S(1)} %get-tuple-element.86.refs_1_, ...), custom_call_target="tpu_custom_call" | custom-call | flops 1024 | bytes 1024 | tf_op jit(solution)/shard_map/pallas_call | solution.py:45
  (13 shorter events, 0.2 us)
Async XLA Ops:
  0.6 0.9 %copy-start = (bf16[41,1024]{1,0:T(8,128)(2,1)S(1)}, bf16[41,1024]{1,0:T(8,128)(2,1)}, u32[]{:S(2)}) copy-start(bf16[41,1024]{1,0:T(8,128)(2,1)} %param.6) | copy-start | bytes 251908
  1.7 11.3 %collective-permute-start = (bf16[32,1024]{1,0:T(8,128)(2,1)S(1)}, bf16[32,1024]{1,0:T(8,128)(2,1)S(1)}, u32[]{:S(2)}, u32[]{:S(2)}) collective-permute-start(bf16[32,1024]{1,0:T(8,128)(2,1)S(1)} %convolution_convert_fusion.refs_0_), channel_id=1, source_target_pairs={{0,2},{1,3},{2,0},{3,1},{4,6},{5,7},{6,4},{7,5},{8,10},{9,11},{10,... | collective-permute-start | bytes 196616 | tf_op jit(solution)/shard_map/ppermute | solution.py:16
  3.9 9.1 %collective-permute-start.1 = (bf16[32,1024]{1,0:T(8,128)(2,1)S(1)}, bf16[32,1024]{1,0:T(8,128)(2,1)S(1)}, u32[]{:S(2)}, u32[]{:S(2)}) collective-permute-start(bf16[32,1024]{1,0:T(8,128)(2,1)S(1)} %convolution_convert_fusion.refs_0_), channel_id=1, source_target_pairs={{0,4},{1,5},{2,6},{3,7},{4,0},{5,1},{6,2},{7,3},{8,12},{9,13},{10,... | collective-permute-start | bytes 196616 | tf_op jit(solution)/shard_map/ppermute | solution.py:16
  6.2 6.8 %collective-permute-start.2 = (bf16[32,1024]{1,0:T(8,128)(2,1)S(1)}, bf16[32,1024]{1,0:T(8,128)(2,1)S(1)}, u32[]{:S(2)}, u32[]{:S(2)}) collective-permute-start(bf16[32,1024]{1,0:T(8,128)(2,1)S(1)} %convolution_convert_fusion.refs_0_), channel_id=1, source_target_pairs={{0,6},{1,7},{2,4},{3,5},{4,2},{5,3},{6,0},{7,1},{8,14},{9,15},{10,... | collective-permute-start | bytes 196616 | tf_op jit(solution)/shard_map/ppermute | solution.py:16
  6.2 1.7 %copy-start.1 = (f32[2048,301]{0,1:T(8,128)S(1)}, f32[2048,301]{0,1:T(8,128)}, u32[]{:S(2)}) copy-start(f32[2048,301]{0,1:T(8,128)} %param.11) | copy-start | bytes 7397380
  7.9 5.1 %copy-start.2 = (f32[32,301]{1,0:T(8,128)S(1)}, f32[32,301]{1,0:T(8,128)}, u32[]{:S(2)}) copy-start(f32[32,301]{1,0:T(8,128)} %targets_ref.1) | copy-start | bytes 115588
  13.2 2.9 %collective-permute-start.3 = (bf16[128,1024]{1,0:T(8,128)(2,1)S(1)}, bf16[128,1024]{1,0:T(8,128)(2,1)S(1)}, u32[]{:S(2)}, u32[]{:S(2)}) collective-permute-start(bf16[128,1024]{1,0:T(8,128)(2,1)S(1)} %get-tuple-element.53.side_ref), channel_id=1, source_target_pairs={{0,1},{1,0},{2,3},{3,2},{4,5},{5,4},{6,7},{7,6},{8,9},{9,8},{10,11... | collective-permute-start | bytes 786440 | tf_op jit(solution)/shard_map/ppermute | solution.py:16
  18.4 1.6 %collective-permute-start.4 = (f32[301,128]{1,0:T(8,128)S(1)}, f32[301,128]{1,0:T(8,128)S(1)}, u32[]{:S(2)}, u32[]{:S(2)}) collective-permute-start(f32[301,128]{1,0:T(8,128)S(1)} %get-tuple-element.64), channel_id=1, source_target_pairs={{0,1},{1,0},{2,3},{3,2},{4,5},{5,4},{6,7},{7,6},{8,9},{9,8},{10,11... | collective-permute-start | bytes 462344 | tf_op jit(solution)/shard_map/ppermute | solution.py:16
  20.1 5.1 %collective-permute-start.5 = (f32[301,128]{1,0:T(8,128)S(1)}, f32[301,128]{1,0:T(8,128)S(1)}, u32[]{:S(2)}, u32[]{:S(2)}) collective-permute-start(f32[301,128]{1,0:T(8,128)S(1)} %subtract_add_fusion), channel_id=1, source_target_pairs={{0,2},{1,3},{2,0},{3,1},{4,6},{5,7},{6,4},{7,5},{8,10},{9,11},{10,... | collective-permute-start | bytes 462344 | tf_op jit(solution)/shard_map/ppermute | solution.py:16
  25.3 11.6 %collective-permute-start.6 = (bf16[301,128]{1,0:T(8,128)(2,1)S(1)}, bf16[301,128]{1,0:T(8,128)(2,1)S(1)}, u32[]{:S(2)}, u32[]{:S(2)}) collective-permute-start(bf16[301,128]{1,0:T(8,128)(2,1)S(1)} %add.14), channel_id=1, source_target_pairs={{0,4},{1,5},{2,6},{3,7},{4,0},{5,1},{6,2},{7,3},{8,12},{9,13},{10,... | collective-permute-start | bytes 231176 | tf_op jit(solution)/shard_map/ppermute | solution.py:16
  28.0 8.9 %collective-permute-start.7 = (bf16[128,1024]{1,0:T(8,128)(2,1)S(1)}, bf16[128,1024]{1,0:T(8,128)(2,1)S(1)}, u32[]{:S(2)}, u32[]{:S(2)}) collective-permute-start(bf16[128,1024]{1,0:T(8,128)(2,1)S(1)} %get-tuple-element.53.side_ref), channel_id=1, source_target_pairs={{0,8},{8,0},{16,24},{24,16},{1,9},{9,1},{17,25},{25,17},{2,10},{10... | collective-permute-start | bytes 786440 | tf_op jit(solution)/shard_map/ppermute | solution.py:16
  29.2 7.7 %collective-permute-start.8 = (bf16[128,1024]{1,0:T(8,128)(2,1)S(1)}, bf16[128,1024]{1,0:T(8,128)(2,1)S(1)}, u32[]{:S(2)}, u32[]{:S(2)}) collective-permute-start(bf16[128,1024]{1,0:T(8,128)(2,1)S(1)} %get-tuple-element.53.side_ref), channel_id=1, source_target_pairs={{0,16},{8,24},{16,0},{24,8},{1,17},{9,25},{17,1},{25,9},{2,18},{10... | collective-permute-start | bytes 786440 | tf_op jit(solution)/shard_map/ppermute | solution.py:16
  30.5 10.7 %collective-permute-start.9 = (bf16[128,1024]{1,0:T(8,128)(2,1)S(1)}, bf16[128,1024]{1,0:T(8,128)(2,1)S(1)}, u32[]{:S(2)}, u32[]{:S(2)}) collective-permute-start(bf16[128,1024]{1,0:T(8,128)(2,1)S(1)} %get-tuple-element.53.side_ref), channel_id=1, source_target_pairs={{0,24},{8,16},{16,8},{24,0},{1,25},{9,17},{17,9},{25,1},{2,26},{10... | collective-permute-start | bytes 786440 | tf_op jit(solution)/shard_map/ppermute | solution.py:16
  41.2 5.2 %collective-permute-start.10 = (bf16[384,1024]{1,0:T(8,128)(2,1)S(1)}, bf16[384,1024]{1,0:T(8,128)(2,1)S(1)}, u32[]{:S(2)}, u32[]{:S(2)}) collective-permute-start(bf16[384,1024]{1,0:T(8,128)(2,1)S(1)} %constant_dynamic-update-slice_fusion.refs_0_), channel_id=1, source_target_pairs={{0,1},{1,0},{2,3},{3,2},{4,5},{5,4},{6,7},{7,6},{8,9},{9,8},{10,11... | collective-permute-start | bytes 2359304 | tf_op jit(solution)/shard_map/ppermute | solution.py:16
  43.7 7.0 %collective-permute-start.11 = (bf16[301,128]{1,0:T(8,128)(2,1)S(1)}, bf16[301,128]{1,0:T(8,128)(2,1)S(1)}, u32[]{:S(2)}, u32[]{:S(2)}) collective-permute-start(bf16[301,128]{1,0:T(8,128)(2,1)S(1)} %convert_element_type.20), channel_id=1, source_target_pairs={{0,8},{8,0},{16,24},{24,16},{1,9},{9,1},{17,25},{25,17},{2,10},{10... | collective-permute-start | bytes 231176 | tf_op jit(solution)/shard_map/ppermute | solution.py:16
  44.8 6.0 %collective-permute-start.12 = (bf16[301,128]{1,0:T(8,128)(2,1)S(1)}, bf16[301,128]{1,0:T(8,128)(2,1)S(1)}, u32[]{:S(2)}, u32[]{:S(2)}) collective-permute-start(bf16[301,128]{1,0:T(8,128)(2,1)S(1)} %convert_element_type.20), channel_id=1, source_target_pairs={{0,16},{8,24},{16,0},{24,8},{1,17},{9,25},{17,1},{25,9},{2,18},{10... | collective-permute-start | bytes 231176 | tf_op jit(solution)/shard_map/ppermute | solution.py:16
  45.3 5.4 %collective-permute-start.13 = (bf16[301,128]{1,0:T(8,128)(2,1)S(1)}, bf16[301,128]{1,0:T(8,128)(2,1)S(1)}, u32[]{:S(2)}, u32[]{:S(2)}) collective-permute-start(bf16[301,128]{1,0:T(8,128)(2,1)S(1)} %convert_element_type.20), channel_id=1, source_target_pairs={{0,24},{8,16},{16,8},{24,0},{1,25},{9,17},{17,9},{25,1},{2,26},{10... | collective-permute-start | bytes 231176 | tf_op jit(solution)/shard_map/ppermute | solution.py:16
  50.8 2.6 %collective-permute-start.14 = (bf16[301,512]{1,0:T(8,128)(2,1)S(1)}, bf16[301,512]{1,0:T(8,128)(2,1)S(1)}, u32[]{:S(2)}, u32[]{:S(2)}) collective-permute-start(bf16[301,512]{1,0:T(8,128)(2,1)S(1)} %constant_dynamic-update-slice_fusion.3.residual_ref), channel_id=1, source_target_pairs={{0,1},{1,0},{2,3},{3,2},{4,5},{5,4},{6,7},{7,6},{8,9},{9,8},{10,11... | collective-permute-start | bytes 924680 | tf_op jit(solution)/shard_map/ppermute | solution.py:16
